TPU v7x, 128 devices: a whole 4x4x4 slice. The times are simulated.
128 devices in a mesh: loc: 32 (over y, x, core), head: 4 (over z).
Axes of the slice: x: 4, y: 4, z: 4, core: 2. Of those that a mesh axis runs over, the one named last changes fastest.
Arguments:
- entities: bfloat16 [32768, 1024], P('loc', 'head'), may hold values from -9 to 9
- attn_gain: float32 [1024], replicated, may hold values from 0.25 to 1.75
- w_qkv: bfloat16 [3, 1024, 1024], P(None, None, 'head'), may hold values from -1 to 1
- w_out: bfloat16 [1024, 1024], P('head'), may hold values from -0.1875 to 0.1875
- mlp_gain: float32 [1024], replicated, may hold values from 0.25 to 1.75
- w_up: bfloat16 [1024, 4096], P(None, 'head'), may hold values from -0.1875 to 0.1875
- w_down: bfloat16 [4096, 1024], P('head'), may hold values from -0.09375 to 0.09375
- far_owner: int32 [256, 4], P('loc'), may hold values from 0 to 31, all different within a row; in each aligned block of 8 rows (0 to 7, 8 to 15, ...) at most 2 rows name the same one
- far_local: int32 [256, 4], P('loc'), may hold values from 0 to 7
- far_live: int32 [256, 4], P('loc'), may hold values 0 or 1
Outputs:
- encoded: bfloat16 [32768, 1024], P('loc', 'head')
Inputs may be any that keep to these rules, and one draw needn't show every extreme that they name: `far_owner`: each row names 4 different owners; among the rows of one index of loc (aligned blocks of 8 rows) no owner is named more than 2 times, a bound that some block reaches.
All inputs are finite; a program needn't handle non-finite values. No bound on the sum of `far_live` on one device may be relied on, other than what follows from the above.
Results may differ from a plain program's by a relative error of at most 0.0065.
Values may be sent and summed in bfloat16 or wider, within the bound.
A program may use at most 128 MiB of HBM per device.

v0:
```python
import math

import jax
import jax.numpy as jnp
from jax import lax
from jax.sharding import PartitionSpec as P

HD = 64


def padded_2(block, sides, width):
    for axis, dim in sides:
        count = lax.axis_size(axis)
        forward = [(i, i + 1) for i in range(count - 1)]
        backward = [(target, source) for source, target in forward]
        low = lax.ppermute(
            lax.slice_in_dim(block, block.shape[dim] - width, None, axis=dim), axis, forward
        )
        high = lax.ppermute(lax.slice_in_dim(block, 0, width, axis=dim), axis, backward)
        block = jnp.concatenate([low, block, high], axis=dim)
    return block


def layer_norm(values, gain):
    center = values - jnp.mean(values, axis=-1, keepdims=True)
    spread = jnp.mean(center * center, axis=-1, keepdims=True)
    return center * lax.rsqrt(spread + 1e-05) * gain


def on_device(
    entities, attn_gain, w_qkv, w_out, mlp_gain, w_up, w_down, far_owner, far_local, far_live
):
    loc_count = lax.axis_size("loc")
    loc_at = lax.axis_index("loc")
    head_at = lax.axis_index("head")
    blocks_here, far_count = far_owner.shape
    row_count = entities.shape[0]
    block_rows = row_count // blocks_here
    entity_full = lax.all_gather(entities, "head", axis=1, tiled=True)
    full_width = entity_full.shape[1]
    normed = layer_norm(entity_full.astype(jnp.float32), attn_gain).astype(jnp.bfloat16)
    queries = jnp.dot(normed, w_qkv[0], preferred_element_type=jnp.float32).astype(jnp.bfloat16)
    keys_mine = jnp.dot(normed, w_qkv[1], preferred_element_type=jnp.float32).astype(jnp.bfloat16)
    values_mine = jnp.dot(normed, w_qkv[2], preferred_element_type=jnp.float32).astype(jnp.bfloat16)
    col_count = queries.shape[1]
    heads_here = col_count // HD
    key_value = jnp.concatenate([keys_mine, values_mine], axis=1)
    padded = padded_2(key_value, (("loc", 0),), block_rows)
    rim_tiles = padded.reshape(blocks_here + 2, block_rows, 2 * col_count)
    near_keys = jnp.concatenate([rim_tiles[:-2], rim_tiles[1:-1], rim_tiles[2:]], axis=1)
    global_block = loc_at * blocks_here + jnp.arange(blocks_here, dtype=jnp.int32)
    prev_valid = global_block >= 1
    next_valid = global_block + 1 < loc_count * blocks_here
    owners = far_owner.reshape(-1)
    far_index = far_local.reshape(-1)
    request_count = blocks_here * far_count
    capacity = max(2, -(-request_count // loc_count))
    positions = jnp.arange(request_count, dtype=jnp.int32)
    matches = owners[:, None] == owners[None, :]
    before = positions[:, None] > positions[None, :]
    order_in = jnp.sum((matches & before).astype(jnp.int32), axis=1)
    slot_of = owners * capacity + order_in
    all_slots = jnp.arange(loc_count * capacity, dtype=jnp.int32)
    onehot = (slot_of[None, :] == all_slots[:, None]).astype(jnp.int32)
    request_ids = jnp.sum(onehot * far_index[None, :], axis=1).reshape(loc_count, capacity)
    asked_ids = lax.all_to_all(request_ids, "loc", split_axis=0, concat_axis=0, tiled=True)
    own_tiles = key_value.reshape(blocks_here, block_rows, 2 * col_count)
    served = own_tiles[asked_ids]
    fetched = lax.all_to_all(served, "loc", split_axis=0, concat_axis=0, tiled=True)
    far_keys = fetched.reshape(loc_count * capacity, block_rows, 2 * col_count)[slot_of]
    far_keys = far_keys.reshape(blocks_here, far_count * block_rows, 2 * col_count)
    listed = jnp.concatenate([near_keys, far_keys], axis=1)
    key_total = listed.shape[1]
    usable = jnp.concatenate(
        [prev_valid[:, None], jnp.ones((blocks_here, 1), bool), next_valid[:, None], far_live == 1],
        axis=1,
    )
    key_valid = jnp.repeat(usable, block_rows, axis=1)
    query_tiles = queries.reshape(blocks_here, block_rows, heads_here, HD)
    key_part = listed[:, :, :col_count].reshape(blocks_here, key_total, heads_here, HD)
    value_part = listed[:, :, col_count:].reshape(blocks_here, key_total, heads_here, HD)
    scale = 1.0 / math.sqrt(HD)
    scores = (
        jnp.einsum("bqhd,bkhd->bhqk", query_tiles, key_part, preferred_element_type=jnp.float32)
        * scale
    )
    scores = jnp.where(key_valid[:, None, None, :], scores, -1e30)
    row_max = jnp.max(scores, axis=-1, keepdims=True)
    weights = jnp.exp(scores - row_max)
    totals = jnp.sum(weights, axis=-1)
    numerator = jnp.einsum(
        "bhqk,bkhd->bqhd",
        weights.astype(jnp.bfloat16),
        value_part,
        preferred_element_type=jnp.float32,
    )
    attended = numerator / jnp.transpose(totals, (0, 2, 1))[:, :, :, None]
    attended = attended.astype(jnp.bfloat16).reshape(row_count, col_count)
    partial_value = jnp.dot(attended, w_out, preferred_element_type=jnp.float32)
    part_width = full_width // lax.axis_size("head")
    attn_share = lax.psum_scatter(partial_value, "head", scatter_dimension=1, tiled=True)
    mixed_mine = entities.astype(jnp.float32) + attn_share
    row_mean = lax.psum(jnp.sum(mixed_mine, axis=1, keepdims=True), "head") / full_width
    centered = mixed_mine - row_mean
    row_var = lax.psum(jnp.sum(centered * centered, axis=1, keepdims=True), "head") / full_width
    gain_mine = lax.dynamic_slice_in_dim(mlp_gain, head_at * part_width, part_width, 0)
    inner_mine = (centered * lax.rsqrt(row_var + 1e-05) * gain_mine).astype(jnp.bfloat16)
    inner = lax.all_gather(inner_mine, "head", axis=1, tiled=True)
    hidden = jax.nn.gelu(
        jnp.dot(inner, w_up, preferred_element_type=jnp.float32), approximate=False
    ).astype(jnp.bfloat16)
    down_terms = jnp.dot(hidden, w_down, preferred_element_type=jnp.float32)
    mlp_output = lax.psum_scatter(down_terms, "head", scatter_dimension=1, tiled=True)
    return (mixed_mine + mlp_output).astype(jnp.bfloat16)


def solution(mesh):
    return jax.shard_map(
        on_device,
        mesh=mesh,
        in_specs=(
            P("loc", "head"),
            P(),
            P(None, None, "head"),
            P("head", None),
            P(),
            P(None, "head"),
            P("head", None),
            P("loc", None),
            P("loc", None),
            P("loc", None),
        ),
        out_specs=P("loc", "head"),
        check_vma=False,
    )
```

profile of v0, /device:TPU:1, one launch (start us, length us, event | category | flops | bytes accessed | tf_op | source)
XLA Modules:
  0.0 407.5 jit_solution(9527792460580962597)
XLA Ops:
  9.8 15.3 %all_to_all.17 = s32[32,1,2]{2,1,0:T(1,128)S(1)} all-to-all(s32[32,1,2]{2,1,0:T(1,128)S(1)} %bitcast.65), channel_id=1, replica_groups=mesh['loc'=32,'head'=4] {'loc'}, dimensions={0} | all-to-all | bytes 512 | tf_op jit(solution)/shard_map/all_to_all | solution.py:66
  25.2 20.9 %all-gather.3.cloned.1.call-done = bf16[1024,1024]{1,0:T(8,128)(2,1)} async-done(((bf16[1024,256]{1,0:T(8,128)(2,1)}), bf16[1024,1024]{1,0:T(8,128)(2,1)}) %all-gather.3.cloned.1.call-update) | async-done | bytes 2097168 | tf_op jit(solution)/shard_map/all_gather | solution.py:39
  46.1 2.1 convert_reduce_fusion
  48.2 2.3 fusion.8
  54.0 4.5 %collective-permute-start = (bf16[128,512]{0,1:T(8,128)(2,1)}, bf16[128,512]{0,1:T(8,128)(2,1)S(1)}, u32[]{:S(2)}, u32[]{:S(2)}) collective-permute-start(bf16[128,512]{0,1:T(8,128)(2,1)} %get-tuple-element.10), channel_id=1, source_target_pairs={{0,4},{4,8},{8,12},{12,16},{16,20},{20,24},{24,28},{28,32},{32,36}... | collective-permute-start | bytes 393224 | tf_op jit(solution)/shard_map/ppermute | solution.py:16
  58.5 1.9 collective-permute-start.1
  63.1 1.8 collective-permute-done.1
  68.1 5.4 %gather_fusion = bf16[64,128,512]{2,1,0:T(8,128)(2,1)} fusion(bf16[8,128,512]{2,1,0:T(8,128)(2,1)S(1)} %bitcast.56, s32[1024]{0:T(1024)S(1)} %pad_clamp_fusion.1), kind=kCustom, calls=%fused_computation | custom fusion | bytes 16777472 | tf_op jit(solution)/shard_map/gather | solution.py:68
  73.5 8.7 %all-to-all-start.1 = ((bf16[32,2,128,512]{3,2,1,0:T(8,128)(2,1)}), bf16[32,2,128,512]{3,2,1,0:T(8,128)(2,1)}, u32[]{:S(2)}, u32[]{:S(2)}) async-start(bf16[32,2,128,512]{3,2,1,0:T(8,128)(2,1)} %bitcast.58), calls=%async_computation.1 | async-start | bytes 16777216 | tf_op jit(solution)/shard_map/all_to_all | solution.py:69
  82.9 3.2 convolution_convert_fusion
  86.1 2.8 reshape.155
  88.8 2.3 copy.64
  91.1 2.3 copy.65
  93.4 88.5 %all-to-all-done.1 = bf16[32,2,128,512]{3,2,1,0:T(8,128)(2,1)} async-done(((bf16[32,2,128,512]{3,2,1,0:T(8,128)(2,1)}), bf16[32,2,128,512]{3,2,1,0:T(8,128)(2,1)}, u32[]{:S(2)}, u32[]{:S(2)}) %all-to-all-start.1) | async-done | bytes 8388640 | tf_op jit(solution)/shard_map/all_to_all | solution.py:69
  181.9 6.3 %gather_fusion.1 = bf16[32,128,512]{2,1,0:T(8,128)(2,1)} fusion(bf16[64,128,512]{2,1,0:T(8,128)(2,1)} %bitcast.7, s32[1024]{0:T(1024)S(1)} %pad_clamp_fusion), kind=kCustom, calls=%fused_computation.1 | custom fusion | bytes 8388736 | tf_op jit(solution)/shard_map/gather | solution.py:70
  188.2 3.6 pad_maximum_fusion
  191.8 3.9 fusion.77
  195.7 6.2 %copy.61 = bf16[8,896,256]{1,2,0:T(8,128)(2,1)} copy(bf16[8,896,256]{2,1,0:T(8,128)(2,1)} %get-tuple-element.5) | data formatting | bytes 7340032 | tf_op jit(solution)/shard_map/slice | solution.py:80
  201.9 6.3 %copy.59 = bf16[8,896,256]{1,2,0:T(8,128)(2,1)} copy(bf16[8,896,256]{2,1,0:T(8,128)(2,1)} %get-tuple-element.6) | data formatting | bytes 7340032 | tf_op jit(solution)/shard_map/slice | solution.py:81
  208.2 3.9 fusion
  212.2 3.7 fusion.1
  215.9 2.5 copy-done.1
  218.4 7.2 %divide_convert_fusion = bf16[8,128,4,64]{1,3,2,0:T(8,128)(2,1)S(1)} fusion(bf16[8,896,4,64]{1,3,2,0:T(8,128)(2,1)S(1)} %bitcast.64, f32[8,4,128,896]{3,2,1,0:T(8,128)} %copy-done.1, f32[8,4,128]{2,1,0:T(4,128)S(1)} %get-tuple-element.12, pred[8,896]{1,0:T(8,128)(4,1)S(1)} %broadcast_bitcast_fusion, f32[8,128,4]{1,2,0:T(4,128)S(1)} %bitcast.68), kind=kOutput, calls=%fused_computation.55 | convolution fusion | flops 484966400 | bytes 18914304 | tf_op jit(solution)/shard_map/bhqk,bkhd->bqhd/dot_general | solution.py:91
  225.9 2.7 fusion.30
  229.5 48.5 %reduce-scatter.3.cloned.1.call-done = f32[1024,256]{1,0:T(8,128)} async-done(((f32[1024,1024]{1,0:T(8,128)}), f32[1024,256]{1,0:T(8,128)}) %reduce-scatter.3.cloned.1.call-update) | async-done | bytes 1048592 | tf_op jit(solution)/shard_map/reduce_scatter | solution.py:101
  279.5 6.5 %psum.14 = f32[1024,1]{0,1:T(1,128)S(1)} all-reduce(f32[1024,1]{0,1:T(1,128)S(1)} %bitcast.70), channel_id=1, replica_groups=mesh['loc'=32,'head'=4] {'head'}, use_global_device_ids=true, to_apply=%region_8.9 | all-reduce | flops 1024 | bytes 8192 | tf_op jit(solution)/shard_map/psum | solution.py:103
  287.6 7.0 %psum.15 = f32[1024,1]{0,1:T(1,128)S(1)} all-reduce(f32[1024,1]{0,1:T(1,128)S(1)} %bitcast.71), channel_id=1, replica_groups=mesh['loc'=32,'head'=4] {'head'}, use_global_device_ids=true, to_apply=%region_10.11 | all-reduce | flops 1024 | bytes 8192 | tf_op jit(solution)/shard_map/psum | solution.py:105
  294.6 2.4 multiply_convert_fusion
  297.2 36.7 %all-gather.5.cloned.1.call-done = bf16[1024,1024]{1,0:T(8,128)(2,1)} async-done(((bf16[1024,256]{1,0:T(8,128)(2,1)}), bf16[1024,1024]{1,0:T(8,128)(2,1)}) %all-gather.5.cloned.1.call-update) | async-done | bytes 2097168 | tf_op jit(solution)/shard_map/all_gather | solution.py:108
  333.9 15.8 %fusion.21 = f32[1024,1024]{1,0:T(8,128)} fusion(bf16[1024,1024]{1,0:T(8,128)(2,1)S(1)} %copy-done, bf16[1024,1024]{1,0:T(8,128)(2,1)} %all-gather.5.cloned.1.call-done, bf16[1024,1024]{1,0:T(8,128)(2,1)} %param.15), kind=kOutput, calls=%fused_computation.36 | convolution fusion | flops 4363124736 | bytes 10485760 | tf_op jit(solution)/shard_map/dot_general | solution.py:112
  349.7 48.9 %reduce-scatter.5.cloned.1.call-done = f32[1024,256]{1,0:T(8,128)} async-done(((f32[1024,1024]{1,0:T(8,128)}), f32[1024,256]{1,0:T(8,128)}) %reduce-scatter.5.cloned.1.call-update) | async-done | bytes 1048592 | tf_op jit(solution)/shard_map/reduce_scatter | solution.py:113
  398.7 2.3 add_convert_fusion
  (75 shorter events, 17.9 us)
Async XLA Ops:
  6.5 327.4 %copy-start = (bf16[1024,1024]{1,0:T(8,128)(2,1)S(1)}, bf16[1024,1024]{1,0:T(8,128)(2,1)}, u32[]{:S(2)}) copy-start(bf16[1024,1024]{1,0:T(8,128)(2,1)} %param.16) | copy-start | bytes 6291460
  6.5 44.0 %copy-start.10 = (f32[1024]{0:T(1024)S(1)}, f32[1024]{0:T(1024)}, u32[]{:S(2)}) copy-start(f32[1024]{0:T(1024)} %param.11) | copy-start | bytes 12292
  6.5 39.6 %all-gather.3.cloned.1.call-start = ((), (), s32[]{:S(2)}) async-start(), calls=%async_computation.4 | async-start | bytes 2621440 | tf_op jit(solution)/shard_map/all_gather | solution.py:39
  9.1 0.5 copy-start.13
  46.1 4.4 %copy-start.2 = (bf16[1024,1024]{1,0:T(8,128)(2,1)S(1)}, bf16[1024,1024]{1,0:T(8,128)(2,1)}, u32[]{:S(2)}) copy-start(bf16[1024,1024]{1,0:T(8,128)(2,1)} %all-gather.3.cloned.1.call-done) | copy-start | bytes 6291460
  46.1 5.1 %copy-start.12 = (bf16[3,1024,256]{2,1,0:T(8,128)(2,1)S(1)}, bf16[3,1024,256]{2,1,0:T(8,128)(2,1)}, u32[]{:S(2)}) copy-start(bf16[3,1024,256]{2,1,0:T(8,128)(2,1)} %param.12) | copy-start | bytes 4718596
  51.2 1.3 copy-start.7
  54.0 9.0 %collective-permute-start = (bf16[128,512]{0,1:T(8,128)(2,1)}, bf16[128,512]{0,1:T(8,128)(2,1)S(1)}, u32[]{:S(2)}, u32[]{:S(2)}) collective-permute-start(bf16[128,512]{0,1:T(8,128)(2,1)} %get-tuple-element.10), channel_id=1, source_target_pairs={{0,4},{4,8},{8,12},{12,16},{16,20},{20,24},{24,28},{28,32},{32,36}... | collective-permute-start | bytes 393224 | tf_op jit(solution)/shard_map/ppermute | solution.py:16
  58.5 6.3 %collective-permute-start.1 = (bf16[128,512]{0,1:T(8,128)(2,1)S(1)}, bf16[128,512]{0,1:T(8,128)(2,1)S(1)}, u32[]{:S(2)}, u32[]{:S(2)}) collective-permute-start(bf16[128,512]{0,1:T(8,128)(2,1)S(1)} %get-tuple-element.11), channel_id=1, source_target_pairs={{4,0},{8,4},{12,8},{16,12},{20,16},{24,20},{28,24},{32,28},{36,32}... | collective-permute-start | bytes 393224 | tf_op jit(solution)/shard_map/ppermute | solution.py:19
  73.5 8.9 %copy-start.9 = (s32[8,4]{0,1:T(4,128)S(1)}, s32[8,4]{0,1:T(4,128)}, u32[]{:S(2)}) copy-start(s32[8,4]{0,1:T(4,128)} %param.17) | copy-start | bytes 388
  73.5 9.2 %copy-start.14 = (s32[32]{0:T(128)S(1)}, s32[32]{0:T(128)}, u32[]{:S(2)}) copy-start(s32[32]{0:T(128)} %copy-done.13) | copy-start | bytes 388
  73.5 9.2 %copy-start.11 = (s32[8,4]{0,1:T(4,128)S(1)}, s32[8,4]{0,1:T(4,128)}, u32[]{:S(2)}) copy-start(s32[8,4]{0,1:T(4,128)} %param.19) | copy-start | bytes 388
  73.5 108.4 %all-to-all-start.1 = ((bf16[32,2,128,512]{3,2,1,0:T(8,128)(2,1)}), bf16[32,2,128,512]{3,2,1,0:T(8,128)(2,1)}, u32[]{:S(2)}, u32[]{:S(2)}) async-start(bf16[32,2,128,512]{3,2,1,0:T(8,128)(2,1)} %bitcast.58), calls=%async_computation.1 | async-start | bytes 16777216 | tf_op jit(solution)/shard_map/all_to_all | solution.py:69
  82.2 195.9 %reduce-scatter.3.cloned.1.call-start = ((), (), s32[]{:S(2)}) async-start(), calls=%async_computation.5 | async-start | bytes 5242880 | tf_op jit(solution)/shard_map/reduce_scatter | solution.py:101
  201.9 6.3 %copy-start.5 = (bf16[8,128,4,64]{3,2,1,0:T(4,128)(2,1)S(1)}, bf16[8,128,4,64]{3,2,1,0:T(4,128)(2,1)}, u32[]{:S(2)}) copy-start(bf16[8,128,4,64]{3,2,1,0:T(4,128)(2,1)} %reshape.155) | copy-start | bytes 1572868
  212.2 6.2 %copy-start.1 = (f32[8,4,128,896]{3,2,1,0:T(8,128)}, f32[8,4,128,896]{3,2,1,0:T(8,128)S(1)}, u32[]{:S(2)}) copy-start(f32[8,4,128,896]{3,2,1,0:T(8,128)S(1)} %get-tuple-element.13) | copy-start | bytes 44040196
  212.2 6.2 %copy-start.6 = (bf16[8,896,256]{1,2,0:T(8,128)(2,1)S(1)}, bf16[8,896,256]{1,2,0:T(8,128)(2,1)}, u32[]{:S(2)}) copy-start(bf16[8,896,256]{1,2,0:T(8,128)(2,1)} %copy.59) | copy-start | bytes 11010052
  218.4 7.5 %copy-start.8 = (bf16[256,1024]{1,0:T(8,128)(2,1)S(1)}, bf16[256,1024]{1,0:T(8,128)(2,1)}, u32[]{:S(2)}) copy-start(bf16[256,1024]{1,0:T(8,128)(2,1)} %param.13) | copy-start | bytes 1572868
  228.6 49.4 %copy-start.4 = (bf16[1024,256]{1,0:T(8,128)(2,1)S(1)}, bf16[1024,256]{1,0:T(8,128)(2,1)}, u32[]{:S(2)}) copy-start(bf16[1024,256]{1,0:T(8,128)(2,1)} %param.10) | copy-start | bytes 1572868
  228.6 105.3 %all-gather.5.cloned.1.call-start = ((), (), s32[]{:S(2)}) async-start(), calls=%async_computation.6 | async-start | bytes 2621440 | tf_op jit(solution)/shard_map/all_gather | solution.py:108
  297.0 101.7 %reduce-scatter.5.cloned.1.call-start = ((), (), s32[]{:S(2)}) async-start(), calls=%async_computation.7 | async-start | bytes 5242880 | tf_op jit(solution)/shard_map/reduce_scatter | solution.py:113
  349.7 49.0 %copy-start.3 = (f32[1024,256]{1,0:T(8,128)S(1)}, f32[1024,256]{1,0:T(8,128)}, u32[]{:S(2)}) copy-start(f32[1024,256]{1,0:T(8,128)} %reduce-scatter.3.cloned.1.call-done) | copy-start | bytes 3145732
Sparse Core Ops, SparseCore 0:
  9.0 37.0 all-gather.2
  228.8 49.2 reduce-scatter.2
  297.1 36.7 all-gather.4
  349.8 48.7 reduce-scatter.4
where the time goes:
time: 409 us; the launch traced here: 408 us
  waiting for transfers between devices  246 us (60%)
  local copies, waits for them, and re-layouts  45.2 us (11%)
  matrix products  34.3 us (8%)
  blocking collectives  28.8 us (7%)
  other arithmetic  24.1 us (6%)
  starting transfers between devices  15.6 us (4%)
  between operations  13.4 us (3%)
    all_to_all x1, waiting for transfers between devices, on_device(): lax.all_to_all(served, 'loc', split_axis=0, concat_axis=0, tiled=True)  88.5 us
    reduce_scatter x1, waiting for transfers between devices, on_device(): lax.psum_scatter(down_terms, 'head', scatter_dimension=1, tiled=True)  48.9 us
    reduce_scatter x1, waiting for transfers between devices, on_device(): lax.psum_scatter(partial_value, 'head', scatter_dimension=1, tiled=True)  48.5 us
    all_gather x1, waiting for transfers between devices, on_device(): inner = lax.all_gather(inner_mine, 'head', axis=1, tiled=True)  36.7 us
    all_gather x1, waiting for transfers between devices, on_device(): entity_full = lax.all_gather(entities, 'head', axis=1, tiled=True)  20.9 us
    dot_general x1, matrix products, on_device(): down_terms = jnp.dot(hidden, w_down, preferred_element_type=jnp.float32)  15.8 us
    all_to_all x1, blocking collectives, on_device(): lax.all_to_all(request_ids, 'loc', split_axis=0, concat_axis=0, tiled=True)  15.3 us
    slice x2, local copies, waits for them, and re-layouts, on_device(): listed[:, :, :col_count].reshape(blocks_here, key_total, heads_here, HD)  10.1 us
  transfers between devices with their start and end apart: 7, of which 6 were waited for; matrix products, arithmetic and copies ran while one was open for 4% of the time, Pallas kernels for 0%

commit v1 on v0

v1 whole, which is shorter than its diff:
```python
import functools

import jax
import jax.numpy as jnp
from jax import lax
from jax.experimental import pallas as pl
from jax.experimental.pallas import tpu as pltpu
from jax.sharding import PartitionSpec as P

MESH = pl.DeviceIdType.MESH
F32 = jnp.float32
BF16 = jnp.bfloat16
BLK = 128
HD = 64
NB = 8
SIDE = 4
CHUNKS = 4
ROWS = NB * BLK
GROUP = ROWS // SIDE
WIDTH = 1024
PART = WIDTH // SIDE
NEG = -1e30
MB = 2**20


def coords():
    loc = lax.axis_index("loc")
    return loc // 8, (loc // 2) % 4, loc % 2, lax.axis_index("head")


def device(y, x, core, z):
    return ((y % 4 * 4 + x % 4) * 2 + core, z % 4)


def shifted(axis, by):
    y, x, core, z = coords()
    if axis == "y":
        return device(y + by + 4, x, core, z)
    if axis == "x":
        return device(y, x + by + 4, core, z)
    if axis == "z":
        return device(y, x, core, z + by + 4)
    return device(y, x, 1 - core, z)


def loc_shifted(by):
    return ((lax.axis_index("loc") + by + 32) % 32, lax.axis_index("head"))


def greet(peers):
    barrier = pltpu.get_barrier_semaphore()
    for peer in peers:
        pl.semaphore_signal(barrier, inc=1, device_id=peer, device_id_type=MESH)
    pl.semaphore_wait(barrier, len(peers))


def remote(src, dst, send, recv, to):
    return pltpu.make_async_remote_copy(
        src_ref=src, dst_ref=dst, send_sem=send, recv_sem=recv, device_id=to, device_id_type=MESH
    )


def norm_rows(values, gain):
    center = values - jnp.mean(values, axis=-1, keepdims=True)
    spread = jnp.mean(center * center, axis=-1, keepdims=True)
    return center * lax.rsqrt(spread + 1e-05) * gain


def split_heads(query):
    zero = jnp.zeros((HD, BLK), query.dtype)
    top = jnp.concatenate([query[:HD], zero], axis=1)
    low = jnp.concatenate([zero, query[HD:]], axis=1)
    return jnp.concatenate([top, low], axis=0)


def gather_kernel(
    ent, gain, wqkv, xbuf, ybuf, near_o, near_st, ent_rows,
    zbuf, xown, yown, halo_low, halo_high,
    zs, zr, xs, xr, ys, yr, cs, cr, hs, hr, ls,
):
    y, x, core, z = coords()
    z_up, z_dn = shifted("z", 1), shifted("z", -1)
    x_up, x_dn = shifted("x", 1), shifted("x", -1)
    y_up, y_dn = shifted("y", 1), shifted("y", -1)
    sib = shifted("c", 0)
    nxt, prv = loc_shifted(1), loc_shifted(-1)
    greet([z_up, z_dn, x_up, x_dn, y_up, y_dn, sib, nxt, prv])
    rows = ROWS // CHUNKS
    blocks = NB // CHUNKS
    pending = []

    def go(copy):
        copy.start()
        pending.append(copy)
        return copy

    z_near = []
    for r in range(CHUNKS):
        at = pl.ds(r * rows, rows)
        z_near.append(
            (
                go(remote(ent.at[at], zbuf.at[z, at], zs.at[r, 0], zr.at[r, 0], z_up)),
                go(remote(ent.at[at], zbuf.at[z, at], zs.at[r, 1], zr.at[r, 1], z_dn)),
            )
        )
    zbuf[z] = ent[...]
    z_far = []

    def z_forward(r):
        a, b = z_near[r]
        low = pl.ds(r * rows, rows // 2)
        high = pl.ds(r * rows + rows // 2, rows // 2)
        a.wait_recv()
        s = (z + 3) % 4
        c = go(remote(zbuf.at[s, low], zbuf.at[s, low], zs.at[r, 2], zr.at[r, 2], z_up))
        b.wait_recv()
        s = (z + 1) % 4
        d = go(remote(zbuf.at[s, high], zbuf.at[s, high], zs.at[r, 3], zr.at[r, 3], z_dn))
        z_far.append((c, d))

    plane = {}
    core_copies = []
    local_copies = []

    def to_sibling(buf, place, blks, sem, src=None):
        view = buf.at[core, place, blks, pl.ds(0, 2)]
        core_copies.append(go(remote(view if src is None else src, view, cs.at[sem], cr.at[sem], sib)))

    def project(r):
        for copy in z_far[r]:
            copy.wait_recv()
        at = pl.ds(r * rows, rows)
        full = jnp.concatenate([zbuf[s, at, :] for s in range(SIDE)], axis=1).astype(F32)
        normed = norm_rows(full, gain[...]).astype(BF16)
        queries = jnp.dot(normed, wqkv[0], preferred_element_type=F32)
        keys = jnp.dot(normed, wqkv[1], preferred_element_type=F32).astype(BF16)
        values = jnp.dot(normed, wqkv[2], preferred_element_type=F32)
        q_t = (queries.T.astype(BF16).astype(F32) * 0.125).astype(BF16)
        v_t = values.T.astype(BF16)
        for i in range(blocks):
            b = r * blocks + i
            cut = slice(i * BLK, (i + 1) * BLK)
            xown[b, 0] = keys[cut, :BLK]
            yown[b, 0] = keys[cut, BLK:]
            xown[b, 1] = v_t[:BLK, cut]
            yown[b, 1] = v_t[BLK:, cut]
            yown[b, 2] = q_t[:BLK, cut]
            xown[b, 2] = q_t[BLK:, cut]
        blks = pl.ds(r * blocks, blocks)
        for name, own, buf, place, send, recv, up, dn, k in (
            ("x", xown, xbuf, x, xs, xr, x_up, x_dn, 0),
            ("y", yown, ybuf, y, ys, yr, y_up, y_dn, 1),
        ):
            src, dst = own.at[blks], buf.at[core, place, blks]
            plane[name, r] = (
                go(remote(src, dst, send.at[r, 0], recv.at[r, 0], up)),
                go(remote(src, dst, send.at[r, 1], recv.at[r, 1], dn)),
            )
            local = pltpu.make_async_copy(src, dst, ls.at[r * 2 + k])
            local.start()
            local_copies.append(local)
            to_sibling(buf, place, blks, r * 10 + k * 5, own.at[blks, pl.ds(0, 2)])

    def plane_forward(r):
        blks = pl.ds(r * blocks, blocks)
        low = pl.ds(r * blocks, blocks // 2)
        high = pl.ds(r * blocks + blocks // 2, blocks // 2)
        for name, buf, place, send, recv, up, dn, k in (
            ("x", xbuf, x, xs, xr, x_up, x_dn, 0),
            ("y", ybuf, y, ys, yr, y_up, y_dn, 1),
        ):
            a, b = plane[name, r]
            a.wait_recv()
            s = (place + 3) % 4
            view = buf.at[core, s, low]
            c = go(remote(view, view, send.at[r, 2], recv.at[r, 2], up))
            to_sibling(buf, s, blks, r * 10 + k * 5 + 1)
            b.wait_recv()
            s = (place + 1) % 4
            view = buf.at[core, s, high]
            d = go(remote(view, view, send.at[r, 3], recv.at[r, 3], dn))
            to_sibling(buf, s, blks, r * 10 + k * 5 + 2)
            plane[name, r] = (c, d)

    def plane_finish(r):
        low = pl.ds(r * blocks, blocks // 2)
        high = pl.ds(r * blocks + blocks // 2, blocks // 2)
        for name, buf, place, k in (("x", xbuf, x, 0), ("y", ybuf, y, 1)):
            c, d = plane[name, r]
            s = (place + 2) % 4
            c.wait_recv()
            to_sibling(buf, s, low, r * 10 + k * 5 + 3)
            d.wait_recv()
            to_sibling(buf, s, high, r * 10 + k * 5 + 4)

    loc = lax.axis_index("loc")

    def near(b):
        for p, (own, other) in enumerate(((xown, yown), (yown, xown))):
            query = split_heads(other[b, 2])
            parts = []
            for step in (-1, 0, 1):
                if b + step < 0:
                    key, val, ok = halo_low[p, 0], halo_low[p, 1], loc > 0
                elif b + step >= NB:
                    key, val, ok = halo_high[p, 0], halo_high[p, 1], loc < 31
                else:
                    key, val, ok = own[b + step, 0], own[b + step, 1], None
                score = jnp.dot(key, query, preferred_element_type=F32)
                if ok is not None:
                    score = jnp.where(ok, score, NEG)
                parts.append((score, val))
            top = functools.reduce(
                jnp.maximum, [jnp.max(score, axis=0, keepdims=True) for score, _ in parts]
            )
            total = jnp.zeros((1, 2 * BLK), F32)
            out = jnp.zeros((BLK, 2 * BLK), F32)
            for score, val in parts:
                weight = jnp.exp(score - top)
                total = total + jnp.sum(weight, axis=0, keepdims=True)
                out = out + jnp.dot(val, weight.astype(BF16), preferred_element_type=F32)
            near_o[b, p] = jnp.concatenate(
                [out[:HD, :BLK] / total[:, :BLK], out[HD:, BLK:] / total[:, BLK:]], axis=0
            )
            near_st[b, p, 0:1] = top[:, :BLK]
            near_st[b, p, 1:2] = top[:, BLK:]
            near_st[b, p, 2:3] = total[:, :BLK]
            near_st[b, p, 3:4] = total[:, BLK:]
            near_st[b, p, 4:8] = jnp.zeros((4, BLK), F32)

    z_forward(0)
    z_forward(1)
    project(0)
    halos = []
    for p, own in enumerate((xown, yown)):
        halos.append(go(remote(own.at[0, pl.ds(0, 2)], halo_high.at[p], hs.at[p], hr.at[p], prv)))
    z_forward(2)
    project(1)
    z_forward(3)
    project(2)
    plane_forward(0)
    project(3)
    for p, own in enumerate((xown, yown)):
        halos.append(
            go(remote(own.at[NB - 1, pl.ds(0, 2)], halo_low.at[p], hs.at[2 + p], hr.at[2 + p], nxt))
        )
    ent_rows[...] = jnp.concatenate(
        [zbuf[s, pl.ds(pl.multiple_of(z * GROUP, GROUP), GROUP), :] for s in range(SIDE)], axis=1
    )
    near(1)
    plane_forward(1)
    near(2)
    near(3)
    plane_forward(2)
    plane_finish(0)
    near(4)
    near(5)
    plane_forward(3)
    plane_finish(1)
    near(6)
    for copy in halos:
        copy.wait_recv()
    near(7)
    plane_finish(2)
    near(0)
    plane_finish(3)
    for copy in core_copies:
        copy.wait_recv()
    for copy in local_copies:
        copy.wait()
    for copy in pending:
        copy.wait_send()


def gather_call(ent, gain, wqkv):
    vmem = pl.BlockSpec(memory_space=pltpu.VMEM)
    hbm = pl.BlockSpec(memory_space=pl.ANY)
    dma = pltpu.SemaphoreType.DMA
    plane_shape = (2, SIDE, NB, 3, BLK, BLK)
    return pl.pallas_call(
        gather_kernel,
        out_shape=(
            jax.ShapeDtypeStruct(plane_shape, BF16),
            jax.ShapeDtypeStruct(plane_shape, BF16),
            jax.ShapeDtypeStruct((NB, 2, BLK, BLK), F32),
            jax.ShapeDtypeStruct((NB, 2, 8, BLK), F32),
            jax.ShapeDtypeStruct((GROUP, WIDTH), BF16),
        ),
        in_specs=[vmem] * 3,
        out_specs=(hbm, hbm, vmem, vmem, vmem),
        scratch_shapes=[
            pltpu.VMEM((SIDE, ROWS, PART), BF16),
            pltpu.VMEM((NB, 3, BLK, BLK), BF16),
            pltpu.VMEM((NB, 3, BLK, BLK), BF16),
            pltpu.VMEM((2, 2, BLK, BLK), BF16),
            pltpu.VMEM((2, 2, BLK, BLK), BF16),
            dma((CHUNKS, 4)), dma((CHUNKS, 4)),
            dma((CHUNKS, 4)), dma((CHUNKS, 4)),
            dma((CHUNKS, 4)), dma((CHUNKS, 4)),
            dma((CHUNKS * 10,)), dma((CHUNKS * 10,)),
            dma((4,)), dma((4,)),
            dma((CHUNKS * 2,)),
        ],
        compiler_params=pltpu.CompilerParams(
            collective_id=0, has_side_effects=True, vmem_limit_bytes=40 * MB
        ),
        name="gather_project",
    )(ent, gain, wqkv)


def far_kernel(tab, xbuf, ybuf, oa, sa, ob, sb, acc, state, hits):
    y, x, core, z = coords()
    live_q = SIDE * NB

    for pair in range(2):
        def find(i, count, pair=pair):
            s, b = i // NB, i % NB
            loc = (s * 4 + x) * 2 + core if pair == 0 else (y * 4 + s) * 2 + core
            base = (loc * NB + b) * 12
            for j in range(4):
                owner, local, live = tab[base + j], tab[base + 4 + j], tab[base + 8 + j]
                oy, ox, oc = owner // 8, (owner // 2) % 4, owner % 2
                if pair == 0:
                    mine, place = oy == y, ox
                else:
                    mine, place = ox == x, oy
                hits[count] = i * 1024 + (oc * 4 + place) * NB + local
                count = count + jnp.where(mine & (live == 1), 1, 0)
            return count

        count = lax.fori_loop(0, live_q, find, 0)
        for extra in range(4):
            hits[count + extra] = live_q * 1024
        keys_ref, query_ref = (xbuf, ybuf) if pair == 0 else (ybuf, xbuf)
        o_ref, s_ref = (oa, sa) if pair == 0 else (ob, sb)

        def clear(i, carry):
            acc[i] = jnp.zeros((BLK, BLK), F32)
            state[i, 0:2] = jnp.full((2, BLK), NEG, F32)
            state[i, 2:8] = jnp.zeros((6, BLK), F32)
            return carry

        lax.fori_loop(0, live_q + 1, clear, 0)

        def four(step, carry):
            work = []
            for u in range(4):
                code = hits[step * 4 + u]
                q, k = code // 1024, code % 1024
                q_at = jnp.minimum(q, live_q - 1)
                query = split_heads(query_ref[core, q_at // NB, q_at % NB, 2])
                kc, kp, kb = k // 32, (k // 8) % 4, k % 8
                key = keys_ref[kc, kp, kb, 0]
                val = keys_ref[kc, kp, kb, 1]
                score = jnp.dot(key, query, preferred_element_type=F32)
                top = jnp.max(score, axis=0, keepdims=True)
                weight = jnp.exp(score - top)
                total = jnp.sum(weight, axis=0, keepdims=True)
                out = jnp.dot(val, weight.astype(BF16), preferred_element_type=F32)
                work.append((q, top, total, out))
            for q, top, total, out in work:
                for h in range(2):
                    cut = slice(h * BLK, (h + 1) * BLK)
                    feat = pl.ds(h * HD, HD)
                    old_top = state[q, h : h + 1]
                    new_top = jnp.maximum(old_top, top[:, cut])
                    keep = jnp.exp(old_top - new_top)
                    add = jnp.exp(top[:, cut] - new_top)
                    acc[q, feat] = acc[q, feat] * keep + out[h * HD : (h + 1) * HD, cut] * add
                    state[q, h : h + 1] = new_top
                    state[q, 2 + h : 3 + h] = state[q, 2 + h : 3 + h] * keep + total[:, cut] * add
            return carry

        lax.fori_loop(0, (count + 3) // 4, four, 0)

        def finish(i, carry):
            s, b = i // NB, i % NB
            st = state[i]
            s_ref[s, b] = st
            for h in range(2):
                total = st[2 + h : 3 + h]
                scale = 1.0 / jnp.where(total > 0, total, 1.0)
                feat = pl.ds(h * HD, HD)
                o_ref[s, b, feat] = (acc[i, feat] * scale).astype(BF16)
            return carry

        lax.fori_loop(0, live_q, finish, 0)


def far_call(tab, xbuf, ybuf):
    vmem = pl.BlockSpec(memory_space=pltpu.VMEM)
    o_shape = jax.ShapeDtypeStruct((SIDE, NB, BLK, BLK), BF16)
    s_shape = jax.ShapeDtypeStruct((SIDE, NB, 8, BLK), F32)
    return pl.pallas_call(
        far_kernel,
        out_shape=(o_shape, s_shape, o_shape, s_shape),
        in_specs=[pl.BlockSpec(memory_space=pltpu.SMEM), vmem, vmem],
        out_specs=(vmem,) * 4,
        scratch_shapes=[
            pltpu.VMEM((SIDE * NB + 1, BLK, BLK), F32),
            pltpu.VMEM((SIDE * NB + 1, 8, BLK), F32),
            pltpu.SMEM((SIDE * NB * 4 + 8,), jnp.int32),
        ],
        compiler_params=pltpu.CompilerParams(vmem_limit_bytes=40 * MB),
        name="far_partials",
    )(tab, xbuf, ybuf)


def merge_kernel(
    oa, sa, ob, sb, near_o, near_st, ent_rows, w_out, gain, mixed, inner,
    ra, rsa, rb, rsb, relay, relay_st, att, part, got_half, got,
    os, orr, fs, fr, zs, zr,
):
    y, x, core, z = coords()
    z_up, z_dn = shifted("z", 1), shifted("z", -1)
    peers = [shifted("y", 1), shifted("y", -1), shifted("x", 1), shifted("x", -1), z_up, z_dn]
    greet(peers)
    pending = []

    def go(copy):
        copy.start()
        pending.append(copy)
        return copy

    half = NB // 2
    lanes = []
    for k, (place, up, dn, o, st, ro, rst) in enumerate(
        (
            (y, peers[0], peers[1], oa, sa, ra, rsa),
            (x, peers[2], peers[3], ob, sb, rb, rsb),
        )
    ):
        far_to, up_to, dn_to = (place + 2) % 4, (place + 1) % 4, (place + 3) % 4
        low, high = pl.ds(0, half), pl.ds(half, half)
        first = []
        for t, (src, hop, dst) in enumerate(((o, relay, ro), (st, relay_st, rst))):
            first.append(
                (
                    go(remote(src.at[far_to, low], hop.at[k, 0], os.at[k, t, 0], orr.at[k, t, 0], up)),
                    go(remote(src.at[far_to, high], hop.at[k, 1], os.at[k, t, 1], orr.at[k, t, 1], dn)),
                )
            )
        direct = []
        for t, (src, dst) in enumerate(((o, ro), (st, rst))):
            direct.append(
                (
                    go(remote(src.at[up_to], dst.at[place], os.at[k, t, 2], orr.at[k, t, 2], up)),
                    go(remote(src.at[dn_to], dst.at[place], os.at[k, t, 3], orr.at[k, t, 3], dn)),
                )
            )
        lanes.append((place, up, dn, ro, rst, first, direct))
    arrivals = []
    for k, (place, up, dn, ro, rst, first, direct) in enumerate(lanes):
        low, high = pl.ds(0, half), pl.ds(half, half)
        for t, (hop, dst) in enumerate(((relay, ro), (relay_st, rst))):
            a, b = first[t]
            a.wait_recv()
            arrivals.append(
                go(remote(hop.at[k, 0], dst.at[(place + 3) % 4, low], fs.at[k, t, 0], fr.at[k, t, 0], up))
            )
            b.wait_recv()
            arrivals.append(
                go(remote(hop.at[k, 1], dst.at[(place + 1) % 4, high], fs.at[k, t, 1], fr.at[k, t, 1], dn))
            )
        for pair in direct:
            arrivals.extend(pair)
    ra[y] = oa[y]
    rsa[y] = sa[y]
    rb[x] = ob[x]
    rsb[x] = sb[x]
    for copy in arrivals:
        copy.wait_recv()

    def merge(b, carry):
        for p, (ro, rst) in enumerate(((ra, rsa), (rb, rsb))):
            stats = [near_st[b, p]] + [rst[s, b] for s in range(SIDE)]
            outs = [near_o[b, p]] + [ro[s, b].astype(F32) for s in range(SIDE)]
            halves = []
            for h in range(2):
                top = functools.reduce(jnp.maximum, [st[h : h + 1] for st in stats])
                scale = [st[2 + h : 3 + h] * jnp.exp(st[h : h + 1] - top) for st in stats]
                inv = 1.0 / functools.reduce(jnp.add, scale)
                halves.append(
                    functools.reduce(
                        jnp.add,
                        [o[h * HD : (h + 1) * HD] * (w * inv) for o, w in zip(outs, scale)],
                    )
                )
            tile = jnp.concatenate(halves, axis=0).T.astype(BF16)
            att[pl.ds(pl.multiple_of(b * BLK, BLK), BLK), p * BLK : (p + 1) * BLK] = tile
        return carry

    lax.fori_loop(0, NB, merge, 0)

    def project(group):
        rows = att[pl.ds(pl.multiple_of(group * GROUP, GROUP), GROUP), :]
        return jnp.dot(rows, w_out[...], preferred_element_type=F32)

    h = GROUP // 2
    part[0] = project((z + 2) % 4).astype(BF16)
    f_up = go(remote(part.at[0, pl.ds(0, h)], got_half.at[0], zs.at[0], zr.at[0], z_up))
    f_dn = go(remote(part.at[0, pl.ds(h, h)], got_half.at[1], zs.at[1], zr.at[1], z_dn))
    to_up = project((z + 1) % 4)
    part[1, h:] = to_up[h:].astype(BF16)
    to_dn = project((z + 3) % 4)
    part[2, :h] = to_dn[:h].astype(BF16)
    f_up.wait_recv()
    part[1, :h] = (to_up[:h] + got_half[0].astype(F32)).astype(BF16)
    s_up = go(remote(part.at[1], got.at[0], zs.at[2], zr.at[2], z_up))
    f_dn.wait_recv()
    part[2, h:] = (to_dn[h:] + got_half[1].astype(F32)).astype(BF16)
    s_dn = go(remote(part.at[2], got.at[1], zs.at[3], zr.at[3], z_dn))
    mine = project(z) + ent_rows[...].astype(F32)
    s_up.wait_recv()
    s_dn.wait_recv()
    total = mine + got[0].astype(F32) + got[1].astype(F32)
    mixed[...] = total
    inner[...] = norm_rows(total, gain[...]).astype(BF16)
    for copy in pending:
        copy.wait_send()


def merge_call(oa, sa, ob, sb, near_o, near_st, ent_rows, w_out, gain):
    vmem = pl.BlockSpec(memory_space=pltpu.VMEM)
    dma = pltpu.SemaphoreType.DMA
    return pl.pallas_call(
        merge_kernel,
        out_shape=(
            jax.ShapeDtypeStruct((GROUP, WIDTH), F32),
            jax.ShapeDtypeStruct((GROUP, WIDTH), BF16),
        ),
        in_specs=[vmem] * 9,
        out_specs=(vmem, vmem),
        scratch_shapes=[
            pltpu.VMEM((SIDE, NB, BLK, BLK), BF16),
            pltpu.VMEM((SIDE, NB, 8, BLK), F32),
            pltpu.VMEM((SIDE, NB, BLK, BLK), BF16),
            pltpu.VMEM((SIDE, NB, 8, BLK), F32),
            pltpu.VMEM((2, 2, NB // 2, BLK, BLK), BF16),
            pltpu.VMEM((2, 2, NB // 2, 8, BLK), F32),
            pltpu.VMEM((ROWS, 2 * BLK), BF16),
            pltpu.VMEM((3, GROUP, WIDTH), BF16),
            pltpu.VMEM((2, GROUP // 2, WIDTH), BF16),
            pltpu.VMEM((2, GROUP, WIDTH), BF16),
            dma((2, 2, 4)), dma((2, 2, 4)),
            dma((2, 2, 2)), dma((2, 2, 2)),
            dma((4,)), dma((4,)),
        ],
        compiler_params=pltpu.CompilerParams(
            collective_id=1, has_side_effects=True, vmem_limit_bytes=40 * MB
        ),
        name="merge_project",
    )(oa, sa, ob, sb, near_o, near_st, ent_rows, w_out, gain)


def gelu(v):
    return 0.5 * v * (1.0 + lax.erf(v * 0.7071067811865476))


def mlp_kernel(inner, mixed, up, down, out, acc, res, landed, ss, rs):
    step = pl.program_id(0)
    last = pl.num_programs(0) - 1
    y, x, core, z = coords()

    @pl.when(step == 0)
    def _():
        greet([shifted("z", 1), shifted("z", 2), shifted("z", 3)])
        acc[...] = mixed[...]

    w_up = up[...].reshape(WIDTH, -1)
    w_down = down[...].reshape(-1, WIDTH)
    hidden = gelu(jnp.dot(inner[...], w_up, preferred_element_type=F32)).astype(BF16)
    acc[...] += jnp.dot(hidden, w_down, preferred_element_type=F32)

    @pl.when(step == last)
    def _():
        final = acc[...].astype(BF16)
        for s in range(SIDE):
            res[s] = final[:, s * PART : (s + 1) * PART]
        here = pl.ds(pl.multiple_of(z * GROUP, GROUP), GROUP)
        copies = []
        for by in (2, 1, 3):
            to = (z + by) % 4
            copies.append(
                remote(res.at[to], landed.at[z], ss.at[by], rs.at[by], shifted("z", by))
            )
            copies[-1].start()
        out[here, :] = res[z]
        for copy in copies:
            copy.wait()
        for by in range(1, SIDE):
            s = (z + by) % 4
            out[pl.ds(pl.multiple_of(s * GROUP, GROUP), GROUP), :] = landed[s]


def mlp_call(inner, mixed, weights, halves):
    vmem = pl.BlockSpec(memory_space=pltpu.VMEM)
    dma = pltpu.SemaphoreType.DMA
    unit = WIDTH // halves
    return pl.pallas_call(
        mlp_kernel,
        grid=(SIDE * halves,),
        out_shape=jax.ShapeDtypeStruct((ROWS, PART), BF16),
        in_specs=[
            vmem,
            vmem,
            pl.BlockSpec((1, 32, 1, 32, unit), lambda i: (i // halves, 0, 0, 0, i % halves)),
            pl.BlockSpec((1, 32 // halves, 1, 32, WIDTH), lambda i: (i // halves, i % halves, 1, 0, 0)),
        ],
        out_specs=vmem,
        scratch_shapes=[
            pltpu.VMEM((GROUP, WIDTH), F32),
            pltpu.VMEM((SIDE, GROUP, PART), BF16),
            pltpu.VMEM((SIDE, GROUP, PART), BF16),
            dma((4,)), dma((4,)),
        ],
        compiler_params=pltpu.CompilerParams(
            collective_id=2, has_side_effects=True, vmem_limit_bytes=40 * MB
        ),
        name="mlp_exchange",
    )(inner, mixed, weights, weights)


def on_device(
    entities, attn_gain, w_qkv, w_out, mlp_gain, w_up, w_down, far_owner, far_local, far_live
):
    loc = lax.axis_index("loc")
    piece = jnp.concatenate(
        [
            lax.dynamic_slice_in_dim(w_up, loc * 32, 32, 0),
            lax.dynamic_slice_in_dim(w_down, loc * 32, 32, 0),
        ],
        axis=0,
    )
    weights = lax.all_gather(piece, ("head", "loc"), axis=0, tiled=True)
    weights = weights.reshape(SIDE, 32, 2, 32, WIDTH)
    tab = jnp.concatenate([far_owner, far_local, far_live], axis=1)
    tab = lax.all_gather(tab, "loc", axis=0, tiled=True).reshape(-1)
    xbuf, ybuf, near_o, near_st, ent_rows = gather_call(
        entities, attn_gain.reshape(1, WIDTH), w_qkv
    )
    oa, sa, ob, sb = far_call(tab, xbuf, ybuf)
    mixed, inner = merge_call(
        oa, sa, ob, sb, near_o, near_st, ent_rows, w_out, mlp_gain.reshape(1, WIDTH)
    )
    return mlp_call(inner, mixed, weights, 2)


def solution(mesh):
    return jax.shard_map(
        on_device,
        mesh=mesh,
        in_specs=(
            P("loc", "head"),
            P(),
            P(None, None, "head"),
            P("head", None),
            P(),
            P(None, "head"),
            P("head", None),
            P("loc", None),
            P("loc", None),
            P("loc", None),
        ),
        out_specs=P("loc", "head"),
        check_vma=False,
    )
```

time: 409 us -> 204 us (0.50)
  waiting for transfers between devices: 246 us -> 0.04 us
  Pallas kernels: 0 us -> 154 us
  local copies, waits for them, and re-layouts: 45.2 us -> 7.2 us
  matrix products: 34.3 us -> 0 us
  other arithmetic: 24.1 us -> 0.74 us
  starting transfers between devices: 15.6 us -> 0.01 us
    pallas_call x0 -> x4, Pallas kernels: none -> 154 us  [the longest x1 81.4 us: gather_call(): pl.pallas_call(gather_kernel, out_shape=(jax.ShapeDtypeStruct(plane_shape...]
    reduce_scatter x2 -> x0, waiting for transfers between devices: 97.5 us -> none  [the longest x1 48.9 us: on_device(): lax.psum_scatter(down_terms, 'head', scatter_dimension=1, tiled=True)]
    all_to_all x1 -> x0, waiting for transfers between devices: 88.5 us -> none  [on_device(): lax.all_to_all(served, 'loc', split_axis=0, concat_axis=0, tiled=True)]
    all_gather x2 -> x1, waiting for transfers between devices: 57.6 us -> 0.02 us  [on_device(): weights = lax.all_gather(piece, ('head', 'loc'), axis=0, tiled=True)]
    dot_general x7 -> x0, matrix products: 34.3 us -> none  [the longest x1 15.8 us: on_device(): down_terms = jnp.dot(hidden, w_down, preferred_element_type=jnp.float32)]
    all_gather x0 -> x1, blocking collectives: none -> 26.2 us  [on_device(): tab = lax.all_gather(tab, 'loc', axis=0, tiled=True).reshape(-1)]
    slice x6 -> x0, local copies, waits for them, and re-layouts: 22.5 us -> none  [the longest x2 10.1 us: on_device(): listed[:, :, :col_count].reshape(blocks_here, key_total, heads_here, HD)]
    all_to_all x1 -> x0, blocking collectives: 15.3 us -> none  [on_device(): lax.all_to_all(request_ids, 'loc', split_axis=0, concat_axis=0, tiled=True)]
  transfers between devices with their start and end apart: 7 -> 1, of which waited for: 6 -> 0; matrix products, arithmetic and copies ran while one was open for 4% -> 1% of each run, Pallas kernels for 0% -> 67%
where the time goes in v1:
time: 204 us; the launch traced here: 202 us
  Pallas kernels  154 us (75%)
  blocking collectives  26.2 us (13%)
  between operations  13.5 us (7%)
  local copies, waits for them, and re-layouts  7.2 us (4%)
    pallas_call x1, Pallas kernels, gather_call(): pl.pallas_call(gather_kernel, out_shape=(jax.ShapeDtypeStruct(plane_shape...  81.4 us
    pallas_call x1, Pallas kernels, merge_call(): pl.pallas_call(merge_kernel, out_shape=(jax.ShapeDtypeStruct((GROUP, WIDT...  38.1 us
    all_gather x1, blocking collectives, on_device(): tab = lax.all_gather(tab, 'loc', axis=0, tiled=True).reshape(-1)  26.2 us
    pallas_call x1, Pallas kernels, mlp_call(): pl.pallas_call(mlp_kernel, grid=(SIDE * halves,), out_shape=jax.ShapeDtyp...  19.4 us
    pallas_call x1, Pallas kernels, far_call(): pl.pallas_call(far_kernel, out_shape=(o_shape, s_shape, o_shape, s_shape)...  15.6 us
    unnamed x14, local copies, waits for them, and re-layouts  6.21 us
  transfers between devices with their start and end apart: 1, of which 0 were waited for; matrix products, arithmetic and copies ran while one was open for 1% of the time, Pallas kernels for 67%

profile of v1, /device:TPU:1, one launch (start us, length us, event | category | flops | bytes accessed | tf_op | source)
XLA Modules:
  0.0 202.1 jit_solution(17277740742383312272)
XLA Ops:
  6.5 0.0 all-gather.2.cloned.1.call-start
  6.5 0.9 constant_dynamic-slice_fusion
  7.4 0.7 pad_maximum_fusion
  8.1 0.0 all-gather.2.cloned.1.call-update
  8.1 0.8 copy.12
  8.9 0.8 copy.13
  9.6 0.8 copy.14
  10.4 0.1 pad_add_fusion
  10.5 26.2 %all_gather.6 = s32[256,12]{1,0:T(8,128)S(1)} all-gather(s32[8,12]{1,0:T(8,128)S(1)} %pad_add_fusion), channel_id=1, replica_groups=mesh['loc'=32,'head'=4] {'loc'}, dimensions={0}, use_global_device_ids=true | all-gather | bytes 12672 | tf_op jit(solution)/shard_map/all_gather | solution.py:638
  36.7 0.1 reshape.12.tab
  36.8 0.0 copy-start
  36.8 1.4 copy-done
  38.2 0.0 copy-start.2
  38.2 1.0 copy-done.2
  39.2 0.0 copy-start.3
  39.2 0.7 copy-done.3
  39.9 81.4 %gather_project.1 = (bf16[2,4,8,3,128,128]{5,4,3,2,1,0:T(8,128)(2,1)S(1)}, bf16[2,4,8,3,128,128]{5,4,3,2,1,0:T(8,128)(2,1)}, f32[8,2,128,128]{3,2,1,0:T(8,128)S(...) custom-call(bf16[1024,256]{1,0:T(8,128)(2,1)S(1)} %copy-done.2, f32[1,1024]{1,0:T(1,128)S(1)} %bitcast.3, ...), custom_call_target="tpu_custom_call" | custom-call | tf_op jit(solution)/shard_map/gather_project/pallas_call | solution.py:280
  121.3 0.0 copy-start.1
  121.3 0.0 copy-start.4
  121.3 15.6 %far_partials.1 = (bf16[4,8,128,128]{3,2,1,0:T(8,128)(2,1)S(1)}, f32[4,8,8,128]{3,2,1,0:T(8,128)S(1)}, bf16[4,8,128,128]{3,2,1,0:T(8,128)(2,1)S(1)}, f32[4,8,8,128]{3,2,1,0:T(8,128)S(1)}) custom-call(s32[3072]{0:T(1024)S(1)} %reshape.12.tab, bf16[2,4,8,3,128,128]{5,4,3,2,1,0:T(8,128)(2,1)S(1)} %get-tuple-element.16.xbuf, ...), custom_call_target="tpu_custom_call" | custom-call | tf_op jit(solution)/shard_map/far_partials/pallas_call | solution.py:394
  137.0 0.0 copy-done.1
  137.0 0.0 copy-done.4
  137.0 38.1 %merge_project.1 = (f32[256,1024]{1,0:T(8,128)S(1)}, bf16[256,1024]{1,0:T(8,128)(2,1)S(1)}) custom-call(bf16[4,8,128,128]{3,2,1,0:T(8,128)(2,1)S(1)} %get-tuple-element.18.oa, f32[4,8,8,128]{3,2,1,0:T(8,128)S(1)} %get-tuple-element.19.sa, bf16[4,8,128,128]{3,2,1,0:T(8,128)(2,1)S(1)} %get-tuple-element.20.ob, f32[4,8,8,128]{3,2,1,0:T(8,128)S(1)} %get-tuple-element.21.sb, ...), custom_call_target="tpu_custom_call" | custom-call | tf_op jit(solution)/shard_map/merge_project/pallas_call | solution.py:526
  175.1 0.0 all-gather.2.cloned.1.call-done
  175.1 19.4 %mlp_exchange.1 = bf16[1024,256]{1,0:T(8,128)(2,1)S(1)} custom-call(bf16[256,1024]{1,0:T(8,128)(2,1)S(1)} %get-tuple-element.25.inner, f32[256,1024]{1,0:T(8,128)S(1)} %get-tuple-element.26.mixed, bf16[4,32,2,32,1024]{4,3,2,1,0:T(8,128)(2,1)} %bitcast.5, bf16[4,32,2,32,1024]{4,3,2,1,0:T(8,128)(2,1)} %bitcast.6), custom_call_target="tpu_custom_call" | custom-call | tf_op jit(solution)/shard_map/mlp_exchange/pallas_call | solution.py:600
  194.5 0.8 copy.16
Async XLA Ops:
  6.5 168.6 %all-gather.2.cloned.1.call-start = ((), (), s32[]{:S(2)}) async-start(), calls=%async_computation | async-start | bytes 16908288 | tf_op jit(solution)/shard_map/all_gather | solution.py:635
  36.8 1.4 copy-start
  38.2 1.0 copy-start.2
  39.2 0.7 copy-start.3
  121.3 15.6 %copy-start.1 = (bf16[256,1024]{1,0:T(8,128)(2,1)S(1)}, bf16[256,1024]{1,0:T(8,128)(2,1)}, u32[]{:S(2)}) copy-start(bf16[256,1024]{1,0:T(8,128)(2,1)} %w_out.1) | copy-start | bytes 1572868
  121.3 15.6 %copy-start.4 = (f32[1024]{0:T(1024)S(1)}, f32[1024]{0:T(1024)}, u32[]{:S(2)}) copy-start(f32[1024]{0:T(1024)} %param.14) | copy-start | bytes 12292
Sparse Core Ops, SparseCore 0:
  10.5 109.1 all-gather.1

commit v2 on v1

--- a/solution.py
+++ b/solution.py
@@ -21,6 +21,7 @@
 PART = WIDTH // SIDE
 NEG = -1e30
 MB = 2**20
+UNITS = 32
 
 
 def coords():
@@ -74,17 +75,35 @@
 
 
 def gather_kernel(
-    ent, gain, wqkv, xbuf, ybuf, near_o, near_st, ent_rows,
-    zbuf, xown, yown, halo_low, halo_high,
-    zs, zr, xs, xr, ys, yr, cs, cr, hs, hr, ls,
+    ent, gain, wqkv, owner, local_at, live, up_hbm, down_hbm,
+    xbuf, ybuf, near_o, near_st, ent_rows, key_a, key_b, wz, wline,
+    zbuf, xown, yown, halo_low, halo_high, tab, tab_y, tab_x, up_cols, up_rows, piece,
+    zs, zr, xs, xr, ys, yr, cs, cr, hs, hr, ls, ts, tr, ws, wr, wl,
 ):
     y, x, core, z = coords()
+    loc = lax.axis_index("loc")
+    load_up = pltpu.make_async_copy(
+        up_hbm.at[:, pl.ds(pl.multiple_of(loc // 4 * BLK, BLK), BLK)], up_cols, wl.at[0]
+    )
+    load_down = pltpu.make_async_copy(
+        down_hbm.at[pl.ds(pl.multiple_of(loc * UNITS, UNITS), UNITS)],
+        piece.at[pl.ds(UNITS, UNITS)],
+        wl.at[1],
+    )
+    load_up.start()
+    load_down.start()
+    tab[...] = jnp.zeros((NB, BLK), jnp.int32)
+    tab[:, 0:4] = (owner[...] * NB + local_at[...]) * 2 + live[...]
     z_up, z_dn = shifted("z", 1), shifted("z", -1)
     x_up, x_dn = shifted("x", 1), shifted("x", -1)
     y_up, y_dn = shifted("y", 1), shifted("y", -1)
     sib = shifted("c", 0)
     nxt, prv = loc_shifted(1), loc_shifted(-1)
-    greet([z_up, z_dn, x_up, x_dn, y_up, y_dn, sib, nxt, prv])
+    w_place = x * (1 - core) + y * core
+    w_up_to = device(y + core, x + 1 - core, core, z)
+    w_dn_to = device(y + 3 * core, x + 3 * (1 - core), core, z)
+    y_opp, x_opp = shifted("y", 2), shifted("x", 2)
+    greet([z_up, z_dn, x_up, x_dn, y_up, y_dn, sib, nxt, prv, y_opp, x_opp])
     rows = ROWS // CHUNKS
     blocks = NB // CHUNKS
     pending = []
@@ -103,6 +122,12 @@
                 go(remote(ent.at[at], zbuf.at[z, at], zs.at[r, 1], zr.at[r, 1], z_dn)),
             )
         )
+    tab_copies = []
+    for k, (dst, place, peers) in enumerate(
+        ((tab_y, y, (y_up, y_dn, y_opp)), (tab_x, x, (x_up, x_dn, x_opp)))
+    ):
+        for n, peer in enumerate(peers):
+            tab_copies.append(go(remote(tab, dst.at[place], ts.at[k, n], tr.at[k, n], peer)))
     zbuf[z] = ent[...]
     z_far = []
 
@@ -193,8 +218,6 @@
             d.wait_recv()
             to_sibling(buf, s, high, r * 10 + k * 5 + 4)
 
-    loc = lax.axis_index("loc")
-
     def near(b):
         for p, (own, other) in enumerate(((xown, yown), (yown, xown))):
             query = split_heads(other[b, 2])
@@ -228,6 +251,16 @@
             near_st[b, p, 3:4] = total[:, BLK:]
             near_st[b, p, 4:8] = jnp.zeros((4, BLK), F32)
 
+    load_up.wait()
+    load_down.wait()
+    up_rows[...] = up_cols[...].astype(F32).T
+    piece[0:UNITS] = up_rows[pl.ds(pl.multiple_of(loc % 4 * UNITS, UNITS), UNITS)].astype(BF16)
+    w_local = pltpu.make_async_copy(piece, wz.at[z], wl.at[2])
+    w_local.start()
+    wz_a = go(remote(piece, wz.at[z], ws.at[0], wr.at[0], z_up))
+    wz_b = go(remote(piece, wz.at[z], ws.at[1], wr.at[1], z_dn))
+    tab_y[y] = tab[...]
+    tab_x[x] = tab[...]
     z_forward(0)
     z_forward(1)
     project(0)
@@ -237,6 +270,13 @@
     z_forward(2)
     project(1)
     z_forward(3)
+    low, high = pl.ds(0, UNITS), pl.ds(UNITS, UNITS)
+    wz_a.wait_recv()
+    view = wz.at[(z + 3) % 4, low]
+    wz_c = go(remote(view, view, ws.at[2], wr.at[2], z_up))
+    wz_b.wait_recv()
+    view = wz.at[(z + 1) % 4, high]
+    wz_d = go(remote(view, view, ws.at[3], wr.at[3], z_dn))
     project(2)
     plane_forward(0)
     project(3)
@@ -257,13 +297,37 @@
     near(5)
     plane_forward(3)
     plane_finish(1)
+    wz_c.wait_recv()
+    wz_d.wait_recv()
+    w_local.wait()
+    wl_a = go(remote(wz, wline.at[w_place], ws.at[4], wr.at[4], w_up_to))
+    wl_b = go(remote(wz, wline.at[w_place], ws.at[5], wr.at[5], w_dn_to))
+    w_local = pltpu.make_async_copy(wz, wline.at[w_place], wl.at[3])
+    w_local.start()
     near(6)
     for copy in halos:
         copy.wait_recv()
     near(7)
     plane_finish(2)
     near(0)
+    for copy in tab_copies:
+        copy.wait_recv()
+    code = tab_y[...]
+    at_key = code // 16 % 2 * 32 + code // 32 % 4 * NB + code // 2 % NB
+    key_a[...] = jnp.where((code % 2 == 1) & (code // 128 == y), at_key, -1)
+    code = tab_x[...]
+    at_key = code // 16 % 2 * 32 + code // 128 * NB + code // 2 % NB
+    key_b[...] = jnp.where((code % 2 == 1) & (code // 32 % 4 == x), at_key, -1)
     plane_finish(3)
+    wl_a.wait_recv()
+    view = wline.at[(w_place + 3) % 4, pl.ds(0, 2)]
+    wl_c = go(remote(view, view, ws.at[6], wr.at[6], w_up_to))
+    wl_b.wait_recv()
+    view = wline.at[(w_place + 1) % 4, pl.ds(2, 2)]
+    wl_d = go(remote(view, view, ws.at[7], wr.at[7], w_dn_to))
+    wl_c.wait_recv()
+    wl_d.wait_recv()
+    w_local.wait()
     for copy in core_copies:
         copy.wait_recv()
     for copy in local_copies:
@@ -272,7 +336,7 @@
         copy.wait_send()
 
 
-def gather_call(ent, gain, wqkv):
+def gather_call(ent, gain, wqkv, owner, local_at, live, w_up, w_down):
     vmem = pl.BlockSpec(memory_space=pltpu.VMEM)
     hbm = pl.BlockSpec(memory_space=pl.ANY)
     dma = pltpu.SemaphoreType.DMA
@@ -285,62 +349,84 @@
             jax.ShapeDtypeStruct((NB, 2, BLK, BLK), F32),
             jax.ShapeDtypeStruct((NB, 2, 8, BLK), F32),
             jax.ShapeDtypeStruct((GROUP, WIDTH), BF16),
+            jax.ShapeDtypeStruct((SIDE, NB, BLK), jnp.int32),
+            jax.ShapeDtypeStruct((SIDE, NB, BLK), jnp.int32),
+            jax.ShapeDtypeStruct((SIDE, 2 * UNITS, WIDTH), BF16),
+            jax.ShapeDtypeStruct((SIDE, SIDE, 2 * UNITS, WIDTH), BF16),
         ),
-        in_specs=[vmem] * 3,
-        out_specs=(hbm, hbm, vmem, vmem, vmem),
+        in_specs=[vmem] * 6 + [hbm] * 2,
+        out_specs=(hbm, hbm, vmem, vmem, vmem, vmem, vmem, hbm, hbm),
         scratch_shapes=[
             pltpu.VMEM((SIDE, ROWS, PART), BF16),
             pltpu.VMEM((NB, 3, BLK, BLK), BF16),
             pltpu.VMEM((NB, 3, BLK, BLK), BF16),
             pltpu.VMEM((2, 2, BLK, BLK), BF16),
             pltpu.VMEM((2, 2, BLK, BLK), BF16),
+            pltpu.VMEM((NB, BLK), jnp.int32),
+            pltpu.VMEM((SIDE, NB, BLK), jnp.int32),
+            pltpu.VMEM((SIDE, NB, BLK), jnp.int32),
+            pltpu.VMEM((WIDTH, BLK), BF16),
+            pltpu.VMEM((BLK, WIDTH), F32),
+            pltpu.VMEM((2 * UNITS, WIDTH), BF16),
             dma((CHUNKS, 4)), dma((CHUNKS, 4)),
             dma((CHUNKS, 4)), dma((CHUNKS, 4)),
             dma((CHUNKS, 4)), dma((CHUNKS, 4)),
             dma((CHUNKS * 10,)), dma((CHUNKS * 10,)),
             dma((4,)), dma((4,)),
             dma((CHUNKS * 2,)),
+            dma((2, 3)), dma((2, 3)),
+            dma((8,)), dma((8,)),
+            dma((4,)),
         ],
         compiler_params=pltpu.CompilerParams(
             collective_id=0, has_side_effects=True, vmem_limit_bytes=40 * MB
         ),
         name="gather_project",
-    )(ent, gain, wqkv)
-
-
-def far_kernel(tab, xbuf, ybuf, oa, sa, ob, sb, acc, state, hits):
-    y, x, core, z = coords()
+    )(ent, gain, wqkv, owner, local_at, live, w_up, w_down)
+
+
+def far_kernel(key_a, key_b, x_hbm, y_hbm, oa, sa, ob, sb, xbuf, ybuf, acc, state, hits_a, hits_b, sems):
+    core = lax.axis_index("loc") % 2
     live_q = SIDE * NB
-
-    for pair in range(2):
-        def find(i, count, pair=pair):
-            s, b = i // NB, i % NB
-            loc = (s * 4 + x) * 2 + core if pair == 0 else (y * 4 + s) * 2 + core
-            base = (loc * NB + b) * 12
-            for j in range(4):
-                owner, local, live = tab[base + j], tab[base + 4 + j], tab[base + 8 + j]
-                oy, ox, oc = owner // 8, (owner // 2) % 4, owner % 2
-                if pair == 0:
-                    mine, place = oy == y, ox
-                else:
-                    mine, place = ox == x, oy
-                hits[count] = i * 1024 + (oc * 4 + place) * NB + local
-                count = count + jnp.where(mine & (live == 1), 1, 0)
-            return count
-
-        count = lax.fori_loop(0, live_q, find, 0)
+    loads = [
+        pltpu.make_async_copy(x_hbm, xbuf, sems.at[0]),
+        pltpu.make_async_copy(y_hbm, ybuf, sems.at[1]),
+    ]
+    for load in loads:
+        load.start()
+
+    def find(i, counts):
+        count_a, count_b = counts
+        s, b = i // NB, i % NB
+        for j in range(4):
+            key = key_a[s, b, j]
+            hits_a[count_a] = i * 1024 + key
+            count_a = count_a + jnp.where(key >= 0, 1, 0)
+            key = key_b[s, b, j]
+            hits_b[count_b] = i * 1024 + key
+            count_b = count_b + jnp.where(key >= 0, 1, 0)
+        return count_a, count_b
+
+    counts = lax.fori_loop(0, live_q, find, (0, 0))
+    for hits, count in zip((hits_a, hits_b), counts):
         for extra in range(4):
             hits[count + extra] = live_q * 1024
+
+    def clear(i, carry):
+        acc[i] = jnp.zeros((BLK, BLK), F32)
+        state[i, 0:2] = jnp.full((2, BLK), NEG, F32)
+        state[i, 2:8] = jnp.zeros((6, BLK), F32)
+        return carry
+
+    lax.fori_loop(0, 2 * (live_q + 1), clear, 0)
+    for load in loads:
+        load.wait()
+
+    for pair in range(2):
+        hits, count = (hits_a, counts[0]) if pair == 0 else (hits_b, counts[1])
         keys_ref, query_ref = (xbuf, ybuf) if pair == 0 else (ybuf, xbuf)
         o_ref, s_ref = (oa, sa) if pair == 0 else (ob, sb)
-
-        def clear(i, carry):
-            acc[i] = jnp.zeros((BLK, BLK), F32)
-            state[i, 0:2] = jnp.full((2, BLK), NEG, F32)
-            state[i, 2:8] = jnp.zeros((6, BLK), F32)
-            return carry
-
-        lax.fori_loop(0, live_q + 1, clear, 0)
+        base = pair * (live_q + 1)
 
         def four(step, carry):
             work = []
@@ -357,7 +443,7 @@
                 weight = jnp.exp(score - top)
                 total = jnp.sum(weight, axis=0, keepdims=True)
                 out = jnp.dot(val, weight.astype(BF16), preferred_element_type=F32)
-                work.append((q, top, total, out))
+                work.append((q + base, top, total, out))
             for q, top, total, out in work:
                 for h in range(2):
                     cut = slice(h * BLK, (h + 1) * BLK)
@@ -375,46 +461,59 @@
 
         def finish(i, carry):
             s, b = i // NB, i % NB
-            st = state[i]
+            st = state[base + i]
             s_ref[s, b] = st
             for h in range(2):
                 total = st[2 + h : 3 + h]
                 scale = 1.0 / jnp.where(total > 0, total, 1.0)
                 feat = pl.ds(h * HD, HD)
-                o_ref[s, b, feat] = (acc[i, feat] * scale).astype(BF16)
+                o_ref[s, b, feat] = (acc[base + i, feat] * scale).astype(BF16)
             return carry
 
         lax.fori_loop(0, live_q, finish, 0)
 
 
-def far_call(tab, xbuf, ybuf):
+def far_call(key_a, key_b, xbuf, ybuf):
     vmem = pl.BlockSpec(memory_space=pltpu.VMEM)
+    smem = pl.BlockSpec(memory_space=pltpu.SMEM)
+    hbm = pl.BlockSpec(memory_space=pl.ANY)
     o_shape = jax.ShapeDtypeStruct((SIDE, NB, BLK, BLK), BF16)
     s_shape = jax.ShapeDtypeStruct((SIDE, NB, 8, BLK), F32)
     return pl.pallas_call(
         far_kernel,
         out_shape=(o_shape, s_shape, o_shape, s_shape),
-        in_specs=[pl.BlockSpec(memory_space=pltpu.SMEM), vmem, vmem],
+        in_specs=[smem, smem, hbm, hbm],
         out_specs=(vmem,) * 4,
         scratch_shapes=[
-            pltpu.VMEM((SIDE * NB + 1, BLK, BLK), F32),
-            pltpu.VMEM((SIDE * NB + 1, 8, BLK), F32),
+            pltpu.VMEM(xbuf.shape, BF16),
+            pltpu.VMEM(ybuf.shape, BF16),
+            pltpu.VMEM((2 * (SIDE * NB + 1), BLK, BLK), F32),
+            pltpu.VMEM((2 * (SIDE * NB + 1), 8, BLK), F32),
             pltpu.SMEM((SIDE * NB * 4 + 8,), jnp.int32),
+            pltpu.SMEM((SIDE * NB * 4 + 8,), jnp.int32),
+            pltpu.SemaphoreType.DMA((2,)),
         ],
         compiler_params=pltpu.CompilerParams(vmem_limit_bytes=40 * MB),
         name="far_partials",
-    )(tab, xbuf, ybuf)
+    )(key_a, key_b, xbuf, ybuf)
 
 
 def merge_kernel(
-    oa, sa, ob, sb, near_o, near_st, ent_rows, w_out, gain, mixed, inner,
+    oa, sa, ob, sb, near_o, near_st, ent_rows, w_out, gain, wline, result,
     ra, rsa, rb, rsb, relay, relay_st, att, part, got_half, got,
-    os, orr, fs, fr, zs, zr,
+    weights, inner, acc, send_sib, got_sib, res, landed,
+    os, orr, fs, fr, zs, zr, ws, wr, wl, ss, sr, es, er,
 ):
     y, x, core, z = coords()
     z_up, z_dn = shifted("z", 1), shifted("z", -1)
+    z_opp, sib = shifted("z", 2), shifted("c", 0)
     peers = [shifted("y", 1), shifted("y", -1), shifted("x", 1), shifted("x", -1), z_up, z_dn]
-    greet(peers)
+    w_place = y * (1 - core) + x * core
+    w_up_to = device(y + 1 - core, x + core, core, z)
+    w_dn_to = device(y + 3 * (1 - core), x + 3 * core, core, z)
+    greet(peers + [z_opp, sib])
+    w_local = pltpu.make_async_copy(wline, weights.at[w_place], wl)
+    w_local.start()
     pending = []
 
     def go(copy):
@@ -464,6 +563,22 @@
             )
         for pair in direct:
             arrivals.extend(pair)
+    w_up_copies, w_dn_copies = [None] * 4, [None] * 4
+    for n in range(SIDE):
+        u, d = n, (n + 2) % 4
+        dst = weights.at[w_place]
+        w_up_copies[u] = go(remote(wline.at[u], dst.at[u], ws.at[0, u], wr.at[0, u], w_up_to))
+        w_dn_copies[d] = go(remote(wline.at[d], dst.at[d], ws.at[1, d], wr.at[1, d], w_dn_to))
+    w_far = []
+
+    def weights_forward(n):
+        w_up_copies[n].wait_recv()
+        view = weights.at[(w_place + 3) % 4, n]
+        w_far.append(go(remote(view, view, ws.at[2, n], wr.at[2, n], w_up_to)))
+        w_dn_copies[n + 2].wait_recv()
+        view = weights.at[(w_place + 1) % 4, n + 2]
+        w_far.append(go(remote(view, view, ws.at[2, n + 2], wr.at[2, n + 2], w_dn_to)))
+
     ra[y] = oa[y]
     rsa[y] = sa[y]
     rb[x] = ob[x]
@@ -511,26 +626,75 @@
     part[2, h:] = (to_dn[h:] + got_half[1].astype(F32)).astype(BF16)
     s_dn = go(remote(part.at[2], got.at[1], zs.at[3], zr.at[3], z_dn))
     mine = project(z) + ent_rows[...].astype(F32)
+    weights_forward(0)
     s_up.wait_recv()
     s_dn.wait_recv()
-    total = mine + got[0].astype(F32) + got[1].astype(F32)
-    mixed[...] = total
-    inner[...] = norm_rows(total, gain[...]).astype(BF16)
+    mixed = mine + got[0].astype(F32) + got[1].astype(F32)
+    inner[core] = norm_rows(mixed, gain[...]).astype(BF16)
+    to_sib = go(remote(inner.at[core], inner.at[core], ss.at[0], sr.at[0], sib))
+    acc[core] = mixed
+    acc[1 - core] = jnp.zeros((GROUP, WIDTH), F32)
+    weights_forward(1)
+    w_local.wait()
+
+    def mlp(slot, who):
+        w_up = weights[slot, :, :, 0:UNITS].reshape(SIDE * SIDE * UNITS, WIDTH)
+        w_down = weights[slot, :, :, UNITS:].reshape(SIDE * SIDE * UNITS, WIDTH)
+        hidden = lax.dot_general(
+            inner[who], w_up, (((1,), (1,)), ((), ())), preferred_element_type=F32
+        )
+        acc[who] += jnp.dot(gelu(hidden).astype(BF16), w_down, preferred_element_type=F32)
+
+    def mlp_both(slot):
+        def body(t, carry):
+            mlp(slot, (core + 1 + t) % 2)
+            return carry
+
+        lax.fori_loop(0, 2, body, 0)
+
+    to_sib.wait_recv()
+    mlp_both(w_place)
+    w_up_copies[2].wait_recv()
+    w_up_copies[3].wait_recv()
+    mlp_both((w_place + 3) % 4)
+    w_dn_copies[0].wait_recv()
+    w_dn_copies[1].wait_recv()
+    mlp_both((w_place + 1) % 4)
+    for copy in w_far:
+        copy.wait_recv()
+    mlp((w_place + 2) % 4, 1 - core)
+    send_sib[...] = acc[1 - core].astype(BF16)
+    back = go(remote(send_sib, got_sib, ss.at[1], sr.at[1], sib))
+    mlp((w_place + 2) % 4, core)
+    back.wait_recv()
+    final = (acc[core] + got_sib[...].astype(F32)).astype(BF16)
+    for s in range(SIDE):
+        res[s] = final[:, s * PART : (s + 1) * PART]
+    copies = []
+    for n, to in ((2, z_opp), (1, z_up), (3, z_dn)):
+        copies.append(go(remote(res.at[(z + n) % 4], landed.at[z], es.at[n], er.at[n], to)))
+    result[pl.ds(pl.multiple_of(z * GROUP, GROUP), GROUP), :] = res[z]
+    for copy in copies:
+        copy.wait_recv()
+    for n in range(1, SIDE):
+        s = (z + n) % 4
+        result[pl.ds(pl.multiple_of(s * GROUP, GROUP), GROUP), :] = landed[s]
     for copy in pending:
         copy.wait_send()
 
 
-def merge_call(oa, sa, ob, sb, near_o, near_st, ent_rows, w_out, gain):
+def gelu(v):
+    return 0.5 * v * (1.0 + lax.erf(v * 0.7071067811865476))
+
+
+def merge_call(oa, sa, ob, sb, near_o, near_st, ent_rows, w_out, gain, wline):
     vmem = pl.BlockSpec(memory_space=pltpu.VMEM)
     dma = pltpu.SemaphoreType.DMA
     return pl.pallas_call(
         merge_kernel,
-        out_shape=(
-            jax.ShapeDtypeStruct((GROUP, WIDTH), F32),
-            jax.ShapeDtypeStruct((GROUP, WIDTH), BF16),
-        ),
-        in_specs=[vmem] * 9,
-        out_specs=(vmem, vmem),
+        out_shape=jax.ShapeDtypeStruct((ROWS, PART), BF16),
+        in_specs=[vmem] * 9 + [pl.BlockSpec(memory_space=pl.ANY)],
+        out_specs=vmem,
         scratch_shapes=[
             pltpu.VMEM((SIDE, NB, BLK, BLK), BF16),
             pltpu.VMEM((SIDE, NB, 8, BLK), F32),
@@ -542,108 +706,44 @@
             pltpu.VMEM((3, GROUP, WIDTH), BF16),
             pltpu.VMEM((2, GROUP // 2, WIDTH), BF16),
             pltpu.VMEM((2, GROUP, WIDTH), BF16),
+            pltpu.VMEM((SIDE, SIDE, SIDE, 2 * UNITS, WIDTH), BF16),
+            pltpu.VMEM((2, GROUP, WIDTH), BF16),
+            pltpu.VMEM((2, GROUP, WIDTH), F32),
+            pltpu.VMEM((GROUP, WIDTH), BF16),
+            pltpu.VMEM((GROUP, WIDTH), BF16),
+            pltpu.VMEM((SIDE, GROUP, PART), BF16),
+            pltpu.VMEM((SIDE, GROUP, PART), BF16),
             dma((2, 2, 4)), dma((2, 2, 4)),
             dma((2, 2, 2)), dma((2, 2, 2)),
+            dma((4,)), dma((4,)),
+            dma((3, 4)), dma((3, 4)), dma,
+            dma((2,)), dma((2,)),
             dma((4,)), dma((4,)),
         ],
         compiler_params=pltpu.CompilerParams(
             collective_id=1, has_side_effects=True, vmem_limit_bytes=40 * MB
         ),
         name="merge_project",
-    )(oa, sa, ob, sb, near_o, near_st, ent_rows, w_out, gain)
-
-
-def gelu(v):
-    return 0.5 * v * (1.0 + lax.erf(v * 0.7071067811865476))
-
-
-def mlp_kernel(inner, mixed, up, down, out, acc, res, landed, ss, rs):
-    step = pl.program_id(0)
-    last = pl.num_programs(0) - 1
-    y, x, core, z = coords()
-
-    @pl.when(step == 0)
-    def _():
-        greet([shifted("z", 1), shifted("z", 2), shifted("z", 3)])
-        acc[...] = mixed[...]
-
-    w_up = up[...].reshape(WIDTH, -1)
-    w_down = down[...].reshape(-1, WIDTH)
-    hidden = gelu(jnp.dot(inner[...], w_up, preferred_element_type=F32)).astype(BF16)
-    acc[...] += jnp.dot(hidden, w_down, preferred_element_type=F32)
-
-    @pl.when(step == last)
-    def _():
-        final = acc[...].astype(BF16)
-        for s in range(SIDE):
-            res[s] = final[:, s * PART : (s + 1) * PART]
-        here = pl.ds(pl.multiple_of(z * GROUP, GROUP), GROUP)
-        copies = []
-        for by in (2, 1, 3):
-            to = (z + by) % 4
-            copies.append(
-                remote(res.at[to], landed.at[z], ss.at[by], rs.at[by], shifted("z", by))
-            )
-            copies[-1].start()
-        out[here, :] = res[z]
-        for copy in copies:
-            copy.wait()
-        for by in range(1, SIDE):
-            s = (z + by) % 4
-            out[pl.ds(pl.multiple_of(s * GROUP, GROUP), GROUP), :] = landed[s]
-
-
-def mlp_call(inner, mixed, weights, halves):
-    vmem = pl.BlockSpec(memory_space=pltpu.VMEM)
-    dma = pltpu.SemaphoreType.DMA
-    unit = WIDTH // halves
-    return pl.pallas_call(
-        mlp_kernel,
-        grid=(SIDE * halves,),
-        out_shape=jax.ShapeDtypeStruct((ROWS, PART), BF16),
-        in_specs=[
-            vmem,
-            vmem,
-            pl.BlockSpec((1, 32, 1, 32, unit), lambda i: (i // halves, 0, 0, 0, i % halves)),
-            pl.BlockSpec((1, 32 // halves, 1, 32, WIDTH), lambda i: (i // halves, i % halves, 1, 0, 0)),
-        ],
-        out_specs=vmem,
-        scratch_shapes=[
-            pltpu.VMEM((GROUP, WIDTH), F32),
-            pltpu.VMEM((SIDE, GROUP, PART), BF16),
-            pltpu.VMEM((SIDE, GROUP, PART), BF16),
-            dma((4,)), dma((4,)),
-        ],
-        compiler_params=pltpu.CompilerParams(
-            collective_id=2, has_side_effects=True, vmem_limit_bytes=40 * MB
-        ),
-        name="mlp_exchange",
-    )(inner, mixed, weights, weights)
+    )(oa, sa, ob, sb, near_o, near_st, ent_rows, w_out, gain, wline)
 
 
 def on_device(
     entities, attn_gain, w_qkv, w_out, mlp_gain, w_up, w_down, far_owner, far_local, far_live
 ):
-    loc = lax.axis_index("loc")
-    piece = jnp.concatenate(
-        [
-            lax.dynamic_slice_in_dim(w_up, loc * 32, 32, 0),
-            lax.dynamic_slice_in_dim(w_down, loc * 32, 32, 0),
-        ],
-        axis=0,
+    xbuf, ybuf, near_o, near_st, ent_rows, key_a, key_b, _, wline = gather_call(
+        entities,
+        attn_gain.reshape(1, WIDTH),
+        w_qkv,
+        far_owner,
+        far_local,
+        far_live,
+        w_up,
+        w_down,
     )
-    weights = lax.all_gather(piece, ("head", "loc"), axis=0, tiled=True)
-    weights = weights.reshape(SIDE, 32, 2, 32, WIDTH)
-    tab = jnp.concatenate([far_owner, far_local, far_live], axis=1)
-    tab = lax.all_gather(tab, "loc", axis=0, tiled=True).reshape(-1)
-    xbuf, ybuf, near_o, near_st, ent_rows = gather_call(
-        entities, attn_gain.reshape(1, WIDTH), w_qkv
+    oa, sa, ob, sb = far_call(key_a, key_b, xbuf, ybuf)
+    return merge_call(
+        oa, sa, ob, sb, near_o, near_st, ent_rows, w_out, mlp_gain.reshape(1, WIDTH), wline
     )
-    oa, sa, ob, sb = far_call(tab, xbuf, ybuf)
-    mixed, inner = merge_call(
-        oa, sa, ob, sb, near_o, near_st, ent_rows, w_out, mlp_gain.reshape(1, WIDTH)
-    )
-    return mlp_call(inner, mixed, weights, 2)
 
 
 def solution(mesh):

time: 204 us -> 154 us (0.75)
  blocking collectives: 26.2 us -> 0 us
  between operations: 13.5 us -> 0.06 us
  Pallas kernels: 154 us -> 142 us
  local copies, waits for them, and re-layouts: 7.2 us -> 12.2 us
    all_gather x1 -> x0, blocking collectives: 26.2 us -> none  [on_device(): tab = lax.all_gather(tab, 'loc', axis=0, tiled=True).reshape(-1)]
    pallas_call x1, Pallas kernels: 81.4 us -> 67.4 us  [gather_call(): pl.pallas_call(gather_kernel, out_shape=(jax.ShapeDtypeStruct(plane_shape...]
    unnamed x14 -> x20, local copies, waits for them, and re-layouts: 6.21 us -> 12.2 us
    pallas_call x2 -> x1, Pallas kernels: 57.4 us -> 63.2 us  [merge_call(): pl.pallas_call(merge_kernel, out_shape=jax.ShapeDtypeStruct((ROWS, PART),...]
    pallas_call x1, Pallas kernels: 15.6 us -> 11.3 us  [far_call(): pl.pallas_call(far_kernel, out_shape=(o_shape, s_shape, o_shape, s_shape)...]
  transfers between devices with their start and end apart: 1 -> 0, of which waited for: 0 -> 0; matrix products, arithmetic and copies ran while one was open for 1% -> 0% of each run, Pallas kernels for 67% -> 0%
where the time goes in v2:
time: 154 us
  Pallas kernels  142 us (92%)
  local copies, waits for them, and re-layouts  12.2 us (8%)
    pallas_call x1, Pallas kernels, gather_call(): pl.pallas_call(gather_kernel, out_shape=(jax.ShapeDtypeStruct(plane_shape...  67.4 us
    pallas_call x1, Pallas kernels, merge_call(): pl.pallas_call(merge_kernel, out_shape=jax.ShapeDtypeStruct((ROWS, PART),...  63.2 us
    unnamed x20, local copies, waits for them, and re-layouts  12.2 us
    pallas_call x1, Pallas kernels, far_call(): pl.pallas_call(far_kernel, out_shape=(o_shape, s_shape, o_shape, s_shape)...  11.3 us

profile of v2, /device:TPU:1, one launch (start us, length us, event | category | flops | bytes accessed | tf_op | source)
XLA Modules:
  0.0 154.1 jit_solution(4516672765420099277)
XLA Ops:
  0.0 0.8 copy.11.owner
  0.8 0.8 copy.12.local_at
  1.5 0.8 copy.13.live
  2.3 0.0 copy-start.1
  2.3 1.6 %copy-done.1 = bf16[1024,1024]{1,0:T(8,128)(2,1)S(1)} copy-done((bf16[1024,1024]{1,0:T(8,128)(2,1)S(1)}, bf16[1024,1024]{1,0:T(8,128)(2,1)}, u32[]{:S(2)}) %copy-start.1) | copy-done | bytes 2097176
  3.9 0.0 copy-start.2
  3.9 1.6 %copy-done.2 = bf16[1024,1024]{1,0:T(8,128)(2,1)S(1)} copy-done((bf16[1024,1024]{1,0:T(8,128)(2,1)S(1)}, bf16[1024,1024]{1,0:T(8,128)(2,1)}, u32[]{:S(2)}) %copy-start.2) | copy-done | bytes 2097176
  5.5 0.0 copy-start.3
  5.5 1.4 copy-done.3
  6.9 0.0 copy-start.4
  6.9 1.0 copy-done.4
  7.9 0.0 copy-start.6
  7.9 0.7 copy-done.6
  8.6 67.4 %gather_project.1 = (bf16[2,4,8,3,128,128]{5,4,3,2,1,0:T(8,128)(2,1)}, bf16[2,4,8,3,128,128]{5,4,3,2,1,0:T(8,128)(2,1)}, f32[8,2,128,128]{3,2,1,0:T(8,128)S(1)},...) custom-call(bf16[1024,256]{1,0:T(8,128)(2,1)S(1)} %copy-done.4, ...), custom_call_target="tpu_custom_call" | custom-call | tf_op jit(solution)/shard_map/gather_project/pallas_call | solution.py:344
  76.0 0.0 copy-start
  76.0 2.8 %copy-done = bf16[2,4,8,3,128,128]{5,4,3,2,1,0:T(8,128)(2,1)S(1)} copy-done((bf16[2,4,8,3,128,128]{5,4,3,2,1,0:T(8,128)(2,1)S(1)}, bf16[2,4,8,3,128,128]{5,4,3,2,1,0:T(8,128)(2,1)}, u32[]{:S(2)}) %copy-start) | copy-done | bytes 6291480
  78.7 0.0 copy-start.5
  78.7 0.0 copy-start.7
  78.7 11.3 %far_partials.1 = (bf16[4,8,128,128]{3,2,1,0:T(8,128)(2,1)S(1)}, f32[4,8,8,128]{3,2,1,0:T(8,128)S(1)}, bf16[4,8,128,128]{3,2,1,0:T(8,128)(2,1)S(1)}, f32[4,8,8,128]{3,2,1,0:T(8,128)S(1)}) custom-call(s32[4,8,128]{2,1,0:T(8,128)S(1)} %get-tuple-element.17.key_a, s32[4,8,128]{2,1,0:T(8,128)S(1)} %get-tuple-element.18.key_b, ...), custom_call_target="tpu_custom_call" | custom-call | tf_op jit(solution)/shard_map/far_partials/pallas_call | solution.py:482
  90.1 0.0 copy-done.5
  90.1 0.0 copy-done.7
  90.1 63.2 %merge_project.1 = bf16[1024,256]{1,0:T(8,128)(2,1)S(1)} custom-call(bf16[4,8,128,128]{3,2,1,0:T(8,128)(2,1)S(1)} %get-tuple-element.21.oa, f32[4,8,8,128]{3,2,1,0:T(8,128)S(1)} %get-tuple-element.22.sa, bf16[4,8,128,128]{3,2,1,0:T(8,128)(2,1)S(1)} %get-tuple-element.23.ob, f32[4,8,8,128]{3,2,1,0:T(8,128)S(1)} %get-tuple-element.24.sb, ...), custom_call_target="tpu_custom_call" | custom-call | tf_op jit(solution)/shard_map/merge_project/pallas_call | solution.py:693
  153.3 0.8 copy.15
Async XLA Ops:
  2.3 1.6 %copy-start.1 = (bf16[1024,1024]{1,0:T(8,128)(2,1)S(1)}, bf16[1024,1024]{1,0:T(8,128)(2,1)}, u32[]{:S(2)}) copy-start(bf16[1024,1024]{1,0:T(8,128)(2,1)} %up_hbm.1) | copy-start | bytes 6291460
  3.9 1.6 %copy-start.2 = (bf16[1024,1024]{1,0:T(8,128)(2,1)S(1)}, bf16[1024,1024]{1,0:T(8,128)(2,1)}, u32[]{:S(2)}) copy-start(bf16[1024,1024]{1,0:T(8,128)(2,1)} %down_hbm.1) | copy-start | bytes 6291460
  5.5 1.4 copy-start.3
  6.9 1.0 copy-start.4
  7.9 0.7 copy-start.6
  76.0 2.8 %copy-start = (bf16[2,4,8,3,128,128]{5,4,3,2,1,0:T(8,128)(2,1)S(1)}, bf16[2,4,8,3,128,128]{5,4,3,2,1,0:T(8,128)(2,1)}, u32[]{:S(2)}) copy-start(bf16[2,4,8,3,128,128]{5,4,3,2,1,0:T(8,128)(2,1)} %get-tuple-element.19.x_hbm) | copy-start | bytes 18874372
  78.7 11.4 %copy-start.5 = (bf16[256,1024]{1,0:T(8,128)(2,1)S(1)}, bf16[256,1024]{1,0:T(8,128)(2,1)}, u32[]{:S(2)}) copy-start(bf16[256,1024]{1,0:T(8,128)(2,1)} %w_out.1) | copy-start | bytes 1572868
  78.7 11.4 %copy-start.7 = (f32[1024]{0:T(1024)S(1)}, f32[1024]{0:T(1024)}, u32[]{:S(2)}) copy-start(f32[1024]{0:T(1024)} %param.14) | copy-start | bytes 12292

commit v3 on v2

--- a/solution.py
+++ b/solution.py
@@ -52,7 +52,10 @@
     barrier = pltpu.get_barrier_semaphore()
     for peer in peers:
         pl.semaphore_signal(barrier, inc=1, device_id=peer, device_id_type=MESH)
-    pl.semaphore_wait(barrier, len(peers))
+
+
+def greeted(peers):
+    pl.semaphore_wait(pltpu.get_barrier_semaphore(), len(peers))
 
 
 def remote(src, dst, send, recv, to):
@@ -74,26 +77,23 @@
     return jnp.concatenate([top, low], axis=0)
 
 
+ORDER = (
+    ("zs", 0), ("zs", 1), ("ts", 0), ("pp", 0), ("zf", 0), ("zs", 2), ("zf", 1), ("zs", 3),
+    ("pr", 0), ("hf", 0), ("zf", 2), ("pr", 1), ("zf", 3), ("ws", 0), ("pf", 0), ("pr", 2),
+    ("pf", 1), ("pr", 3), ("hl", 0), ("pf", 2), ("wf", 0), ("pf", 3), ("ls", 0), ("ro", 0),
+    ("pe", 0), ("n", 1), ("n", 2), ("n", 3), ("n", 4), ("n", 5), ("pe", 1), ("n", 6), ("hw", 0),
+    ("n", 7), ("n", 0), ("ko", 0), ("pe", 2), ("lf", 0), ("pe", 3), ("le", 0),
+)
+
+
 def gather_kernel(
-    ent, gain, wqkv, owner, local_at, live, up_hbm, down_hbm,
+    ent_hbm, gain, wqkv_hbm, owner, local_at, live, up_hbm, down_hbm,
     xbuf, ybuf, near_o, near_st, ent_rows, key_a, key_b, wz, wline,
-    zbuf, xown, yown, halo_low, halo_high, tab, tab_y, tab_x, up_cols, up_rows, piece,
+    ent, wqkv, zbuf, xown, yown, halo_low, halo_high, tab, tab_y, tab_x, up_cols, up_rows, piece,
     zs, zr, xs, xr, ys, yr, cs, cr, hs, hr, ls, ts, tr, ws, wr, wl,
 ):
     y, x, core, z = coords()
     loc = lax.axis_index("loc")
-    load_up = pltpu.make_async_copy(
-        up_hbm.at[:, pl.ds(pl.multiple_of(loc // 4 * BLK, BLK), BLK)], up_cols, wl.at[0]
-    )
-    load_down = pltpu.make_async_copy(
-        down_hbm.at[pl.ds(pl.multiple_of(loc * UNITS, UNITS), UNITS)],
-        piece.at[pl.ds(UNITS, UNITS)],
-        wl.at[1],
-    )
-    load_up.start()
-    load_down.start()
-    tab[...] = jnp.zeros((NB, BLK), jnp.int32)
-    tab[:, 0:4] = (owner[...] * NB + local_at[...]) * 2 + live[...]
     z_up, z_dn = shifted("z", 1), shifted("z", -1)
     x_up, x_dn = shifted("x", 1), shifted("x", -1)
     y_up, y_dn = shifted("y", 1), shifted("y", -1)
@@ -103,7 +103,28 @@
     w_up_to = device(y + core, x + 1 - core, core, z)
     w_dn_to = device(y + 3 * core, x + 3 * (1 - core), core, z)
     y_opp, x_opp = shifted("y", 2), shifted("x", 2)
-    greet([z_up, z_dn, x_up, x_dn, y_up, y_dn, sib, nxt, prv, y_opp, x_opp])
+    peers = [z_up, z_dn, x_up, x_dn, y_up, y_dn, sib, nxt, prv, y_opp, x_opp]
+    greet(peers)
+    load_up = pltpu.make_async_copy(
+        up_hbm.at[:, pl.ds(pl.multiple_of(loc // 4 * BLK, BLK), BLK)], up_cols, wl.at[0]
+    )
+    load_down = pltpu.make_async_copy(
+        down_hbm.at[pl.ds(pl.multiple_of(loc * UNITS, UNITS), UNITS)],
+        piece.at[pl.ds(UNITS, UNITS)],
+        wl.at[1],
+    )
+    load_ent = pltpu.make_async_copy(ent_hbm, ent, wl.at[4])
+    load_qkv = pltpu.make_async_copy(wqkv_hbm, wqkv, wl.at[5])
+    load_ent.start()
+    load_up.start()
+    load_down.start()
+    load_qkv.start()
+    tab[...] = jnp.zeros((NB, BLK), jnp.int32)
+    tab[:, 0:4] = (owner[...] * NB + local_at[...]) * 2 + live[...]
+    tab_y[y] = tab[...]
+    tab_x[x] = tab[...]
+    load_ent.wait()
+    greeted(peers)
     rows = ROWS // CHUNKS
     blocks = NB // CHUNKS
     pending = []
@@ -114,7 +135,8 @@
         return copy
 
     z_near = []
-    for r in range(CHUNKS):
+
+    def z_start(r):
         at = pl.ds(r * rows, rows)
         z_near.append(
             (
@@ -122,13 +144,69 @@
                 go(remote(ent.at[at], zbuf.at[z, at], zs.at[r, 1], zr.at[r, 1], z_dn)),
             )
         )
+
     tab_copies = []
-    for k, (dst, place, peers) in enumerate(
-        ((tab_y, y, (y_up, y_dn, y_opp)), (tab_x, x, (x_up, x_dn, x_opp)))
-    ):
-        for n, peer in enumerate(peers):
-            tab_copies.append(go(remote(tab, dst.at[place], ts.at[k, n], tr.at[k, n], peer)))
-    zbuf[z] = ent[...]
+
+    def tab_start(_):
+        for k, (dst, place, to) in enumerate(
+            ((tab_y, y, (y_up, y_dn, y_opp)), (tab_x, x, (x_up, x_dn, x_opp)))
+        ):
+            for n, peer in enumerate(to):
+                tab_copies.append(go(remote(tab, dst.at[place], ts.at[k, n], tr.at[k, n], peer)))
+
+    lines = {}
+    place_copies = []
+
+    def weights_start(_):
+        load_up.wait()
+        load_down.wait()
+        up_rows[...] = up_cols[...].astype(F32).T
+        piece[0:UNITS] = up_rows[pl.ds(pl.multiple_of(loc % 4 * UNITS, UNITS), UNITS)].astype(BF16)
+        lines["z"] = (
+            go(remote(piece, wz.at[z], ws.at[0], wr.at[0], z_up)),
+            go(remote(piece, wz.at[z], ws.at[1], wr.at[1], z_dn)),
+        )
+        local = pltpu.make_async_copy(piece, wz.at[z], wl.at[2])
+        local.start()
+        place_copies.append(local)
+
+    def line_pass(name, buf, place, sem, up, dn, half):
+        a, b = lines[name]
+        a.wait_recv()
+        view = buf.at[(place + 3) % 4, pl.ds(0, half)]
+        c = go(remote(view, view, ws.at[sem], wr.at[sem], up))
+        b.wait_recv()
+        view = buf.at[(place + 1) % 4, pl.ds(half, half)]
+        d = go(remote(view, view, ws.at[sem + 1], wr.at[sem + 1], dn))
+        lines[name] = (c, d)
+
+    def weights_forward(_):
+        line_pass("z", wz, z, 2, z_up, z_dn, UNITS)
+
+    def line_start(_):
+        for copy in lines["z"]:
+            copy.wait_recv()
+        place_copies.pop().wait()
+        lines["line"] = (
+            go(remote(wz, wline.at[w_place], ws.at[4], wr.at[4], w_up_to)),
+            go(remote(wz, wline.at[w_place], ws.at[5], wr.at[5], w_dn_to)),
+        )
+        local = pltpu.make_async_copy(wz, wline.at[w_place], wl.at[3])
+        local.start()
+        place_copies.append(local)
+
+    def line_forward(_):
+        line_pass("line", wline, w_place, 6, w_up_to, w_dn_to, SIDE // 2)
+
+    def line_finish(_):
+        for copy in lines["line"]:
+            copy.wait_recv()
+        place_copies.pop().wait()
+
+    def prepare(_):
+        zbuf[z] = ent[...]
+        load_qkv.wait()
+
     z_far = []
 
     def z_forward(r):
@@ -251,83 +329,43 @@
             near_st[b, p, 3:4] = total[:, BLK:]
             near_st[b, p, 4:8] = jnp.zeros((4, BLK), F32)
 
-    load_up.wait()
-    load_down.wait()
-    up_rows[...] = up_cols[...].astype(F32).T
-    piece[0:UNITS] = up_rows[pl.ds(pl.multiple_of(loc % 4 * UNITS, UNITS), UNITS)].astype(BF16)
-    w_local = pltpu.make_async_copy(piece, wz.at[z], wl.at[2])
-    w_local.start()
-    wz_a = go(remote(piece, wz.at[z], ws.at[0], wr.at[0], z_up))
-    wz_b = go(remote(piece, wz.at[z], ws.at[1], wr.at[1], z_dn))
-    tab_y[y] = tab[...]
-    tab_x[x] = tab[...]
-    z_forward(0)
-    z_forward(1)
-    project(0)
     halos = []
-    for p, own in enumerate((xown, yown)):
-        halos.append(go(remote(own.at[0, pl.ds(0, 2)], halo_high.at[p], hs.at[p], hr.at[p], prv)))
-    z_forward(2)
-    project(1)
-    z_forward(3)
-    low, high = pl.ds(0, UNITS), pl.ds(UNITS, UNITS)
-    wz_a.wait_recv()
-    view = wz.at[(z + 3) % 4, low]
-    wz_c = go(remote(view, view, ws.at[2], wr.at[2], z_up))
-    wz_b.wait_recv()
-    view = wz.at[(z + 1) % 4, high]
-    wz_d = go(remote(view, view, ws.at[3], wr.at[3], z_dn))
-    project(2)
-    plane_forward(0)
-    project(3)
-    for p, own in enumerate((xown, yown)):
-        halos.append(
-            go(remote(own.at[NB - 1, pl.ds(0, 2)], halo_low.at[p], hs.at[2 + p], hr.at[2 + p], nxt))
-        )
-    ent_rows[...] = jnp.concatenate(
-        [zbuf[s, pl.ds(pl.multiple_of(z * GROUP, GROUP), GROUP), :] for s in range(SIDE)], axis=1
-    )
-    near(1)
-    plane_forward(1)
-    near(2)
-    near(3)
-    plane_forward(2)
-    plane_finish(0)
-    near(4)
-    near(5)
-    plane_forward(3)
-    plane_finish(1)
-    wz_c.wait_recv()
-    wz_d.wait_recv()
-    w_local.wait()
-    wl_a = go(remote(wz, wline.at[w_place], ws.at[4], wr.at[4], w_up_to))
-    wl_b = go(remote(wz, wline.at[w_place], ws.at[5], wr.at[5], w_dn_to))
-    w_local = pltpu.make_async_copy(wz, wline.at[w_place], wl.at[3])
-    w_local.start()
-    near(6)
-    for copy in halos:
-        copy.wait_recv()
-    near(7)
-    plane_finish(2)
-    near(0)
-    for copy in tab_copies:
-        copy.wait_recv()
-    code = tab_y[...]
-    at_key = code // 16 % 2 * 32 + code // 32 % 4 * NB + code // 2 % NB
-    key_a[...] = jnp.where((code % 2 == 1) & (code // 128 == y), at_key, -1)
-    code = tab_x[...]
-    at_key = code // 16 % 2 * 32 + code // 128 * NB + code // 2 % NB
-    key_b[...] = jnp.where((code % 2 == 1) & (code // 32 % 4 == x), at_key, -1)
-    plane_finish(3)
-    wl_a.wait_recv()
-    view = wline.at[(w_place + 3) % 4, pl.ds(0, 2)]
-    wl_c = go(remote(view, view, ws.at[6], wr.at[6], w_up_to))
-    wl_b.wait_recv()
-    view = wline.at[(w_place + 1) % 4, pl.ds(2, 2)]
-    wl_d = go(remote(view, view, ws.at[7], wr.at[7], w_dn_to))
-    wl_c.wait_recv()
-    wl_d.wait_recv()
-    w_local.wait()
+
+    def halo_first(_):
+        for p, own in enumerate((xown, yown)):
+            halos.append(go(remote(own.at[0, pl.ds(0, 2)], halo_high.at[p], hs.at[p], hr.at[p], prv)))
+
+    def halo_last(_):
+        for p, own in enumerate((xown, yown)):
+            src = own.at[NB - 1, pl.ds(0, 2)]
+            halos.append(go(remote(src, halo_low.at[p], hs.at[2 + p], hr.at[2 + p], nxt)))
+
+    def halo_wait(_):
+        for copy in halos:
+            copy.wait_recv()
+
+    def rows_out(_):
+        mine = pl.ds(pl.multiple_of(z * GROUP, GROUP), GROUP)
+        ent_rows[...] = jnp.concatenate([zbuf[s, mine, :] for s in range(SIDE)], axis=1)
+
+    def keys_out(_):
+        for copy in tab_copies:
+            copy.wait_recv()
+        code = tab_y[...]
+        at_key = code // 16 % 2 * 32 + code // 32 % 4 * NB + code // 2 % NB
+        key_a[...] = jnp.where((code % 2 == 1) & (code // 128 == y), at_key, -1)
+        code = tab_x[...]
+        at_key = code // 16 % 2 * 32 + code // 128 * NB + code // 2 % NB
+        key_b[...] = jnp.where((code % 2 == 1) & (code // 32 % 4 == x), at_key, -1)
+
+    steps = {
+        "zs": z_start, "zf": z_forward, "pr": project, "pf": plane_forward, "pe": plane_finish,
+        "n": near, "ts": tab_start, "ws": weights_start, "wf": weights_forward, "ls": line_start,
+        "lf": line_forward, "le": line_finish, "hf": halo_first, "hl": halo_last, "hw": halo_wait,
+        "ro": rows_out, "ko": keys_out, "pp": prepare,
+    }
+    for name, place in ORDER:
+        steps[name](place)
     for copy in core_copies:
         copy.wait_recv()
     for copy in local_copies:
@@ -339,6 +377,7 @@
 def gather_call(ent, gain, wqkv, owner, local_at, live, w_up, w_down):
     vmem = pl.BlockSpec(memory_space=pltpu.VMEM)
     hbm = pl.BlockSpec(memory_space=pl.ANY)
+    pinned = pl.BlockSpec(memory_space=pltpu.HBM)
     dma = pltpu.SemaphoreType.DMA
     plane_shape = (2, SIDE, NB, 3, BLK, BLK)
     return pl.pallas_call(
@@ -354,9 +393,11 @@
             jax.ShapeDtypeStruct((SIDE, 2 * UNITS, WIDTH), BF16),
             jax.ShapeDtypeStruct((SIDE, SIDE, 2 * UNITS, WIDTH), BF16),
         ),
-        in_specs=[vmem] * 6 + [hbm] * 2,
-        out_specs=(hbm, hbm, vmem, vmem, vmem, vmem, vmem, hbm, hbm),
+        in_specs=[pinned, vmem, pinned] + [vmem] * 3 + [pinned] * 2,
+        out_specs=(hbm, hbm) + (vmem,) * 5 + (hbm, hbm),
         scratch_shapes=[
+            pltpu.VMEM((ROWS, PART), BF16),
+            pltpu.VMEM((3, WIDTH, PART), BF16),
             pltpu.VMEM((SIDE, ROWS, PART), BF16),
             pltpu.VMEM((NB, 3, BLK, BLK), BF16),
             pltpu.VMEM((NB, 3, BLK, BLK), BF16),
@@ -376,10 +417,10 @@
             dma((CHUNKS * 2,)),
             dma((2, 3)), dma((2, 3)),
             dma((8,)), dma((8,)),
-            dma((4,)),
+            dma((6,)),
         ],
         compiler_params=pltpu.CompilerParams(
-            collective_id=0, has_side_effects=True, vmem_limit_bytes=40 * MB
+            collective_id=0, has_side_effects=True, vmem_limit_bytes=60 * MB
         ),
         name="gather_project",
     )(ent, gain, wqkv, owner, local_at, live, w_up, w_down)
@@ -476,7 +517,7 @@
 def far_call(key_a, key_b, xbuf, ybuf):
     vmem = pl.BlockSpec(memory_space=pltpu.VMEM)
     smem = pl.BlockSpec(memory_space=pltpu.SMEM)
-    hbm = pl.BlockSpec(memory_space=pl.ANY)
+    hbm = pl.BlockSpec(memory_space=pltpu.HBM)
     o_shape = jax.ShapeDtypeStruct((SIDE, NB, BLK, BLK), BF16)
     s_shape = jax.ShapeDtypeStruct((SIDE, NB, 8, BLK), F32)
     return pl.pallas_call(
@@ -493,7 +534,7 @@
             pltpu.SMEM((SIDE * NB * 4 + 8,), jnp.int32),
             pltpu.SemaphoreType.DMA((2,)),
         ],
-        compiler_params=pltpu.CompilerParams(vmem_limit_bytes=40 * MB),
+        compiler_params=pltpu.CompilerParams(vmem_limit_bytes=58 * MB),
         name="far_partials",
     )(key_a, key_b, xbuf, ybuf)
 
@@ -511,7 +552,9 @@
     w_place = y * (1 - core) + x * core
     w_up_to = device(y + 1 - core, x + core, core, z)
     w_dn_to = device(y + 3 * (1 - core), x + 3 * core, core, z)
-    greet(peers + [z_opp, sib])
+    peers = peers + [z_opp, sib]
+    greet(peers)
+    greeted(peers)
     w_local = pltpu.make_async_copy(wline, weights.at[w_place], wl)
     w_local.start()
     pending = []

time: 154 us -> 151 us (0.981)
  local copies, waits for them, and re-layouts: 12.2 us -> 9.1 us
    pallas_call x1, Pallas kernels: 67.4 us -> 61.6 us  [gather_call(): pl.pallas_call(gather_kernel, out_shape=(jax.ShapeDtypeStruct(plane_shape...]
    pallas_call x1, Pallas kernels: 11.3 us -> 16.8 us  [far_call(): pl.pallas_call(far_kernel, out_shape=(o_shape, s_shape, o_shape, s_shape)...]
    unnamed x20 -> x24, local copies, waits for them, and re-layouts: 12.2 us -> 9.1 us
where the time goes in v3:
time: 151 us; the launch traced here: 150 us
  Pallas kernels  141 us (93%)
  local copies, waits for them, and re-layouts  9.1 us (6%)
    pallas_call x1, Pallas kernels, merge_call(): pl.pallas_call(merge_kernel, out_shape=jax.ShapeDtypeStruct((ROWS, PART),...  62.8 us
    pallas_call x1, Pallas kernels, gather_call(): pl.pallas_call(gather_kernel, out_shape=(jax.ShapeDtypeStruct(plane_shape...  61.6 us
    pallas_call x1, Pallas kernels, far_call(): pl.pallas_call(far_kernel, out_shape=(o_shape, s_shape, o_shape, s_shape)...  16.8 us
    unnamed x24, local copies, waits for them, and re-layouts  9.1 us

profile of v3, /device:TPU:1, one launch (start us, length us, event | category | flops | bytes accessed | tf_op | source)
XLA Modules:
  0.0 150.5 jit_solution(12410841846561864755)
XLA Ops:
  0.0 1.3 copy.11.owner
  1.3 1.3 copy.12.local_at
  2.7 1.4 copy.13.live
  4.0 61.6 %gather_project.1 = (bf16[2,4,8,3,128,128]{5,4,3,2,1,0:T(8,128)(2,1)}, bf16[2,4,8,3,128,128]{5,4,3,2,1,0:T(8,128)(2,1)}, f32[8,2,128,128]{3,2,1,0:T(8,128)}, f32...) custom-call(bf16[1024,256]{1,0:T(8,128)(2,1)} %ent_hbm.1, ...), custom_call_target="tpu_custom_call" | custom-call | tf_op jit(solution)/shard_map/gather_project/pallas_call | solution.py:383
  65.7 0.0 copy-start
  65.7 0.0 copy-start.1
  65.7 0.0 copy-start.4
  65.7 0.0 copy-start.5
  65.7 0.0 copy-start.8
  65.7 0.0 copy-start.9
  65.7 16.8 %far_partials.1 = (bf16[4,8,128,128]{3,2,1,0:T(8,128)(2,1)}, f32[4,8,8,128]{3,2,1,0:T(8,128)}, bf16[4,8,128,128]{3,2,1,0:T(8,128)(2,1)}, f32[4,8,8,128]{3,2,1,0:T(8,128)}) custom-call(s32[4,8,128]{2,1,0:T(8,128)} %get-tuple-element.17.key_a, s32[4,8,128]{2,1,0:T(8,128)} %get-tuple-element.18.key_b, bf16[2,4,8,3,128,128]{5,4,3,2,1,0:T(8,128)(2,1)} %get-tuple-element.19.x_hbm, ...), custom_call_target="tpu_custom_call" | custom-call | tf_op jit(solution)/shard_map/far_partials/pallas_call | solution.py:523
  82.5 0.0 copy-done
  82.6 0.0 copy-done.1
  82.6 0.0 copy-done.4
  82.6 0.0 copy-done.5
  82.6 0.0 copy-done.8
  82.6 0.0 copy-done.9
  82.6 0.0 copy-start.2
  82.6 1.2 copy-done.2
  83.8 0.0 copy-start.3
  83.8 1.2 copy-done.3
  85.1 0.0 copy-start.6
  85.1 0.9 copy-done.6
  86.0 0.0 copy-start.7
  86.0 0.9 copy-done.7
  86.9 62.8 %merge_project.1 = bf16[1024,256]{1,0:T(8,128)(2,1)S(1)} custom-call(bf16[4,8,128,128]{3,2,1,0:T(8,128)(2,1)S(1)} %copy-done.2, f32[4,8,8,128]{3,2,1,0:T(8,128)S(1)} %copy-done.6, bf16[4,8,128,128]{3,2,1,0:T(8,128)(2,1)S(1)} %copy-done.3, f32[4,8,8,128]{3,2,1,0:T(8,128)S(1)} %copy-done.7, f32[8,2,128,128]{3,2,1,0:T(8,128)S(1)} %copy-done.1, ...), custom_call_target="tpu_custom_call" | custom-call | tf_op jit(solution)/shard_map/merge_project/pallas_call | solution.py:736
  149.7 0.8 copy.15
Async XLA Ops:
  65.7 16.9 %copy-start = (bf16[4,4,64,1024]{3,2,1,0:T(8,128)(2,1)S(1)}, bf16[4,4,64,1024]{3,2,1,0:T(8,128)(2,1)}, u32[]{:S(2)}) copy-start(bf16[4,4,64,1024]{3,2,1,0:T(8,128)(2,1)} %get-tuple-element.28.wline) | copy-start | bytes 6291460
  65.7 16.9 %copy-start.1 = (f32[8,2,128,128]{3,2,1,0:T(8,128)S(1)}, f32[8,2,128,128]{3,2,1,0:T(8,128)}, u32[]{:S(2)}) copy-start(f32[8,2,128,128]{3,2,1,0:T(8,128)} %get-tuple-element.25.near_o) | copy-start | bytes 3145732
  65.7 16.9 %copy-start.4 = (bf16[256,1024]{1,0:T(8,128)(2,1)S(1)}, bf16[256,1024]{1,0:T(8,128)(2,1)}, u32[]{:S(2)}) copy-start(bf16[256,1024]{1,0:T(8,128)(2,1)} %w_out.1) | copy-start | bytes 1572868
  65.7 16.9 %copy-start.5 = (bf16[256,1024]{1,0:T(8,128)(2,1)S(1)}, bf16[256,1024]{1,0:T(8,128)(2,1)}, u32[]{:S(2)}) copy-start(bf16[256,1024]{1,0:T(8,128)(2,1)} %get-tuple-element.27.ent_rows) | copy-start | bytes 1572868
  65.7 16.9 %copy-start.8 = (f32[8,2,8,128]{3,2,1,0:T(8,128)S(1)}, f32[8,2,8,128]{3,2,1,0:T(8,128)}, u32[]{:S(2)}) copy-start(f32[8,2,8,128]{3,2,1,0:T(8,128)} %get-tuple-element.26.near_st) | copy-start | bytes 196612
  65.7 16.9 %copy-start.9 = (f32[1024]{0:T(1024)S(1)}, f32[1024]{0:T(1024)}, u32[]{:S(2)}) copy-start(f32[1024]{0:T(1024)} %param.14) | copy-start | bytes 12292
  82.6 1.2 copy-start.2
  83.8 1.2 copy-start.3
  85.1 0.9 copy-start.6
  86.0 0.9 copy-start.7

commit v4 on v3

--- a/solution.py
+++ b/solution.py
@@ -21,6 +21,7 @@
 PART = WIDTH // SIDE
 NEG = -1e30
 MB = 2**20
+TALL = BLK + 16
 UNITS = 32
 
 
@@ -80,16 +81,16 @@
 ORDER = (
     ("zs", 0), ("zs", 1), ("ts", 0), ("pp", 0), ("zf", 0), ("zs", 2), ("zf", 1), ("zs", 3),
     ("pr", 0), ("hf", 0), ("zf", 2), ("pr", 1), ("zf", 3), ("ws", 0), ("pf", 0), ("pr", 2),
-    ("pf", 1), ("pr", 3), ("hl", 0), ("pf", 2), ("wf", 0), ("pf", 3), ("ls", 0), ("ro", 0),
+    ("pf", 1), ("pr", 3), ("hl", 0), ("pf", 2), ("wf", 0), ("pf", 3), ("ro", 0),
     ("pe", 0), ("n", 1), ("n", 2), ("n", 3), ("n", 4), ("n", 5), ("pe", 1), ("n", 6), ("hw", 0),
-    ("n", 7), ("n", 0), ("ko", 0), ("pe", 2), ("lf", 0), ("pe", 3), ("le", 0),
+    ("n", 7), ("n", 0), ("ko", 0), ("pe", 2), ("pe", 3), ("we", 0),
 )
 
 
 def gather_kernel(
-    ent_hbm, gain, wqkv_hbm, owner, local_at, live, up_hbm, down_hbm,
-    xbuf, ybuf, near_o, near_st, ent_rows, key_a, key_b, wz, wline,
-    ent, wqkv, zbuf, xown, yown, halo_low, halo_high, tab, tab_y, tab_x, up_cols, up_rows, piece,
+    ent_hbm, gain, wqkv_hbm, tab, up_hbm, down_hbm,
+    xbuf, ybuf, near_o, near_st, ent_rows, key_a, key_b, wz,
+    ent, wqkv, zbuf, xown, yown, halo_low, halo_high, tab_y, tab_x, up_cols, up_rows, piece,
     zs, zr, xs, xr, ys, yr, cs, cr, hs, hr, ls, ts, tr, ws, wr, wl,
 ):
     y, x, core, z = coords()
@@ -99,9 +100,6 @@
     y_up, y_dn = shifted("y", 1), shifted("y", -1)
     sib = shifted("c", 0)
     nxt, prv = loc_shifted(1), loc_shifted(-1)
-    w_place = x * (1 - core) + y * core
-    w_up_to = device(y + core, x + 1 - core, core, z)
-    w_dn_to = device(y + 3 * core, x + 3 * (1 - core), core, z)
     y_opp, x_opp = shifted("y", 2), shifted("x", 2)
     peers = [z_up, z_dn, x_up, x_dn, y_up, y_dn, sib, nxt, prv, y_opp, x_opp]
     greet(peers)
@@ -119,8 +117,6 @@
     load_up.start()
     load_down.start()
     load_qkv.start()
-    tab[...] = jnp.zeros((NB, BLK), jnp.int32)
-    tab[:, 0:4] = (owner[...] * NB + local_at[...]) * 2 + live[...]
     tab_y[y] = tab[...]
     tab_x[x] = tab[...]
     load_ent.wait()
@@ -183,23 +179,8 @@
     def weights_forward(_):
         line_pass("z", wz, z, 2, z_up, z_dn, UNITS)
 
-    def line_start(_):
+    def weights_finish(_):
         for copy in lines["z"]:
-            copy.wait_recv()
-        place_copies.pop().wait()
-        lines["line"] = (
-            go(remote(wz, wline.at[w_place], ws.at[4], wr.at[4], w_up_to)),
-            go(remote(wz, wline.at[w_place], ws.at[5], wr.at[5], w_dn_to)),
-        )
-        local = pltpu.make_async_copy(wz, wline.at[w_place], wl.at[3])
-        local.start()
-        place_copies.append(local)
-
-    def line_forward(_):
-        line_pass("line", wline, w_place, 6, w_up_to, w_dn_to, SIDE // 2)
-
-    def line_finish(_):
-        for copy in lines["line"]:
             copy.wait_recv()
         place_copies.pop().wait()
 
@@ -351,17 +332,17 @@
     def keys_out(_):
         for copy in tab_copies:
             copy.wait_recv()
-        code = tab_y[...]
+        code = jnp.concatenate([tab_y[s][:, :NB] for s in range(SIDE)], axis=1)
         at_key = code // 16 % 2 * 32 + code // 32 % 4 * NB + code // 2 % NB
         key_a[...] = jnp.where((code % 2 == 1) & (code // 128 == y), at_key, -1)
-        code = tab_x[...]
+        code = jnp.concatenate([tab_x[s][:, :NB] for s in range(SIDE)], axis=1)
         at_key = code // 16 % 2 * 32 + code // 128 * NB + code // 2 % NB
         key_b[...] = jnp.where((code % 2 == 1) & (code // 32 % 4 == x), at_key, -1)
 
     steps = {
         "zs": z_start, "zf": z_forward, "pr": project, "pf": plane_forward, "pe": plane_finish,
-        "n": near, "ts": tab_start, "ws": weights_start, "wf": weights_forward, "ls": line_start,
-        "lf": line_forward, "le": line_finish, "hf": halo_first, "hl": halo_last, "hw": halo_wait,
+        "n": near, "ts": tab_start, "ws": weights_start, "wf": weights_forward, "we": weights_finish,
+        "hf": halo_first, "hl": halo_last, "hw": halo_wait,
         "ro": rows_out, "ko": keys_out, "pp": prepare,
     }
     for name, place in ORDER:
@@ -374,7 +355,7 @@
         copy.wait_send()
 
 
-def gather_call(ent, gain, wqkv, owner, local_at, live, w_up, w_down):
+def gather_call(ent, gain, wqkv, tab, w_up, w_down):
     vmem = pl.BlockSpec(memory_space=pltpu.VMEM)
     hbm = pl.BlockSpec(memory_space=pl.ANY)
     pinned = pl.BlockSpec(memory_space=pltpu.HBM)
@@ -388,13 +369,12 @@
             jax.ShapeDtypeStruct((NB, 2, BLK, BLK), F32),
             jax.ShapeDtypeStruct((NB, 2, 8, BLK), F32),
             jax.ShapeDtypeStruct((GROUP, WIDTH), BF16),
-            jax.ShapeDtypeStruct((SIDE, NB, BLK), jnp.int32),
-            jax.ShapeDtypeStruct((SIDE, NB, BLK), jnp.int32),
+            jax.ShapeDtypeStruct((8, SIDE * NB), jnp.int32),
+            jax.ShapeDtypeStruct((8, SIDE * NB), jnp.int32),
             jax.ShapeDtypeStruct((SIDE, 2 * UNITS, WIDTH), BF16),
-            jax.ShapeDtypeStruct((SIDE, SIDE, 2 * UNITS, WIDTH), BF16),
         ),
-        in_specs=[pinned, vmem, pinned] + [vmem] * 3 + [pinned] * 2,
-        out_specs=(hbm, hbm) + (vmem,) * 5 + (hbm, hbm),
+        in_specs=[pinned, vmem, pinned, vmem, pinned, pinned],
+        out_specs=(hbm, hbm) + (vmem,) * 5 + (hbm,),
         scratch_shapes=[
             pltpu.VMEM((ROWS, PART), BF16),
             pltpu.VMEM((3, WIDTH, PART), BF16),
@@ -403,7 +383,6 @@
             pltpu.VMEM((NB, 3, BLK, BLK), BF16),
             pltpu.VMEM((2, 2, BLK, BLK), BF16),
             pltpu.VMEM((2, 2, BLK, BLK), BF16),
-            pltpu.VMEM((NB, BLK), jnp.int32),
             pltpu.VMEM((SIDE, NB, BLK), jnp.int32),
             pltpu.VMEM((SIDE, NB, BLK), jnp.int32),
             pltpu.VMEM((WIDTH, BLK), BF16),
@@ -423,32 +402,38 @@
             collective_id=0, has_side_effects=True, vmem_limit_bytes=60 * MB
         ),
         name="gather_project",
-    )(ent, gain, wqkv, owner, local_at, live, w_up, w_down)
-
-
-def far_kernel(key_a, key_b, x_hbm, y_hbm, oa, sa, ob, sb, xbuf, ybuf, acc, state, hits_a, hits_b, sems):
+    )(ent, gain, wqkv, tab, w_up, w_down)
+
+
+def far_kernel(
+    key_a, key_b, x_hbm, y_hbm, oa, ob, query, pairs, acc, state, hits_a, hits_b, qs, ks
+):
     core = lax.axis_index("loc") % 2
     live_q = SIDE * NB
-    loads = [
-        pltpu.make_async_copy(x_hbm, xbuf, sems.at[0]),
-        pltpu.make_async_copy(y_hbm, ybuf, sems.at[1]),
-    ]
-    for load in loads:
-        load.start()
-
-    def find(i, counts):
-        count_a, count_b = counts
-        s, b = i // NB, i % NB
-        for j in range(4):
-            key = key_a[s, b, j]
-            hits_a[count_a] = i * 1024 + key
-            count_a = count_a + jnp.where(key >= 0, 1, 0)
-            key = key_b[s, b, j]
-            hits_b[count_b] = i * 1024 + key
-            count_b = count_b + jnp.where(key >= 0, 1, 0)
-        return count_a, count_b
-
-    counts = lax.fori_loop(0, live_q, find, (0, 0))
+    mine = pl.ds(core * live_q, live_q)
+    loads = []
+    for pair, (keys_hbm, query_hbm) in enumerate(((x_hbm, y_hbm), (y_hbm, x_hbm))):
+        loads.append(
+            (
+                pltpu.make_async_copy(query_hbm.at[mine, 2], query.at[pair], qs.at[pair]),
+                pltpu.make_async_copy(keys_hbm.at[:, pl.ds(0, 2)], pairs.at[pair], ks.at[pair]),
+            )
+        )
+    for pair in loads:
+        for load in pair:
+            load.start()
+
+    def find(s, counts):
+        counts = list(counts)
+        for b in range(NB):
+            for j in range(4):
+                for pair, (keys, hits) in enumerate(((key_a, hits_a), (key_b, hits_b))):
+                    key = keys[j, s * NB + b]
+                    hits[counts[pair]] = (s * NB + b) * 1024 + key
+                    counts[pair] = counts[pair] + jnp.where(key >= 0, 1, 0)
+        return tuple(counts)
+
+    counts = lax.fori_loop(0, SIDE, find, (0, 0))
     for hits, count in zip((hits_a, hits_b), counts):
         for extra in range(4):
             hits[count + extra] = live_q * 1024
@@ -460,26 +445,23 @@
         return carry
 
     lax.fori_loop(0, 2 * (live_q + 1), clear, 0)
-    for load in loads:
-        load.wait()
 
     for pair in range(2):
         hits, count = (hits_a, counts[0]) if pair == 0 else (hits_b, counts[1])
-        keys_ref, query_ref = (xbuf, ybuf) if pair == 0 else (ybuf, xbuf)
-        o_ref, s_ref = (oa, sa) if pair == 0 else (ob, sb)
+        o_ref = oa if pair == 0 else ob
         base = pair * (live_q + 1)
+        for load in loads[pair]:
+            load.wait()
 
         def four(step, carry):
             work = []
             for u in range(4):
                 code = hits[step * 4 + u]
-                q, k = code // 1024, code % 1024
-                q_at = jnp.minimum(q, live_q - 1)
-                query = split_heads(query_ref[core, q_at // NB, q_at % NB, 2])
-                kc, kp, kb = k // 32, (k // 8) % 4, k % 8
-                key = keys_ref[kc, kp, kb, 0]
-                val = keys_ref[kc, kp, kb, 1]
-                score = jnp.dot(key, query, preferred_element_type=F32)
+                q, k = lax.shift_right_logical(code, 10), code & 1023
+                asked = split_heads(query[pair, jnp.minimum(q, live_q - 1)])
+                key = pairs[pair, k, 0]
+                val = pairs[pair, k, 1]
+                score = jnp.dot(key, asked, preferred_element_type=F32)
                 top = jnp.max(score, axis=0, keepdims=True)
                 weight = jnp.exp(score - top)
                 total = jnp.sum(weight, axis=0, keepdims=True)
@@ -498,17 +480,21 @@
                     state[q, 2 + h : 3 + h] = state[q, 2 + h : 3 + h] * keep + total[:, cut] * add
             return carry
 
-        lax.fori_loop(0, (count + 3) // 4, four, 0)
+        lax.fori_loop(0, lax.shift_right_logical(count + 3, 2), four, 0)
 
         def finish(i, carry):
-            s, b = i // NB, i % NB
             st = state[base + i]
-            s_ref[s, b] = st
+            left, terms = st[0:4], []
+            for _ in range(3):
+                terms.append(left.astype(BF16).astype(F32))
+                left = left - terms[-1]
+            terms.append(jnp.zeros((4, BLK), F32))
+            o_ref[i, BLK:] = jnp.concatenate(terms, axis=0).astype(BF16)
             for h in range(2):
                 total = st[2 + h : 3 + h]
                 scale = 1.0 / jnp.where(total > 0, total, 1.0)
                 feat = pl.ds(h * HD, HD)
-                o_ref[s, b, feat] = (acc[base + i, feat] * scale).astype(BF16)
+                o_ref[i, feat] = (acc[base + i, feat] * scale).astype(BF16)
             return carry
 
         lax.fori_loop(0, live_q, finish, 0)
@@ -518,32 +504,40 @@
     vmem = pl.BlockSpec(memory_space=pltpu.VMEM)
     smem = pl.BlockSpec(memory_space=pltpu.SMEM)
     hbm = pl.BlockSpec(memory_space=pltpu.HBM)
-    o_shape = jax.ShapeDtypeStruct((SIDE, NB, BLK, BLK), BF16)
-    s_shape = jax.ShapeDtypeStruct((SIDE, NB, 8, BLK), F32)
-    return pl.pallas_call(
+    dma = pltpu.SemaphoreType.DMA
+    live_q = SIDE * NB
+    o_shape = jax.ShapeDtypeStruct((live_q, TALL, BLK), BF16)
+    flat = (2 * live_q, 3, BLK, BLK)
+    oa, ob = pl.pallas_call(
         far_kernel,
-        out_shape=(o_shape, s_shape, o_shape, s_shape),
+        out_shape=(o_shape, o_shape),
         in_specs=[smem, smem, hbm, hbm],
-        out_specs=(vmem,) * 4,
+        out_specs=(vmem, vmem),
         scratch_shapes=[
-            pltpu.VMEM(xbuf.shape, BF16),
-            pltpu.VMEM(ybuf.shape, BF16),
-            pltpu.VMEM((2 * (SIDE * NB + 1), BLK, BLK), F32),
-            pltpu.VMEM((2 * (SIDE * NB + 1), 8, BLK), F32),
-            pltpu.SMEM((SIDE * NB * 4 + 8,), jnp.int32),
-            pltpu.SMEM((SIDE * NB * 4 + 8,), jnp.int32),
-            pltpu.SemaphoreType.DMA((2,)),
+            pltpu.VMEM((2, live_q, BLK, BLK), BF16),
+            pltpu.VMEM((2, 2 * live_q, 2, BLK, BLK), BF16),
+            pltpu.VMEM((2 * (live_q + 1), BLK, BLK), F32),
+            pltpu.VMEM((2 * (live_q + 1), 8, BLK), F32),
+            pltpu.SMEM((live_q * 4 + 8,), jnp.int32),
+            pltpu.SMEM((live_q * 4 + 8,), jnp.int32),
+            dma((2,)),
+            dma((2,)),
         ],
         compiler_params=pltpu.CompilerParams(vmem_limit_bytes=58 * MB),
+        cost_estimate=pl.CostEstimate(
+            flops=8 * 10**9, bytes_accessed=30 * MB, transcendentals=3 * 10**6
+        ),
         name="far_partials",
-    )(key_a, key_b, xbuf, ybuf)
+    )(key_a, key_b, xbuf.reshape(flat), ybuf.reshape(flat))
+    shape = (SIDE, NB, TALL, BLK)
+    return oa.reshape(shape), ob.reshape(shape)
 
 
 def merge_kernel(
-    oa, sa, ob, sb, near_o, near_st, ent_rows, w_out, gain, wline, result,
-    ra, rsa, rb, rsb, relay, relay_st, att, part, got_half, got,
-    weights, inner, acc, send_sib, got_sib, res, landed,
-    os, orr, fs, fr, zs, zr, ws, wr, wl, ss, sr, es, er,
+    oa, ob, near_o_hbm, near_st_hbm, ent_rows_hbm, w_out_hbm, gain, line_0, line_1, line_2, line_3, result,
+    ra, rb, relay, att, part, got_half, got,
+    weights, inner, acc, send_sib, got_sib, res, landed, near_o, near_st, ent_rows, w_out,
+    os, orr, fs, fr, zs, zr, ws, wr, wl, ss, sr, es, er, ls,
 ):
     y, x, core, z = coords()
     z_up, z_dn = shifted("z", 1), shifted("z", -1)
@@ -554,9 +548,28 @@
     w_dn_to = device(y + 3 * (1 - core), x + 3 * core, core, z)
     peers = peers + [z_opp, sib]
     greet(peers)
+    loads = [
+        pltpu.make_async_copy(src, dst, ls.at[n])
+        for n, (src, dst) in enumerate(
+            (
+                (oa.at[y], ra.at[y]),
+                (ob.at[x], rb.at[x]),
+                (near_o_hbm, near_o),
+                (near_st_hbm, near_st),
+                (w_out_hbm, w_out),
+                (ent_rows_hbm, ent_rows),
+            )
+        )
+    ]
+    for load in loads:
+        load.start()
+    line = (line_0, line_1, line_2, line_3)
+    w_local = [
+        pltpu.make_async_copy(line[n], weights.at[w_place, n], wl.at[n]) for n in range(SIDE)
+    ]
+    for copy in w_local:
+        copy.start()
     greeted(peers)
-    w_local = pltpu.make_async_copy(wline, weights.at[w_place], wl)
-    w_local.start()
     pending = []
 
     def go(copy):
@@ -564,54 +577,50 @@
         pending.append(copy)
         return copy
 
-    half = NB // 2
-    lanes = []
-    for k, (place, up, dn, o, st, ro, rst) in enumerate(
-        (
-            (y, peers[0], peers[1], oa, sa, ra, rsa),
-            (x, peers[2], peers[3], ob, sb, rb, rsb),
-        )
-    ):
-        far_to, up_to, dn_to = (place + 2) % 4, (place + 1) % 4, (place + 3) % 4
-        low, high = pl.ds(0, half), pl.ds(half, half)
-        first = []
-        for t, (src, hop, dst) in enumerate(((o, relay, ro), (st, relay_st, rst))):
-            first.append(
-                (
-                    go(remote(src.at[far_to, low], hop.at[k, 0], os.at[k, t, 0], orr.at[k, t, 0], up)),
-                    go(remote(src.at[far_to, high], hop.at[k, 1], os.at[k, t, 1], orr.at[k, t, 1], dn)),
-                )
+    groups = [(z + by) % 4 for by in (2, 1, 3, 0)]
+    per = NB // SIDE
+    lanes = ((y, peers[0], peers[1], oa, ra), (x, peers[2], peers[3], ob, rb))
+    relays, arrivals = {}, {}
+    for n, g in enumerate(groups):
+        arrivals[n] = []
+        for k, (place, up, dn, o, ro) in enumerate(lanes):
+            send, recv = os.at[k, n], orr.at[k, n]
+            far_to, up_to, dn_to = (place + 2) % 4, (place + 1) % 4, (place + 3) % 4
+            relays[k, n] = (
+                go(remote(o.at[far_to, g * per], relay.at[k, n, 0], send.at[0], recv.at[0], up)),
+                go(remote(o.at[far_to, g * per + 1], relay.at[k, n, 1], send.at[1], recv.at[1], dn)),
             )
-        direct = []
-        for t, (src, dst) in enumerate(((o, ro), (st, rst))):
-            direct.append(
-                (
-                    go(remote(src.at[up_to], dst.at[place], os.at[k, t, 2], orr.at[k, t, 2], up)),
-                    go(remote(src.at[dn_to], dst.at[place], os.at[k, t, 3], orr.at[k, t, 3], dn)),
-                )
-            )
-        lanes.append((place, up, dn, ro, rst, first, direct))
-    arrivals = []
-    for k, (place, up, dn, ro, rst, first, direct) in enumerate(lanes):
-        low, high = pl.ds(0, half), pl.ds(half, half)
-        for t, (hop, dst) in enumerate(((relay, ro), (relay_st, rst))):
-            a, b = first[t]
+            both = pl.ds(g * per, per)
+            arrivals[n] += [
+                go(remote(o.at[up_to, both], ro.at[place, both], send.at[2], recv.at[2], up)),
+                go(remote(o.at[dn_to, both], ro.at[place, both], send.at[3], recv.at[3], dn)),
+            ]
+
+    def pass_on(n):
+        g = groups[n]
+        for k, (place, up, dn, o, ro) in enumerate(lanes):
+            a, b = relays[k, n]
             a.wait_recv()
-            arrivals.append(
-                go(remote(hop.at[k, 0], dst.at[(place + 3) % 4, low], fs.at[k, t, 0], fr.at[k, t, 0], up))
-            )
+            dst = ro.at[(place + 3) % 4, g * per]
+            arrivals[n].append(go(remote(relay.at[k, n, 0], dst, fs.at[k, n, 0], fr.at[k, n, 0], up)))
             b.wait_recv()
-            arrivals.append(
-                go(remote(hop.at[k, 1], dst.at[(place + 1) % 4, high], fs.at[k, t, 1], fr.at[k, t, 1], dn))
-            )
-        for pair in direct:
-            arrivals.extend(pair)
+            dst = ro.at[(place + 1) % 4, g * per + 1]
+            arrivals[n].append(go(remote(relay.at[k, n, 1], dst, fs.at[k, n, 1], fr.at[k, n, 1], dn)))
+
+    pass_on(0)
+    pass_on(1)
     w_up_copies, w_dn_copies = [None] * 4, [None] * 4
-    for n in range(SIDE):
-        u, d = n, (n + 2) % 4
-        dst = weights.at[w_place]
-        w_up_copies[u] = go(remote(wline.at[u], dst.at[u], ws.at[0, u], wr.at[0, u], w_up_to))
-        w_dn_copies[d] = go(remote(wline.at[d], dst.at[d], ws.at[1, d], wr.at[1, d], w_dn_to))
+
+    def weights_start():
+        for n in range(SIDE):
+            u, d = n, (n + 2) % 4
+            dst = weights.at[w_place]
+            w_up_copies[u] = go(remote(line[u], dst.at[u], ws.at[0, u], wr.at[0, u], w_up_to))
+            w_dn_copies[d] = go(remote(line[d], dst.at[d], ws.at[1, d], wr.at[1, d], w_dn_to))
+
+    pass_on(2)
+    pass_on(3)
+    weights_start()
     w_far = []
 
     def weights_forward(n):
@@ -622,17 +631,16 @@
         view = weights.at[(w_place + 1) % 4, n + 2]
         w_far.append(go(remote(view, view, ws.at[2, n + 2], wr.at[2, n + 2], w_dn_to)))
 
-    ra[y] = oa[y]
-    rsa[y] = sa[y]
-    rb[x] = ob[x]
-    rsb[x] = sb[x]
-    for copy in arrivals:
-        copy.wait_recv()
+    for load in loads:
+        load.wait()
 
     def merge(b, carry):
-        for p, (ro, rst) in enumerate(((ra, rsa), (rb, rsb))):
-            stats = [near_st[b, p]] + [rst[s, b] for s in range(SIDE)]
-            outs = [near_o[b, p]] + [ro[s, b].astype(F32) for s in range(SIDE)]
+        for p, ro in enumerate((ra, rb)):
+            stats, outs = [near_st[b, p]], [near_o[b, p]]
+            for s in range(SIDE):
+                tail = ro[s, b, BLK:].astype(F32)
+                stats.append(tail[0:4] + tail[4:8] + tail[8:12])
+                outs.append(ro[s, b, :BLK].astype(F32))
             halves = []
             for h in range(2):
                 top = functools.reduce(jnp.maximum, [st[h : h + 1] for st in stats])
@@ -648,28 +656,30 @@
             att[pl.ds(pl.multiple_of(b * BLK, BLK), BLK), p * BLK : (p + 1) * BLK] = tile
         return carry
 
-    lax.fori_loop(0, NB, merge, 0)
-
-    def project(group):
-        rows = att[pl.ds(pl.multiple_of(group * GROUP, GROUP), GROUP), :]
+    def project(n):
+        for copy in arrivals[n]:
+            copy.wait_recv()
+        lax.fori_loop(groups[n] * per, groups[n] * per + per, merge, 0)
+        rows = att[pl.ds(pl.multiple_of(groups[n] * GROUP, GROUP), GROUP), :]
         return jnp.dot(rows, w_out[...], preferred_element_type=F32)
 
     h = GROUP // 2
-    part[0] = project((z + 2) % 4).astype(BF16)
+    part[0] = project(0).astype(BF16)
     f_up = go(remote(part.at[0, pl.ds(0, h)], got_half.at[0], zs.at[0], zr.at[0], z_up))
     f_dn = go(remote(part.at[0, pl.ds(h, h)], got_half.at[1], zs.at[1], zr.at[1], z_dn))
-    to_up = project((z + 1) % 4)
+    to_up = project(1)
     part[1, h:] = to_up[h:].astype(BF16)
-    to_dn = project((z + 3) % 4)
-    part[2, :h] = to_dn[:h].astype(BF16)
     f_up.wait_recv()
     part[1, :h] = (to_up[:h] + got_half[0].astype(F32)).astype(BF16)
     s_up = go(remote(part.at[1], got.at[0], zs.at[2], zr.at[2], z_up))
+    weights_forward(0)
+    to_dn = project(2)
+    part[2, :h] = to_dn[:h].astype(BF16)
     f_dn.wait_recv()
     part[2, h:] = (to_dn[h:] + got_half[1].astype(F32)).astype(BF16)
     s_dn = go(remote(part.at[2], got.at[1], zs.at[3], zr.at[3], z_dn))
-    mine = project(z) + ent_rows[...].astype(F32)
-    weights_forward(0)
+    mine = project(3) + ent_rows[...].astype(F32)
+    weights_forward(1)
     s_up.wait_recv()
     s_dn.wait_recv()
     mixed = mine + got[0].astype(F32) + got[1].astype(F32)
@@ -677,8 +687,8 @@
     to_sib = go(remote(inner.at[core], inner.at[core], ss.at[0], sr.at[0], sib))
     acc[core] = mixed
     acc[1 - core] = jnp.zeros((GROUP, WIDTH), F32)
-    weights_forward(1)
-    w_local.wait()
+    for copy in w_local:
+        copy.wait()
 
     def mlp(slot, who):
         w_up = weights[slot, :, :, 0:UNITS].reshape(SIDE * SIDE * UNITS, WIDTH)
@@ -730,21 +740,19 @@
     return 0.5 * v * (1.0 + lax.erf(v * 0.7071067811865476))
 
 
-def merge_call(oa, sa, ob, sb, near_o, near_st, ent_rows, w_out, gain, wline):
+def merge_call(oa, ob, near_o, near_st, ent_rows, w_out, gain, lines):
     vmem = pl.BlockSpec(memory_space=pltpu.VMEM)
+    hbm = pl.BlockSpec(memory_space=pltpu.HBM)
     dma = pltpu.SemaphoreType.DMA
     return pl.pallas_call(
         merge_kernel,
         out_shape=jax.ShapeDtypeStruct((ROWS, PART), BF16),
-        in_specs=[vmem] * 9 + [pl.BlockSpec(memory_space=pl.ANY)],
+        in_specs=[hbm] * 6 + [vmem] + [hbm] * 4,
         out_specs=vmem,
         scratch_shapes=[
-            pltpu.VMEM((SIDE, NB, BLK, BLK), BF16),
-            pltpu.VMEM((SIDE, NB, 8, BLK), F32),
-            pltpu.VMEM((SIDE, NB, BLK, BLK), BF16),
-            pltpu.VMEM((SIDE, NB, 8, BLK), F32),
-            pltpu.VMEM((2, 2, NB // 2, BLK, BLK), BF16),
-            pltpu.VMEM((2, 2, NB // 2, 8, BLK), F32),
+            pltpu.VMEM((SIDE, NB, TALL, BLK), BF16),
+            pltpu.VMEM((SIDE, NB, TALL, BLK), BF16),
+            pltpu.VMEM((2, SIDE, 2, TALL, BLK), BF16),
             pltpu.VMEM((ROWS, 2 * BLK), BF16),
             pltpu.VMEM((3, GROUP, WIDTH), BF16),
             pltpu.VMEM((2, GROUP // 2, WIDTH), BF16),
@@ -756,36 +764,48 @@
             pltpu.VMEM((GROUP, WIDTH), BF16),
             pltpu.VMEM((SIDE, GROUP, PART), BF16),
             pltpu.VMEM((SIDE, GROUP, PART), BF16),
-            dma((2, 2, 4)), dma((2, 2, 4)),
-            dma((2, 2, 2)), dma((2, 2, 2)),
+            pltpu.VMEM((NB, 2, BLK, BLK), F32),
+            pltpu.VMEM((NB, 2, 8, BLK), F32),
+            pltpu.VMEM((GROUP, WIDTH), BF16),
+            pltpu.VMEM((PART, WIDTH), BF16),
+            dma((2, 4, 4)), dma((2, 4, 4)),
+            dma((2, 4, 2)), dma((2, 4, 2)),
             dma((4,)), dma((4,)),
-            dma((3, 4)), dma((3, 4)), dma,
+            dma((3, 4)), dma((3, 4)), dma((4,)),
             dma((2,)), dma((2,)),
             dma((4,)), dma((4,)),
+            dma((8,)),
         ],
         compiler_params=pltpu.CompilerParams(
-            collective_id=1, has_side_effects=True, vmem_limit_bytes=40 * MB
+            collective_id=1, has_side_effects=True, vmem_limit_bytes=60 * MB
         ),
         name="merge_project",
-    )(oa, sa, ob, sb, near_o, near_st, ent_rows, w_out, gain, wline)
+    )(oa, ob, near_o, near_st, ent_rows, w_out, gain, *lines)
 
 
 def on_device(
     entities, attn_gain, w_qkv, w_out, mlp_gain, w_up, w_down, far_owner, far_local, far_live
 ):
-    xbuf, ybuf, near_o, near_st, ent_rows, key_a, key_b, _, wline = gather_call(
+    xbuf, ybuf, near_o, near_st, ent_rows, key_a, key_b, piece = gather_call(
         entities,
         attn_gain.reshape(1, WIDTH),
         w_qkv,
-        far_owner,
-        far_local,
-        far_live,
+        jnp.pad(((far_owner * NB + far_local) * 2 + far_live).T, ((0, 4), (0, BLK - NB))),
         w_up,
         w_down,
     )
-    oa, sa, ob, sb = far_call(key_a, key_b, xbuf, ybuf)
+    def along(by):
+        pairs = []
+        for i in range(lax.axis_size("loc")):
+            y, x, core = i // 8, i // 2 % 4, i % 2
+            y, x = (y, (x + by) % 4) if core == 0 else ((y + by) % 4, x)
+            pairs.append((i, (y * 4 + x) * 2 + core))
+        return lax.ppermute(piece, "loc", pairs)
+
+    lines = [piece] + [along(by) for by in (2, 1, 3)]
+    oa, ob = far_call(key_a, key_b, xbuf, ybuf)
     return merge_call(
-        oa, sa, ob, sb, near_o, near_st, ent_rows, w_out, mlp_gain.reshape(1, WIDTH), wline
+        oa, ob, near_o, near_st, ent_rows, w_out, mlp_gain.reshape(1, WIDTH), lines
     )
 
 

time: 151 us -> 141 us (0.934)
  Pallas kernels: 141 us -> 132 us
  local copies, waits for them, and re-layouts: 9.1 us -> 3.43 us
  starting transfers between devices: 0 us -> 3.38 us
    pallas_call x1, Pallas kernels: 61.6 us -> 54.3 us  [gather_call(): pl.pallas_call(gather_kernel, out_shape=(jax.ShapeDtypeStruct(plane_shape...]
    unnamed x24 -> x7, local copies, waits for them, and re-layouts: 9.1 us -> 2.83 us
    pallas_call x1, Pallas kernels: 16.8 us -> 12.9 us  [far_call(): pl.pallas_call(far_kernel, out_shape=(o_shape, o_shape), in_specs=[smem,...]
    ppermute x0 -> x3, starting transfers between devices: none -> 3.38 us  [along(): return lax.ppermute(piece, 'loc', pairs)]
    pallas_call x1, Pallas kernels: 62.8 us -> 64.7 us  [merge_call(): pl.pallas_call(merge_kernel, out_shape=jax.ShapeDtypeStruct((ROWS, PART),...]
  transfers between devices with their start and end apart: 0 -> 3, of which waited for: 0 -> 1; matrix products, arithmetic and copies ran while one was open for 0% -> 0% of each run, Pallas kernels for 0% -> 9%
where the time goes in v4:
time: 141 us
  Pallas kernels  132 us (94%)
  local copies, waits for them, and re-layouts  3.43 us (2%)
  starting transfers between devices  3.38 us (2%)
    pallas_call x1, Pallas kernels, merge_call(): pl.pallas_call(merge_kernel, out_shape=jax.ShapeDtypeStruct((ROWS, PART),...  64.7 us
    pallas_call x1, Pallas kernels, gather_call(): pl.pallas_call(gather_kernel, out_shape=(jax.ShapeDtypeStruct(plane_shape...  54.3 us
    pallas_call x1, Pallas kernels, far_call(): pl.pallas_call(far_kernel, out_shape=(o_shape, o_shape), in_specs=[smem,...  12.9 us
    ppermute x3, starting transfers between devices, along(): return lax.ppermute(piece, 'loc', pairs)  3.38 us
    unnamed x7, local copies, waits for them, and re-layouts  2.83 us
  transfers between devices with their start and end apart: 3, of which 1 were waited for; matrix products, arithmetic and copies ran while one was open for 0% of the time, Pallas kernels for 9%

profile of v4, /device:TPU:1, one launch (start us, length us, event | category | flops | bytes accessed | tf_op | source)
XLA Modules:
  0.0 140.7 jit_solution(10134379937363579722)
XLA Ops:
  0.0 0.7 add_bitcast_fusion
  0.7 0.6 pad.4.tab
  1.3 54.3 %gather_project.1 = (bf16[2,4,8,3,128,128]{5,4,3,2,1,0:T(8,128)(2,1)}, bf16[2,4,8,3,128,128]{5,4,3,2,1,0:T(8,128)(2,1)}, f32[8,2,128,128]{3,2,1,0:T(8,128)}, f32...) custom-call(bf16[1024,256]{1,0:T(8,128)(2,1)} %ent_hbm.1, ...), custom_call_target="tpu_custom_call" | custom-call | tf_op jit(solution)/shard_map/gather_project/pallas_call | solution.py:364
  55.6 2.1 %collective-permute-start.2 = (bf16[4,64,1024]{2,1,0:T(8,128)(2,1)}, bf16[4,64,1024]{2,1,0:T(8,128)(2,1)S(1)}, u32[]{:S(2)}, u32[]{:S(2)}) collective-permute-start(bf16[4,64,1024]{2,1,0:T(8,128)(2,1)} %get-tuple-element.24.line_0), channel_id=1, source_target_pairs={{0,24},{4,100},{8,0},{12,108},{16,8},{20,116},{24,16},{28,124},{32... | collective-permute-start | bytes 1572872 | tf_op jit(solution)/shard_map/ppermute | solution.py:803
  57.7 0.0 collective-permute-start.1
  57.7 1.3 collective-permute-start
  59.0 12.9 %far_partials.1 = (bf16[32,144,128]{2,1,0:T(8,128)(2,1)}, bf16[32,144,128]{2,1,0:T(8,128)(2,1)}) custom-call(s32[8,32]{1,0:T(8,128)} %get-tuple-element.15.key_a, s32[8,32]{1,0:T(8,128)} %get-tuple-element.16.key_b, bf16[64,3,128,128]{3,2,1,0:T(8,128)(2,1)} %bitcast.12, bf16[64,3,128,128]{3,2,1,0:T(8,128)(2,1)} %bitcast.13), custom_call_target="tpu_custom_call" | custom-call | flops 8000000000 | bytes 31457280 | tf_op jit(solution)/shard_map/far_partials/pallas_call | solution.py:511
  71.9 0.0 collective-permute-done.2.line_3
  71.9 0.0 copy-start
  71.9 1.2 collective-permute-done.1.line_2
  73.1 0.0 copy-start.1
  73.1 0.0 collective-permute-done.line_1
  73.1 0.0 copy-start.2
  73.1 0.0 copy-done
  73.1 0.8 copy-done.1
  73.9 0.2 copy-done.2
  74.1 64.7 %merge_project.1 = bf16[1024,256]{1,0:T(8,128)(2,1)} custom-call(bf16[4,8,144,128]{3,2,1,0:T(8,128)(2,1)} %bitcast.8, bf16[4,8,144,128]{3,2,1,0:T(8,128)(2,1)} %bitcast.9, f32[8,2,128,128]{3,2,1,0:T(8,128)} %get-tuple-element.21.near_o_hbm, f32[8,2,8,128]{3,2,1,0:T(8,128)} %get-tuple-element.22.near_st_hbm, ...), custom_call_target="tpu_custom_call" | custom-call | tf_op jit(solution)/shard_map/merge_project/pallas_call | solution.py:747
  138.8 1.9 %copy.12 = bf16[1024,256]{1,0:T(8,128)(2,1)} copy(bf16[1024,256]{1,0:T(8,128)(2,1)} %merge_project.1) | data formatting | bytes 1048576
Async XLA Ops:
  55.6 16.3 %collective-permute-start.2 = (bf16[4,64,1024]{2,1,0:T(8,128)(2,1)}, bf16[4,64,1024]{2,1,0:T(8,128)(2,1)S(1)}, u32[]{:S(2)}, u32[]{:S(2)}) collective-permute-start(bf16[4,64,1024]{2,1,0:T(8,128)(2,1)} %get-tuple-element.24.line_0), channel_id=1, source_target_pairs={{0,24},{4,100},{8,0},{12,108},{16,8},{20,116},{24,16},{28,124},{32... | collective-permute-start | bytes 1572872 | tf_op jit(solution)/shard_map/ppermute | solution.py:803
  57.7 15.4 %collective-permute-start.1 = (bf16[4,64,1024]{2,1,0:T(8,128)(2,1)}, bf16[4,64,1024]{2,1,0:T(8,128)(2,1)S(1)}, u32[]{:S(2)}, u32[]{:S(2)}) collective-permute-start(bf16[4,64,1024]{2,1,0:T(8,128)(2,1)} %get-tuple-element.24.line_0), channel_id=1, source_target_pairs={{0,8},{4,36},{8,16},{12,44},{16,24},{20,52},{24,0},{28,60},{32,40}... | collective-permute-start | bytes 1572872 | tf_op jit(solution)/shard_map/ppermute | solution.py:803
  57.7 15.4 %collective-permute-start = (bf16[4,64,1024]{2,1,0:T(8,128)(2,1)}, bf16[4,64,1024]{2,1,0:T(8,128)(2,1)S(1)}, u32[]{:S(2)}, u32[]{:S(2)}) collective-permute-start(bf16[4,64,1024]{2,1,0:T(8,128)(2,1)} %get-tuple-element.24.line_0), channel_id=1, source_target_pairs={{0,16},{4,68},{8,24},{12,76},{16,0},{20,84},{24,8},{28,92},{32,48}... | collective-permute-start | bytes 1572872 | tf_op jit(solution)/shard_map/ppermute | solution.py:803
  71.9 1.2 copy-start
  73.1 0.8 copy-start.1
  73.1 1.0 copy-start.2

commit v5 on v4

--- a/solution.py
+++ b/solution.py
@@ -435,7 +435,7 @@
 
     counts = lax.fori_loop(0, SIDE, find, (0, 0))
     for hits, count in zip((hits_a, hits_b), counts):
-        for extra in range(4):
+        for extra in range(8):
             hits[count + extra] = live_q * 1024
 
     def clear(i, carry):
@@ -453,10 +453,10 @@
         for load in loads[pair]:
             load.wait()
 
-        def four(step, carry):
+        def eight(step, carry):
             work = []
-            for u in range(4):
-                code = hits[step * 4 + u]
+            for u in range(8):
+                code = hits[step * 8 + u]
                 q, k = lax.shift_right_logical(code, 10), code & 1023
                 asked = split_heads(query[pair, jnp.minimum(q, live_q - 1)])
                 key = pairs[pair, k, 0]
@@ -480,7 +480,7 @@
                     state[q, 2 + h : 3 + h] = state[q, 2 + h : 3 + h] * keep + total[:, cut] * add
             return carry
 
-        lax.fori_loop(0, lax.shift_right_logical(count + 3, 2), four, 0)
+        lax.fori_loop(0, lax.shift_right_logical(count + 7, 3), eight, 0)
 
         def finish(i, carry):
             st = state[base + i]
@@ -747,7 +747,7 @@
     return pl.pallas_call(
         merge_kernel,
         out_shape=jax.ShapeDtypeStruct((ROWS, PART), BF16),
-        in_specs=[hbm] * 6 + [vmem] + [hbm] * 4,
+        in_specs=[hbm] * 6 + [vmem] + [pl.BlockSpec(memory_space=pl.ANY)] * 4,
         out_specs=vmem,
         scratch_shapes=[
             pltpu.VMEM((SIDE, NB, TALL, BLK), BF16),
@@ -777,7 +777,7 @@
             dma((8,)),
         ],
         compiler_params=pltpu.CompilerParams(
-            collective_id=1, has_side_effects=True, vmem_limit_bytes=60 * MB
+            collective_id=1, has_side_effects=True, vmem_limit_bytes=50 * MB
         ),
         name="merge_project",
     )(oa, ob, near_o, near_st, ent_rows, w_out, gain, *lines)

time: 141 us -> 137 us (0.972)
  Pallas kernels: 132 us -> 128 us
  waiting for transfers between devices: 1.2 us -> 3.43 us
  local copies, waits for them, and re-layouts: 3.43 us -> 1.42 us
    pallas_call x1, Pallas kernels: 12.9 us -> 10.6 us  [far_call(): pl.pallas_call(far_kernel, out_shape=(o_shape, o_shape), in_specs=[smem,...]
    ppermute x3, waiting for transfers between devices: 1.2 us -> 3.43 us  [along(): return lax.ppermute(piece, 'loc', pairs)]
    unnamed x7 -> x11, local copies, waits for them, and re-layouts: 2.83 us -> 0.82 us
    pallas_call x1, Pallas kernels: 64.7 us -> 63.2 us  [merge_call(): pl.pallas_call(merge_kernel, out_shape=jax.ShapeDtypeStruct((ROWS, PART),...]
  transfers between devices with their start and end apart: 3 -> 3, of which waited for: 1 -> 2; matrix products, arithmetic and copies ran while one was open for 0% -> 0% of each run, Pallas kernels for 9% -> 8%
where the time goes in v5:
time: 137 us
  Pallas kernels  128 us (93%)
  waiting for transfers between devices  3.43 us (3%)
  starting transfers between devices  3.38 us (2%)
  local copies, waits for them, and re-layouts  1.42 us (1%)
    pallas_call x1, Pallas kernels, merge_call(): pl.pallas_call(merge_kernel, out_shape=jax.ShapeDtypeStruct((ROWS, PART),...  63.2 us
    pallas_call x1, Pallas kernels, gather_call(): pl.pallas_call(gather_kernel, out_shape=(jax.ShapeDtypeStruct(plane_shape...  54.3 us
    pallas_call x1, Pallas kernels, far_call(): pl.pallas_call(far_kernel, out_shape=(o_shape, o_shape), in_specs=[smem,...  10.6 us
    ppermute x3, waiting for transfers between devices, along(): return lax.ppermute(piece, 'loc', pairs)  3.43 us
    ppermute x3, starting transfers between devices, along(): return lax.ppermute(piece, 'loc', pairs)  3.38 us
  transfers between devices with their start and end apart: 3, of which 2 were waited for; matrix products, arithmetic and copies ran while one was open for 0% of the time, Pallas kernels for 8%

profile of v5, /device:TPU:1, one launch (start us, length us, event | category | flops | bytes accessed | tf_op | source)
XLA Modules:
  0.0 137.1 jit_solution(10846099342820674423)
XLA Ops:
  0.0 0.7 add_bitcast_fusion
  0.7 0.6 pad.4.tab
  1.3 54.3 %gather_project.1 = (bf16[2,4,8,3,128,128]{5,4,3,2,1,0:T(8,128)(2,1)}, bf16[2,4,8,3,128,128]{5,4,3,2,1,0:T(8,128)(2,1)}, f32[8,2,128,128]{3,2,1,0:T(8,128)}, f32...) custom-call(bf16[1024,256]{1,0:T(8,128)(2,1)} %ent_hbm.1, ...), custom_call_target="tpu_custom_call" | custom-call | tf_op jit(solution)/shard_map/gather_project/pallas_call | solution.py:364
  55.6 2.1 %collective-permute-start.2 = (bf16[4,64,1024]{2,1,0:T(8,128)(2,1)}, bf16[4,64,1024]{2,1,0:T(8,128)(2,1)S(1)}, u32[]{:S(2)}, u32[]{:S(2)}) collective-permute-start(bf16[4,64,1024]{2,1,0:T(8,128)(2,1)} %get-tuple-element.24.line_0), channel_id=1, source_target_pairs={{0,24},{4,100},{8,0},{12,108},{16,8},{20,116},{24,16},{28,124},{32... | collective-permute-start | bytes 1572872 | tf_op jit(solution)/shard_map/ppermute | solution.py:803
  57.7 0.0 collective-permute-start.1
  57.7 1.3 collective-permute-start
  59.0 0.0 copy-start
  59.0 0.0 copy-start.1
  59.0 0.0 copy-start.2
  59.0 0.0 copy-start.3
  59.0 0.0 copy-start.4
  59.0 10.6 %far_partials.1 = (bf16[32,144,128]{2,1,0:T(8,128)(2,1)}, bf16[32,144,128]{2,1,0:T(8,128)(2,1)}) custom-call(s32[8,32]{1,0:T(8,128)} %get-tuple-element.15.key_a, s32[8,32]{1,0:T(8,128)} %get-tuple-element.16.key_b, bf16[64,3,128,128]{3,2,1,0:T(8,128)(2,1)} %bitcast.12, bf16[64,3,128,128]{3,2,1,0:T(8,128)(2,1)} %bitcast.13), custom_call_target="tpu_custom_call" | custom-call | flops 8000000000 | bytes 31457280 | tf_op jit(solution)/shard_map/far_partials/pallas_call | solution.py:511
  69.7 0.1 collective-permute-done.2.line_3
  69.8 3.3 %collective-permute-done.1.line_2 = bf16[4,64,1024]{2,1,0:T(8,128)(2,1)S(1)} collective-permute-done((bf16[4,64,1024]{2,1,0:T(8,128)(2,1)}, bf16[4,64,1024]{2,1,0:T(8,128)(2,1)S(1)}, u32[]{:S(2)}, u32[]{:S(2)}) %collective-permute-start.1) | collective-permute-done | bytes 524320 | tf_op jit(solution)/shard_map/ppermute | solution.py:803
  73.1 0.0 collective-permute-done.line_1
  73.1 0.0 copy-done
  73.1 0.0 copy-done.1
  73.1 0.0 copy-done.2
  73.1 0.0 copy-done.3
  73.1 0.0 copy-done.4
  73.1 63.2 %merge_project.1 = bf16[1024,256]{1,0:T(8,128)(2,1)S(1)} custom-call(bf16[4,8,144,128]{3,2,1,0:T(8,128)(2,1)} %bitcast.9, bf16[4,8,144,128]{3,2,1,0:T(8,128)(2,1)} %bitcast.10, f32[8,2,128,128]{3,2,1,0:T(8,128)} %get-tuple-element.21.near_o_hbm, f32[8,2,8,128]{3,2,1,0:T(8,128)S(1)} %copy-done.3, bf16[256,1024]{1,0:T(8,128)(2,1)S(1)} %copy-done.1, ...), custom_call_target="tpu_custom_call" | custom-call | tf_op jit(solution)/shard_map/merge_project/pallas_call | solution.py:747
  136.3 0.8 copy.12
Async XLA Ops:
  55.6 14.2 %collective-permute-start.2 = (bf16[4,64,1024]{2,1,0:T(8,128)(2,1)}, bf16[4,64,1024]{2,1,0:T(8,128)(2,1)S(1)}, u32[]{:S(2)}, u32[]{:S(2)}) collective-permute-start(bf16[4,64,1024]{2,1,0:T(8,128)(2,1)} %get-tuple-element.24.line_0), channel_id=1, source_target_pairs={{0,24},{4,100},{8,0},{12,108},{16,8},{20,116},{24,16},{28,124},{32... | collective-permute-start | bytes 1572872 | tf_op jit(solution)/shard_map/ppermute | solution.py:803
  57.7 15.4 %collective-permute-start.1 = (bf16[4,64,1024]{2,1,0:T(8,128)(2,1)}, bf16[4,64,1024]{2,1,0:T(8,128)(2,1)S(1)}, u32[]{:S(2)}, u32[]{:S(2)}) collective-permute-start(bf16[4,64,1024]{2,1,0:T(8,128)(2,1)} %get-tuple-element.24.line_0), channel_id=1, source_target_pairs={{0,8},{4,36},{8,16},{12,44},{16,24},{20,52},{24,0},{28,60},{32,40}... | collective-permute-start | bytes 1572872 | tf_op jit(solution)/shard_map/ppermute | solution.py:803
  57.7 15.4 %collective-permute-start = (bf16[4,64,1024]{2,1,0:T(8,128)(2,1)}, bf16[4,64,1024]{2,1,0:T(8,128)(2,1)S(1)}, u32[]{:S(2)}, u32[]{:S(2)}) collective-permute-start(bf16[4,64,1024]{2,1,0:T(8,128)(2,1)} %get-tuple-element.24.line_0), channel_id=1, source_target_pairs={{0,16},{4,68},{8,24},{12,76},{16,0},{20,84},{24,8},{28,92},{32,48}... | collective-permute-start | bytes 1572872 | tf_op jit(solution)/shard_map/ppermute | solution.py:803
  59.0 14.1 %copy-start = (bf16[256,1024]{1,0:T(8,128)(2,1)S(1)}, bf16[256,1024]{1,0:T(8,128)(2,1)}, u32[]{:S(2)}) copy-start(bf16[256,1024]{1,0:T(8,128)(2,1)} %w_out_hbm.1) | copy-start | bytes 1572868
  59.0 14.1 %copy-start.1 = (bf16[256,1024]{1,0:T(8,128)(2,1)S(1)}, bf16[256,1024]{1,0:T(8,128)(2,1)}, u32[]{:S(2)}) copy-start(bf16[256,1024]{1,0:T(8,128)(2,1)} %get-tuple-element.23.ent_rows_hbm) | copy-start | bytes 1572868
  59.0 14.1 %copy-start.2 = (bf16[4,64,1024]{2,1,0:T(8,128)(2,1)S(1)}, bf16[4,64,1024]{2,1,0:T(8,128)(2,1)}, u32[]{:S(2)}) copy-start(bf16[4,64,1024]{2,1,0:T(8,128)(2,1)} %get-tuple-element.24.line_0) | copy-start | bytes 1572868
  59.0 14.1 %copy-start.3 = (f32[8,2,8,128]{3,2,1,0:T(8,128)S(1)}, f32[8,2,8,128]{3,2,1,0:T(8,128)}, u32[]{:S(2)}) copy-start(f32[8,2,8,128]{3,2,1,0:T(8,128)} %get-tuple-element.22.near_st_hbm) | copy-start | bytes 196612
  59.0 14.1 %copy-start.4 = (f32[1024]{0:T(1024)S(1)}, f32[1024]{0:T(1024)}, u32[]{:S(2)}) copy-start(f32[1024]{0:T(1024)} %param.14) | copy-start | bytes 12292

commit v6 on v5

--- a/solution.py
+++ b/solution.py
@@ -802,7 +802,7 @@
             pairs.append((i, (y * 4 + x) * 2 + core))
         return lax.ppermute(piece, "loc", pairs)
 
-    lines = [piece] + [along(by) for by in (2, 1, 3)]
+    lines = [piece] + [along(by) for by in (3, 1, 2)]
     oa, ob = far_call(key_a, key_b, xbuf, ybuf)
     return merge_call(
         oa, ob, near_o, near_st, ent_rows, w_out, mlp_gain.reshape(1, WIDTH), lines

time: 137 us -> 136 us (level)
  waiting for transfers between devices: 3.43 us -> 1.29 us
    ppermute x3, waiting for transfers between devices: 3.43 us -> 1.29 us  [along(): return lax.ppermute(piece, 'loc', pairs)]
  transfers between devices with their start and end apart: 3 -> 3, of which waited for: 2 -> 1; matrix products, arithmetic and copies ran while one was open for 0% -> 0% of each run, Pallas kernels for 8% -> 8%
where the time goes in v6:
time: 136 us
  Pallas kernels  129 us (95%)
  starting transfers between devices  3.77 us (3%)
  local copies, waits for them, and re-layouts  1.42 us (1%)
    pallas_call x1, Pallas kernels, merge_call(): pl.pallas_call(merge_kernel, out_shape=jax.ShapeDtypeStruct((ROWS, PART),...  63.7 us
    pallas_call x1, Pallas kernels, gather_call(): pl.pallas_call(gather_kernel, out_shape=(jax.ShapeDtypeStruct(plane_shape...  54.3 us
    pallas_call x1, Pallas kernels, far_call(): pl.pallas_call(far_kernel, out_shape=(o_shape, o_shape), in_specs=[smem,...  10.6 us
    ppermute x3, starting transfers between devices, along(): return lax.ppermute(piece, 'loc', pairs)  3.77 us
  transfers between devices with their start and end apart: 3, of which 1 were waited for; matrix products, arithmetic and copies ran while one was open for 0% of the time, Pallas kernels for 8%

profile of v6, /device:TPU:1, one launch (start us, length us, event | category | flops | bytes accessed | tf_op | source)
XLA Modules:
  0.0 135.9 jit_solution(11510473758232143200)
XLA Ops:
  0.0 0.7 add_bitcast_fusion
  0.7 0.6 pad.4.tab
  1.3 54.3 %gather_project.1 = (bf16[2,4,8,3,128,128]{5,4,3,2,1,0:T(8,128)(2,1)}, bf16[2,4,8,3,128,128]{5,4,3,2,1,0:T(8,128)(2,1)}, f32[8,2,128,128]{3,2,1,0:T(8,128)}, f32...) custom-call(bf16[1024,256]{1,0:T(8,128)(2,1)} %ent_hbm.1, ...), custom_call_target="tpu_custom_call" | custom-call | tf_op jit(solution)/shard_map/gather_project/pallas_call | solution.py:364
  55.6 1.1 collective-permute-start.2
  56.7 1.6 %collective-permute-start.1 = (bf16[4,64,1024]{2,1,0:T(8,128)(2,1)}, bf16[4,64,1024]{2,1,0:T(8,128)(2,1)S(1)}, u32[]{:S(2)}, u32[]{:S(2)}) collective-permute-start(bf16[4,64,1024]{2,1,0:T(8,128)(2,1)} %get-tuple-element.24.line_0), channel_id=1, source_target_pairs={{0,8},{4,36},{8,16},{12,44},{16,24},{20,52},{24,0},{28,60},{32,40}... | collective-permute-start | bytes 1572872 | tf_op jit(solution)/shard_map/ppermute | solution.py:803
  58.3 1.1 collective-permute-start
  59.4 0.0 copy-start
  59.4 0.0 copy-start.1
  59.4 0.0 copy-start.2
  59.4 0.0 copy-start.3
  59.4 0.0 copy-start.4
  59.4 10.6 %far_partials.1 = (bf16[32,144,128]{2,1,0:T(8,128)(2,1)}, bf16[32,144,128]{2,1,0:T(8,128)(2,1)}) custom-call(s32[8,32]{1,0:T(8,128)} %get-tuple-element.15.key_a, s32[8,32]{1,0:T(8,128)} %get-tuple-element.16.key_b, bf16[64,3,128,128]{3,2,1,0:T(8,128)(2,1)} %bitcast.12, bf16[64,3,128,128]{3,2,1,0:T(8,128)(2,1)} %bitcast.13), custom_call_target="tpu_custom_call" | custom-call | flops 8000000000 | bytes 31457280 | tf_op jit(solution)/shard_map/far_partials/pallas_call | solution.py:511
  70.1 0.0 collective-permute-done.2.line_3
  70.1 1.3 collective-permute-done.1.line_2
  71.4 0.0 collective-permute-done.line_1
  71.4 0.0 copy-done
  71.4 0.0 copy-done.1
  71.4 0.0 copy-done.2
  71.4 0.0 copy-done.3
  71.4 0.0 copy-done.4
  71.4 63.7 %merge_project.1 = bf16[1024,256]{1,0:T(8,128)(2,1)S(1)} custom-call(bf16[4,8,144,128]{3,2,1,0:T(8,128)(2,1)} %bitcast.9, bf16[4,8,144,128]{3,2,1,0:T(8,128)(2,1)} %bitcast.10, f32[8,2,128,128]{3,2,1,0:T(8,128)} %get-tuple-element.21.near_o_hbm, f32[8,2,8,128]{3,2,1,0:T(8,128)S(1)} %copy-done.3, bf16[256,1024]{1,0:T(8,128)(2,1)S(1)} %copy-done.1, ...), custom_call_target="tpu_custom_call" | custom-call | tf_op jit(solution)/shard_map/merge_project/pallas_call | solution.py:747
  135.1 0.8 copy.12
Async XLA Ops:
  55.6 14.4 %collective-permute-start.2 = (bf16[4,64,1024]{2,1,0:T(8,128)(2,1)}, bf16[4,64,1024]{2,1,0:T(8,128)(2,1)S(1)}, u32[]{:S(2)}, u32[]{:S(2)}) collective-permute-start(bf16[4,64,1024]{2,1,0:T(8,128)(2,1)} %get-tuple-element.24.line_0), channel_id=1, source_target_pairs={{0,16},{4,68},{8,24},{12,76},{16,0},{20,84},{24,8},{28,92},{32,48}... | collective-permute-start | bytes 1572872 | tf_op jit(solution)/shard_map/ppermute | solution.py:803
  56.7 14.6 %collective-permute-start.1 = (bf16[4,64,1024]{2,1,0:T(8,128)(2,1)}, bf16[4,64,1024]{2,1,0:T(8,128)(2,1)S(1)}, u32[]{:S(2)}, u32[]{:S(2)}) collective-permute-start(bf16[4,64,1024]{2,1,0:T(8,128)(2,1)} %get-tuple-element.24.line_0), channel_id=1, source_target_pairs={{0,8},{4,36},{8,16},{12,44},{16,24},{20,52},{24,0},{28,60},{32,40}... | collective-permute-start | bytes 1572872 | tf_op jit(solution)/shard_map/ppermute | solution.py:803
  58.3 13.0 %collective-permute-start = (bf16[4,64,1024]{2,1,0:T(8,128)(2,1)}, bf16[4,64,1024]{2,1,0:T(8,128)(2,1)S(1)}, u32[]{:S(2)}, u32[]{:S(2)}) collective-permute-start(bf16[4,64,1024]{2,1,0:T(8,128)(2,1)} %get-tuple-element.24.line_0), channel_id=1, source_target_pairs={{0,24},{4,100},{8,0},{12,108},{16,8},{20,116},{24,16},{28,124},{32... | collective-permute-start | bytes 1572872 | tf_op jit(solution)/shard_map/ppermute | solution.py:803
  59.4 12.0 %copy-start = (bf16[256,1024]{1,0:T(8,128)(2,1)S(1)}, bf16[256,1024]{1,0:T(8,128)(2,1)}, u32[]{:S(2)}) copy-start(bf16[256,1024]{1,0:T(8,128)(2,1)} %w_out_hbm.1) | copy-start | bytes 1572868
  59.4 12.0 %copy-start.1 = (bf16[256,1024]{1,0:T(8,128)(2,1)S(1)}, bf16[256,1024]{1,0:T(8,128)(2,1)}, u32[]{:S(2)}) copy-start(bf16[256,1024]{1,0:T(8,128)(2,1)} %get-tuple-element.23.ent_rows_hbm) | copy-start | bytes 1572868
  59.4 12.0 %copy-start.2 = (bf16[4,64,1024]{2,1,0:T(8,128)(2,1)S(1)}, bf16[4,64,1024]{2,1,0:T(8,128)(2,1)}, u32[]{:S(2)}) copy-start(bf16[4,64,1024]{2,1,0:T(8,128)(2,1)} %get-tuple-element.24.line_0) | copy-start | bytes 1572868
  59.4 12.0 %copy-start.3 = (f32[8,2,8,128]{3,2,1,0:T(8,128)S(1)}, f32[8,2,8,128]{3,2,1,0:T(8,128)}, u32[]{:S(2)}) copy-start(f32[8,2,8,128]{3,2,1,0:T(8,128)} %get-tuple-element.22.near_st_hbm) | copy-start | bytes 196612
  59.4 12.0 %copy-start.4 = (f32[1024]{0:T(1024)S(1)}, f32[1024]{0:T(1024)}, u32[]{:S(2)}) copy-start(f32[1024]{0:T(1024)} %param.14) | copy-start | bytes 12292

commit v7 on v6

--- a/solution.py
+++ b/solution.py
@@ -534,7 +534,7 @@
 
 
 def merge_kernel(
-    oa, ob, near_o_hbm, near_st_hbm, ent_rows_hbm, w_out_hbm, gain, line_0, line_1, line_2, line_3, result,
+    oa, ob, near_o_hbm, near_st_hbm, ent_rows_hbm, w_out_hbm, gain, line_0, line_1, line_2, line_3, side_dn, side_up, result,
     ra, rb, relay, att, part, got_half, got,
     weights, inner, acc, send_sib, got_sib, res, landed, near_o, near_st, ent_rows, w_out,
     os, orr, fs, fr, zs, zr, ws, wr, wl, ss, sr, es, er, ls,
@@ -567,7 +567,11 @@
     w_local = [
         pltpu.make_async_copy(line[n], weights.at[w_place, n], wl.at[n]) for n in range(SIDE)
     ]
-    for copy in w_local:
+    w_sides = [
+        pltpu.make_async_copy(side_dn, weights.at[(w_place + 3) % 4, 0], wl.at[SIDE]),
+        pltpu.make_async_copy(side_up, weights.at[(w_place + 1) % 4, 0], wl.at[SIDE + 1]),
+    ]
+    for copy in w_local + w_sides:
         copy.start()
     greeted(peers)
     pending = []
@@ -612,9 +616,8 @@
     w_up_copies, w_dn_copies = [None] * 4, [None] * 4
 
     def weights_start():
-        for n in range(SIDE):
-            u, d = n, (n + 2) % 4
-            dst = weights.at[w_place]
+        dst = weights.at[w_place]
+        for u, d in ((1, 2), (2, 3), (3, 1)):
             w_up_copies[u] = go(remote(line[u], dst.at[u], ws.at[0, u], wr.at[0, u], w_up_to))
             w_dn_copies[d] = go(remote(line[d], dst.at[d], ws.at[1, d], wr.at[1, d], w_dn_to))
 
@@ -624,7 +627,11 @@
     w_far = []
 
     def weights_forward(n):
-        w_up_copies[n].wait_recv()
+        if n == 0:
+            for copy in w_sides:
+                copy.wait()
+        else:
+            w_up_copies[n].wait_recv()
         view = weights.at[(w_place + 3) % 4, n]
         w_far.append(go(remote(view, view, ws.at[2, n], wr.at[2, n], w_up_to)))
         w_dn_copies[n + 2].wait_recv()
@@ -710,7 +717,6 @@
     w_up_copies[2].wait_recv()
     w_up_copies[3].wait_recv()
     mlp_both((w_place + 3) % 4)
-    w_dn_copies[0].wait_recv()
     w_dn_copies[1].wait_recv()
     mlp_both((w_place + 1) % 4)
     for copy in w_far:
@@ -747,7 +753,7 @@
     return pl.pallas_call(
         merge_kernel,
         out_shape=jax.ShapeDtypeStruct((ROWS, PART), BF16),
-        in_specs=[hbm] * 6 + [vmem] + [pl.BlockSpec(memory_space=pl.ANY)] * 4,
+        in_specs=[hbm] * 6 + [vmem] + [pl.BlockSpec(memory_space=pl.ANY)] * 6,
         out_specs=vmem,
         scratch_shapes=[
             pltpu.VMEM((SIDE, NB, TALL, BLK), BF16),
@@ -771,7 +777,7 @@
             dma((2, 4, 4)), dma((2, 4, 4)),
             dma((2, 4, 2)), dma((2, 4, 2)),
             dma((4,)), dma((4,)),
-            dma((3, 4)), dma((3, 4)), dma((4,)),
+            dma((3, 4)), dma((3, 4)), dma((6,)),
             dma((2,)), dma((2,)),
             dma((4,)), dma((4,)),
             dma((8,)),
@@ -794,15 +800,15 @@
         w_up,
         w_down,
     )
-    def along(by):
+    def along(by, turn=0):
         pairs = []
         for i in range(lax.axis_size("loc")):
             y, x, core = i // 8, i // 2 % 4, i % 2
-            y, x = (y, (x + by) % 4) if core == 0 else ((y + by) % 4, x)
+            y, x = (y, (x + by) % 4) if core == turn else ((y + by) % 4, x)
             pairs.append((i, (y * 4 + x) * 2 + core))
         return lax.ppermute(piece, "loc", pairs)
 
-    lines = [piece] + [along(by) for by in (3, 1, 2)]
+    lines = [piece] + [along(by) for by in (3, 1, 2)] + [along(by, 1) for by in (1, 3)]
     oa, ob = far_call(key_a, key_b, xbuf, ybuf)
     return merge_call(
         oa, ob, near_o, near_st, ent_rows, w_out, mlp_gain.reshape(1, WIDTH), lines

time: 136 us -> 138 us (1.015)
  Pallas kernels: 129 us -> 122 us
  waiting for transfers between devices: 1.29 us -> 6.8 us
  starting transfers between devices: 3.77 us -> 5.96 us
    pallas_call x1, Pallas kernels: 63.7 us -> 57.5 us  [merge_call(): pl.pallas_call(merge_kernel, out_shape=jax.ShapeDtypeStruct((ROWS, PART),...]
    ppermute x3 -> x5, waiting for transfers between devices: 1.29 us -> 6.8 us  [along(): return lax.ppermute(piece, 'loc', pairs)]
    ppermute x3 -> x5, starting transfers between devices: 3.77 us -> 5.96 us  [along(): return lax.ppermute(piece, 'loc', pairs)]
  transfers between devices with their start and end apart: 3 -> 5, of which waited for: 1 -> 2; matrix products, arithmetic and copies ran while one was open for 0% -> 0% of each run, Pallas kernels for 8% -> 8%
where the time goes in v7:
time: 138 us; the launch traced here: 137 us
  Pallas kernels  122 us (88%)
  waiting for transfers between devices  6.8 us (5%)
  starting transfers between devices  5.96 us (4%)
  local copies, waits for them, and re-layouts  1.42 us (1%)
    pallas_call x1, Pallas kernels, merge_call(): pl.pallas_call(merge_kernel, out_shape=jax.ShapeDtypeStruct((ROWS, PART),...  57.5 us
    pallas_call x1, Pallas kernels, gather_call(): pl.pallas_call(gather_kernel, out_shape=(jax.ShapeDtypeStruct(plane_shape...  54.3 us
    pallas_call x1, Pallas kernels, far_call(): pl.pallas_call(far_kernel, out_shape=(o_shape, o_shape), in_specs=[smem,...  10.6 us
    ppermute x5, waiting for transfers between devices, along(): return lax.ppermute(piece, 'loc', pairs)  6.8 us
    ppermute x5, starting transfers between devices, along(): return lax.ppermute(piece, 'loc', pairs)  5.96 us
  transfers between devices with their start and end apart: 5, of which 2 were waited for; matrix products, arithmetic and copies ran while one was open for 0% of the time, Pallas kernels for 8%

profile of v7, /device:TPU:1, one launch (start us, length us, event | category | flops | bytes accessed | tf_op | source)
XLA Modules:
  0.0 137.5 jit_solution(3426497780445180828)
XLA Ops:
  0.0 0.7 add_bitcast_fusion
  0.7 0.6 pad.4.tab
  1.3 54.3 %gather_project.1 = (bf16[2,4,8,3,128,128]{5,4,3,2,1,0:T(8,128)(2,1)}, bf16[2,4,8,3,128,128]{5,4,3,2,1,0:T(8,128)(2,1)}, f32[8,2,128,128]{3,2,1,0:T(8,128)}, f32...) custom-call(bf16[1024,256]{1,0:T(8,128)(2,1)} %ent_hbm.1, ...), custom_call_target="tpu_custom_call" | custom-call | tf_op jit(solution)/shard_map/gather_project/pallas_call | solution.py:364
  55.6 2.2 %collective-permute-start.4 = (bf16[4,64,1024]{2,1,0:T(8,128)(2,1)}, bf16[4,64,1024]{2,1,0:T(8,128)(2,1)S(1)}, u32[]{:S(2)}, u32[]{:S(2)}) collective-permute-start(bf16[4,64,1024]{2,1,0:T(8,128)(2,1)} %get-tuple-element.24.line_0), channel_id=1, source_target_pairs={{0,96},{4,28},{8,104},{12,4},{16,112},{20,12},{24,120},{28,20},{32... | collective-permute-start | bytes 1572872 | tf_op jit(solution)/shard_map/ppermute | solution.py:809
  57.8 0.0 collective-permute-start.3
  57.8 1.1 collective-permute-start.2
  58.9 0.9 collective-permute-start.1
  59.8 1.8 %collective-permute-start = (bf16[4,64,1024]{2,1,0:T(8,128)(2,1)}, bf16[4,64,1024]{2,1,0:T(8,128)(2,1)S(1)}, u32[]{:S(2)}, u32[]{:S(2)}) collective-permute-start(bf16[4,64,1024]{2,1,0:T(8,128)(2,1)} %get-tuple-element.24.line_0), channel_id=1, source_target_pairs={{0,24},{4,100},{8,0},{12,108},{16,8},{20,116},{24,16},{28,124},{32... | collective-permute-start | bytes 1572872 | tf_op jit(solution)/shard_map/ppermute | solution.py:809
  61.6 0.0 copy-start
  61.6 0.0 copy-start.1
  61.6 0.0 copy-start.2
  61.6 0.0 copy-start.3
  61.6 0.0 copy-start.4
  61.6 10.6 %far_partials.1 = (bf16[32,144,128]{2,1,0:T(8,128)(2,1)}, bf16[32,144,128]{2,1,0:T(8,128)(2,1)}) custom-call(s32[8,32]{1,0:T(8,128)} %get-tuple-element.15.key_a, s32[8,32]{1,0:T(8,128)} %get-tuple-element.16.key_b, bf16[64,3,128,128]{3,2,1,0:T(8,128)(2,1)} %bitcast.12, bf16[64,3,128,128]{3,2,1,0:T(8,128)(2,1)} %bitcast.13), custom_call_target="tpu_custom_call" | custom-call | flops 8000000000 | bytes 31457280 | tf_op jit(solution)/shard_map/far_partials/pallas_call | solution.py:511
  72.3 0.0 collective-permute-done.4.side_up
  72.3 0.0 copy-start.5
  72.3 4.8 %collective-permute-done.3.side_dn = bf16[4,64,1024]{2,1,0:T(8,128)(2,1)S(1)} collective-permute-done((bf16[4,64,1024]{2,1,0:T(8,128)(2,1)}, bf16[4,64,1024]{2,1,0:T(8,128)(2,1)S(1)}, u32[]{:S(2)}, u32[]{:S(2)}) %collective-permute-start.3) | collective-permute-done | bytes 524320 | tf_op jit(solution)/shard_map/ppermute | solution.py:809
  77.1 0.0 copy-start.6
  77.1 0.0 collective-permute-done.2.line_3
  77.1 2.0 %collective-permute-done.1.line_2 = bf16[4,64,1024]{2,1,0:T(8,128)(2,1)S(1)} collective-permute-done((bf16[4,64,1024]{2,1,0:T(8,128)(2,1)}, bf16[4,64,1024]{2,1,0:T(8,128)(2,1)S(1)}, u32[]{:S(2)}, u32[]{:S(2)}) %collective-permute-start.1) | collective-permute-done | bytes 524320 | tf_op jit(solution)/shard_map/ppermute | solution.py:809
  79.1 0.0 collective-permute-done.line_1
  79.1 0.0 copy-done.5
  79.1 0.0 copy-done.6
  79.1 0.0 copy-done
  79.1 0.0 copy-done.1
  79.1 0.0 copy-done.2
  79.1 0.0 copy-done.3
  79.1 0.0 copy-done.4
  79.2 57.5 %merge_project.1 = bf16[1024,256]{1,0:T(8,128)(2,1)S(1)} custom-call(bf16[4,8,144,128]{3,2,1,0:T(8,128)(2,1)} %bitcast.9, bf16[4,8,144,128]{3,2,1,0:T(8,128)(2,1)} %bitcast.10, f32[8,2,128,128]{3,2,1,0:T(8,128)} %get-tuple-element.21.near_o_hbm, f32[8,2,8,128]{3,2,1,0:T(8,128)S(1)} %copy-done.3, bf16[256,1024]{1,0:T(8,128)(2,1)S(1)} %copy-done.1, ...), custom_call_target="tpu_custom_call" | custom-call | tf_op jit(solution)/shard_map/merge_project/pallas_call | solution.py:753
  136.7 0.8 copy.12
Async XLA Ops:
  55.6 16.6 %collective-permute-start.4 = (bf16[4,64,1024]{2,1,0:T(8,128)(2,1)}, bf16[4,64,1024]{2,1,0:T(8,128)(2,1)S(1)}, u32[]{:S(2)}, u32[]{:S(2)}) collective-permute-start(bf16[4,64,1024]{2,1,0:T(8,128)(2,1)} %get-tuple-element.24.line_0), channel_id=1, source_target_pairs={{0,96},{4,28},{8,104},{12,4},{16,112},{20,12},{24,120},{28,20},{32... | collective-permute-start | bytes 1572872 | tf_op jit(solution)/shard_map/ppermute | solution.py:809
  57.8 19.3 %collective-permute-start.3 = (bf16[4,64,1024]{2,1,0:T(8,128)(2,1)}, bf16[4,64,1024]{2,1,0:T(8,128)(2,1)S(1)}, u32[]{:S(2)}, u32[]{:S(2)}) collective-permute-start(bf16[4,64,1024]{2,1,0:T(8,128)(2,1)} %get-tuple-element.24.line_0), channel_id=1, source_target_pairs={{0,32},{4,12},{8,40},{12,20},{16,48},{20,28},{24,56},{28,4},{32,64... | collective-permute-start | bytes 1572872 | tf_op jit(solution)/shard_map/ppermute | solution.py:809
  57.8 19.3 %collective-permute-start.2 = (bf16[4,64,1024]{2,1,0:T(8,128)(2,1)}, bf16[4,64,1024]{2,1,0:T(8,128)(2,1)S(1)}, u32[]{:S(2)}, u32[]{:S(2)}) collective-permute-start(bf16[4,64,1024]{2,1,0:T(8,128)(2,1)} %get-tuple-element.24.line_0), channel_id=1, source_target_pairs={{0,16},{4,68},{8,24},{12,76},{16,0},{20,84},{24,8},{28,92},{32,48}... | collective-permute-start | bytes 1572872 | tf_op jit(solution)/shard_map/ppermute | solution.py:809
  58.9 20.2 %collective-permute-start.1 = (bf16[4,64,1024]{2,1,0:T(8,128)(2,1)}, bf16[4,64,1024]{2,1,0:T(8,128)(2,1)S(1)}, u32[]{:S(2)}, u32[]{:S(2)}) collective-permute-start(bf16[4,64,1024]{2,1,0:T(8,128)(2,1)} %get-tuple-element.24.line_0), channel_id=1, source_target_pairs={{0,8},{4,36},{8,16},{12,44},{16,24},{20,52},{24,0},{28,60},{32,40}... | collective-permute-start | bytes 1572872 | tf_op jit(solution)/shard_map/ppermute | solution.py:809
  59.8 19.3 %collective-permute-start = (bf16[4,64,1024]{2,1,0:T(8,128)(2,1)}, bf16[4,64,1024]{2,1,0:T(8,128)(2,1)S(1)}, u32[]{:S(2)}, u32[]{:S(2)}) collective-permute-start(bf16[4,64,1024]{2,1,0:T(8,128)(2,1)} %get-tuple-element.24.line_0), channel_id=1, source_target_pairs={{0,24},{4,100},{8,0},{12,108},{16,8},{20,116},{24,16},{28,124},{32... | collective-permute-start | bytes 1572872 | tf_op jit(solution)/shard_map/ppermute | solution.py:809
  61.6 17.5 %copy-start = (bf16[256,1024]{1,0:T(8,128)(2,1)S(1)}, bf16[256,1024]{1,0:T(8,128)(2,1)}, u32[]{:S(2)}) copy-start(bf16[256,1024]{1,0:T(8,128)(2,1)} %w_out_hbm.1) | copy-start | bytes 1572868
  61.6 17.5 %copy-start.1 = (bf16[256,1024]{1,0:T(8,128)(2,1)S(1)}, bf16[256,1024]{1,0:T(8,128)(2,1)}, u32[]{:S(2)}) copy-start(bf16[256,1024]{1,0:T(8,128)(2,1)} %get-tuple-element.23.ent_rows_hbm) | copy-start | bytes 1572868
  61.6 17.5 %copy-start.2 = (bf16[4,64,1024]{2,1,0:T(8,128)(2,1)S(1)}, bf16[4,64,1024]{2,1,0:T(8,128)(2,1)}, u32[]{:S(2)}) copy-start(bf16[4,64,1024]{2,1,0:T(8,128)(2,1)} %get-tuple-element.24.line_0) | copy-start | bytes 1572868
  61.6 17.5 %copy-start.3 = (f32[8,2,8,128]{3,2,1,0:T(8,128)S(1)}, f32[8,2,8,128]{3,2,1,0:T(8,128)}, u32[]{:S(2)}) copy-start(f32[8,2,8,128]{3,2,1,0:T(8,128)} %get-tuple-element.22.near_st_hbm) | copy-start | bytes 196612
  61.6 17.5 %copy-start.4 = (f32[1024]{0:T(1024)S(1)}, f32[1024]{0:T(1024)}, u32[]{:S(2)}) copy-start(f32[1024]{0:T(1024)} %param.14) | copy-start | bytes 12292
  72.3 6.8 %copy-start.5 = (bf16[4,64,1024]{2,1,0:T(8,128)(2,1)}, bf16[4,64,1024]{2,1,0:T(8,128)(2,1)S(1)}, u32[]{:S(2)}) copy-start(bf16[4,64,1024]{2,1,0:T(8,128)(2,1)S(1)} %collective-permute-done.4.side_up) | copy-start | bytes 1572868
  77.1 2.0 %copy-start.6 = (bf16[4,64,1024]{2,1,0:T(8,128)(2,1)}, bf16[4,64,1024]{2,1,0:T(8,128)(2,1)S(1)}, u32[]{:S(2)}) copy-start(bf16[4,64,1024]{2,1,0:T(8,128)(2,1)S(1)} %collective-permute-done.3.side_dn) | copy-start | bytes 1572868
